TPU v7x, 256 devices: a whole 4x4x8 slice. The times are simulated.
256 devices in a mesh: dp: 8 (over x, core), mp: 32 (over y, z).
Axes of the slice: x: 4, y: 4, z: 8, core: 2. Of those that a mesh axis runs over, the one named last changes fastest.
Arguments:
- inputs: bfloat16 [1536, 8192], P('dp', 'mp'), may hold values from -6 to 6
- out_grad: bfloat16 [1536, 8192], P('dp', 'mp'), may hold values from -6 to 6
- frozen_gu: bfloat16 [2, 8192, 16384], P(None, 'dp', 'mp'), may hold values from -0.0625 to 0.0625
- left_gu: bfloat16 [2, 8192, 32], replicated, may hold values from -0.0625 to 0.0625
- right_gu: bfloat16 [2, 32, 16384], P(None, None, 'mp'), may hold values from -0.29882812 to 0.29882812
- magnitude_gu: float32 [2, 16384], P(None, 'mp'), may hold values from 0.5 to 2
- frozen_down: bfloat16 [16384, 8192], P('mp'), may hold values from -0.046875 to 0.046875
- left_down: bfloat16 [16384, 32], P('mp'), may hold values from -0.046875 to 0.046875
- right_down: bfloat16 [32, 8192], replicated, may hold values from -0.29882812 to 0.29882812
- magnitude_down: float32 [8192], replicated, may hold values from 0.5 to 2
Outputs:
- grad_inputs: bfloat16 [1536, 8192], P('dp', 'mp')
- grad_mag_gu: float32 [2, 16384], P(None, 'mp')
- grad_left_gu: float32 [2, 8192, 32], P(None, 'mp')
- grad_right_gu: float32 [2, 32, 16384], P(None, None, 'mp')
- grad_mag_down: float32 [8192], P('mp')
- grad_left_down: float32 [16384, 32], P('mp')
- grad_right_down: float32 [32, 8192], P(None, 'mp')
All inputs are finite; a program needn't handle non-finite values.
Results may differ from a plain program's by a relative error of at most 0.0078.
Values may be sent and summed in bfloat16 or wider, within the bound.
No kernel may reach another device: no remote copies, remote signals or barrier semaphores. Data moves between devices by JAX's collectives and lax.ppermute only.
A program may use at most 192 MiB of HBM per device.

v0:
```python
import jax
import jax.numpy as jnp
from jax import lax
from jax.sharding import PartitionSpec as P


def merge_rows(frozen, left, right):
    return frozen.astype(jnp.float32) + 2.0 * jnp.einsum(
        "kir,krj->kij", left, right, preferred_element_type=jnp.float32
    )


def shards(
    inputs,
    out_grad,
    frozen_gu,
    left_gu,
    right_gu,
    magnitude_gu,
    frozen_down,
    left_down,
    right_down,
    magnitude_down,
):
    highest = lax.Precision.HIGHEST
    in_full, grad_full = (
        lax.all_gather(inputs, "mp", axis=1, tiled=True),
        lax.all_gather(out_grad, "mp", axis=1, tiled=True),
    )
    arrived = lax.all_gather(frozen_gu, "dp", axis=1, tiled=True)
    merged_gu = merge_rows(arrived, left_gu, right_gu)
    square_sums = jnp.sum(merged_gu * merged_gu, axis=1)
    tile_gu = merged_gu.astype(jnp.bfloat16)
    norm_gu = jnp.sqrt(square_sums + 1e-06)
    scale_gu = magnitude_gu / norm_gu
    merged_down = frozen_down.astype(jnp.float32) + 2.0 * jnp.dot(
        left_down, right_down, preferred_element_type=jnp.float32
    )
    down_squares = lax.psum(jnp.sum(merged_down * merged_down, axis=0), "mp")
    tile_down = merged_down.astype(jnp.bfloat16)
    norm_down = jnp.sqrt(down_squares + 1e-06)
    scale_down = magnitude_down / norm_down
    pre_gu = jnp.einsum("td,kdf->ktf", in_full, tile_gu, preferred_element_type=jnp.float32)
    hid_gu = pre_gu * scale_gu[:, None, :]
    sig = jax.nn.sigmoid(hid_gu[0])
    silu_gate = hid_gu[0] * sig
    act = (silu_gate * hid_gu[1]).astype(jnp.bfloat16)
    out_pre = jnp.dot(act, tile_down, preferred_element_type=jnp.float32)
    dot_down = jnp.sum(grad_full.astype(jnp.float32) * out_pre, axis=0)
    grad_pre_down = (grad_full.astype(jnp.float32) * scale_down[None, :]).astype(jnp.bfloat16)
    grad_act = jnp.einsum("td,fd->tf", grad_pre_down, tile_down, preferred_element_type=jnp.float32)
    grad_gate = grad_act * hid_gu[1] * sig * (1.0 + hid_gu[0] * (1.0 - sig))
    grad_up = grad_act * silu_gate
    grad_hid = jnp.stack([grad_gate, grad_up])
    dot_gu = jnp.sum(grad_hid * pre_gu, axis=1)
    pre_grads = (grad_hid * scale_gu[:, None, :]).astype(jnp.bfloat16)
    input_terms = jnp.einsum("ktf,kdf->td", pre_grads, tile_gu, preferred_element_type=jnp.float32)
    rows_gu = jnp.einsum("ktf,krf->ktr", pre_grads, right_gu, preferred_element_type=jnp.float32)
    proj_gu = jnp.einsum("td,kdr->ktr", in_full, left_gu, preferred_element_type=jnp.float32)
    right_gu_part = 2.0 * jnp.einsum(
        "ktr,ktf->krf", proj_gu, pre_grads.astype(jnp.float32), precision=highest
    )
    rows_down = jnp.einsum(
        "td,rd->tr", grad_pre_down, right_down, preferred_element_type=jnp.float32
    )
    left_down_part = 2.0 * jnp.einsum(
        "tf,tr->fr", act.astype(jnp.float32), rows_down, precision=highest
    )
    proj_down = jnp.dot(act, left_down, preferred_element_type=jnp.float32)
    width_own = inputs.shape[1]
    model_index = lax.axis_index("mp")
    left_gu_part = 2.0 * jnp.einsum(
        "td,ktr->kdr", in_full.astype(jnp.float32), rows_gu, precision=highest
    )
    right_down_part = 2.0 * jnp.einsum(
        "tr,td->rd", proj_down, grad_pre_down.astype(jnp.float32), precision=highest
    )
    grad_in, left_gu_own, right_down_own, dot_down_own = (
        lax.psum_scatter(input_terms, "mp", scatter_dimension=1, tiled=True),
        lax.psum_scatter(left_gu_part, "mp", scatter_dimension=1, tiled=True),
        lax.psum_scatter(right_down_part, "mp", scatter_dimension=1, tiled=True),
        lax.psum_scatter(dot_down[None, :], "mp", scatter_dimension=1, tiled=True),
    )
    left_gu_tot, right_down_tot, dot_down_tot, dot_gu_tot, right_gu_tot, left_down_tot = lax.psum(
        (left_gu_own, right_down_own, dot_down_own, dot_gu, right_gu_part, left_down_part), "dp"
    )
    norm_down_own = lax.dynamic_slice_in_dim(norm_down, model_index * width_own, width_own, 0)
    grad_mag_gu = dot_gu_tot / norm_gu
    grad_mag_down = dot_down_tot[0] / norm_down_own
    return (
        grad_in.astype(jnp.bfloat16),
        grad_mag_gu,
        left_gu_tot,
        right_gu_tot,
        grad_mag_down,
        left_down_tot,
        right_down_tot,
    )


def solution(mesh):
    in_specs = (
        P("dp", "mp"),
        P("dp", "mp"),
        P(None, "dp", "mp"),
        P(),
        P(None, None, "mp"),
        P(None, "mp"),
        P("mp", None),
        P("mp", None),
        P(),
        P(),
    )
    out_specs = (
        P("dp", "mp"),
        P(None, "mp"),
        P(None, "mp", None),
        P(None, None, "mp"),
        P("mp"),
        P("mp", None),
        P(None, "mp"),
    )
    return jax.shard_map(shards, mesh=mesh, in_specs=in_specs, out_specs=out_specs, check_vma=False)
```

profile of v0, /device:TPU:2, one launch (start us, length us, event | category | flops | bytes accessed | tf_op | source)
XLA Modules:
  0.0 1238.8 jit_solution(17227871348000152877)
XLA Ops:
  7.2 0.0 copy-start
  7.2 0.0 all-gather.6.cloned.1.call-start
  7.2 0.7 all-gather.6.cloned.1.call-update
  7.9 0.0 all-gather.8.cloned.1.call-start
  8.0 0.7 all-gather.8.cloned.1.call-update
  8.7 0.0 all-gather.4.cloned.1.call-start
  8.7 0.7 all-gather.4.cloned.1.call-update
  9.4 0.0 copy-start.5
  9.4 0.0 copy-start.3
  9.4 0.0 reduce-scatter.13.cloned.1.call-start
  9.5 10.4 multiply_reduce_fusion.1
  19.9 146.3 %psum.49 = f32[8192]{0:T(1024)S(1)} all-reduce(f32[8192]{0:T(1024)S(1)} %get-tuple-element.20), channel_id=1, replica_groups=mesh['dp'=8,'mp'=32] {'mp'}, use_global_device_ids=true, to_apply=%region_1.0 | all-reduce | flops 8192 | bytes 65536 | tf_op jit(solution)/shard_map/psum | solution.py:39
  166.2 0.0 copy-done.5
  166.2 0.0 copy-start.6
  166.2 0.0 all-gather.6.cloned.1.call-done
  166.2 0.0 copy-done
  166.2 0.0 copy-done.3
  166.2 17.6 %multiply_reduce_fusion = (f32[2,512]{1,0:T(2,128)S(1)}, f32[2,8192,512]{2,1,0:T(8,128)}) fusion(bf16[2,8192,512]{2,1,0:T(8,128)(2,1)} %all-gather.6.cloned.1.call-done, bf16[2,8192,32]{1,2,0:T(8,128)(2,1)S(1)} %copy-done, bf16[2,32,512]{2,1,0:T(8,128)(2,1)S(1)} %copy-done.3), kind=kOutput, calls=%fused_computation | convolution fusion | flops 578812928 | bytes 51449856 | tf_op jit(solution)/shard_map/kir,krj->kij/dot_general | solution.py:8
  183.8 0.0 copy-done.6
  183.9 0.0 all-gather.8.cloned.1.call-done
  183.9 18.0 %broadcast_multiply_fusion = (f32[2,192,512]{2,1,0:T(8,128)S(1)}, f32[2,192,512]{2,1,0:T(8,128)S(1)}) fusion(f32[2,512]{1,0:T(2,128)S(1)} %fusion.23, f32[2,8192,512]{2,1,0:T(8,128)} %get-tuple-element.23, bf16[2,8192,512]{2,1,0:T(8,128)(2,1)} %all-gather.6.cloned.1.call-done, bf16[192,8192]{1,0:T(8,128)(2,1)} %all-gather.8.cloned.1.call-done), kind=kOutput, calls=%fused_computation.35 | convolution fusion | flops 3254976512 | bytes 55054336 | tf_op jit(solution)/shard_map/td,kdf->ktf/dot_general | solution.py:43
  201.9 0.0 copy-start.4
  201.9 61.5 %all-gather.4.cloned.1.call-done = bf16[192,8192]{1,0:T(8,128)(2,1)} async-done(((bf16[192,256]{1,0:T(8,128)(2,1)}), bf16[192,8192]{1,0:T(8,128)(2,1)}) %all-gather.4.cloned.1.call-update) | async-done | bytes 3145744 | tf_op jit(solution)/shard_map/all_gather | solution.py:28
  263.4 0.0 copy-start.1
  263.4 8.2 multiply_bitcast_fusion.1
  271.7 0.0 copy-done.4
  271.7 0.2 fusion.32
  271.9 0.0 copy-done.1
  271.9 5.3 fusion.15
  277.2 0.0 copy-start.2
  277.2 2.7 copy.17
  279.8 0.0 reduce-scatter.13.cloned.1.call-update
  279.9 0.0 reduce-scatter.11.cloned.1.call-start
  279.9 4.8 convolution_multiply_fusion.2
  284.7 0.0 reduce-scatter.11.cloned.1.call-update
  284.7 0.3 reduce-scatter.9.cloned.1.call-start
  285.0 0.0 copy-done.2
  285.0 0.2 multiply_reduce_fusion.2
  285.2 0.2 fusion.31
  285.4 5.0 fusion.1
  290.4 0.0 reduce-scatter.9.cloned.1.call-update
  290.4 0.0 reduce-scatter.7.cloned.1.call-start
  290.5 20.2 %convolution_bitcast_fusion = f32[192,8192]{1,0:T(8,128)} fusion(bf16[2,192,512]{2,1,0:T(8,128)(2,1)S(1)} %get-tuple-element.17, f32[2,8192,512]{2,1,0:T(8,128)} %get-tuple-element.23, bf16[2,8192,512]{2,1,0:T(8,128)(2,1)} %all-gather.6.cloned.1.call-done), kind=kOutput, calls=%fused_computation.6 | convolution fusion | flops 3254779904 | bytes 57016320 | tf_op jit(solution)/shard_map/ktf,kdf->td/dot_general | solution.py:57
  310.7 0.0 reduce-scatter.7.cloned.1.call-update
  310.7 0.0 all-reduce.4.cloned.1.call-start
  310.8 3.1 fusion.6
  313.8 0.0 copy-done.7
  313.8 2.9 fusion.12
  316.7 0.9 convolution_multiply_fusion.4
  317.6 1.0 convolution_multiply_fusion.3
  318.5 183.3 %reduce-scatter.13.cloned.1.call-done = f32[256,1]{1,0:T(8,128)} async-done(((f32[8192,1]{1,0:T(8,128)}), f32[256,1]{1,0:T(8,128)}) %reduce-scatter.13.cloned.1.call-update) | async-done | bytes 1040
  501.9 1.0 copy.18
  502.8 215.8 %reduce-scatter.11.cloned.1.call-done = f32[32,256]{1,0:T(8,128)} async-done(((f32[32,8192]{1,0:T(8,128)}), f32[32,256]{1,0:T(8,128)}) %reduce-scatter.11.cloned.1.call-update) | async-done | bytes 32784 | tf_op jit(solution)/shard_map/reduce_scatter | solution.py:81
  718.7 21.5 %all-reduce = (f32[2,512]{1,0:T(2,128)S(1)}, f32[256]{0:T(256)S(1)}, f32[32,256]{1,0:T(8,128)}) all-reduce(f32[2,512]{1,0:T(2,128)S(1)} %get-tuple-element.16, f32[256]{0:T(256)S(1)} %bitcast.64, f32[32,256]{1,0:T(8,128)} %reduce-scatter.11.cloned.1.call-done), channel_id=1, replica_groups=mesh['dp'=8,'mp'=32] {'dp'}, use_global_device_ids=true, to_apply=%region_5.0 | all-reduce | flops 9472 | bytes 75776 | tf_op jit(solution)/shard_map/psum | solution.py:84
  740.2 0.6 fusion.22
  740.8 196.5 %reduce-scatter.9.cloned.1.call-done = f32[2,256,32]{1,2,0:T(8,128)} async-done(((f32[2,8192,32]{1,2,0:T(8,128)}), f32[2,256,32]{1,2,0:T(8,128)}) %reduce-scatter.9.cloned.1.call-update) | async-done | bytes 65552 | tf_op jit(solution)/shard_map/reduce_scatter | solution.py:80
  937.3 0.0 all-reduce.4.cloned.1.call-update
  937.3 0.6 dynamic-slice_divide_fusion
  938.0 225.2 %reduce-scatter.7.cloned.1.call-done = f32[192,256]{1,0:T(8,128)} async-done(((f32[192,8192]{1,0:T(8,128)}), f32[192,256]{1,0:T(8,128)}) %reduce-scatter.7.cloned.1.call-update) | async-done | bytes 196624 | tf_op jit(solution)/shard_map/reduce_scatter | solution.py:79
  1163.2 1.6 convert_element_type.39
  1164.7 62.7 %all-reduce.4.cloned.1.call-done = (f32[2,256,32]{1,2,0:T(8,128)}, f32[2,32,512]{2,1,0:T(8,128)}, f32[512,32]{0,1:T(8,128)}) async-done(((f32[2,256,32]{1,2,0:T(8,128)}, f32[2,32,512]{2,1,0:T(8,128)}, f32[512,32]{0,1:T(8,128)}), (f32[2,256,32]{1,2,0:T(8,128)}, f32[2,32,512]{2,1,0:T(8,128)}, f32[512,32]{0,1:T(8,128)})) %all-reduce.4.cloned.1.call-update) | async-done | bytes 262160 | tf_op jit(solution)/shard_map/psum | solution.py:84
  1227.5 1.5 copy.22
  1228.9 1.6 copy.23
  1230.5 1.5 copy.24
  (3 shorter events, 0.0 us)
Async XLA Ops:
  7.2 159.1 %copy-start = (bf16[2,8192,32]{1,2,0:T(8,128)(2,1)S(1)}, bf16[2,8192,32]{1,2,0:T(8,128)(2,1)}, u32[]{:S(2)}) copy-start(bf16[2,8192,32]{1,2,0:T(8,128)(2,1)} %param.13) | copy-start | bytes 3145732
  7.2 159.0 %all-gather.6.cloned.1.call-start = ((), (), s32[]{:S(2)}) async-start(), calls=%async_computation.5 | async-start | bytes 18874368 | tf_op jit(solution)/shard_map/all_gather | solution.py:30
  7.9 176.0 %all-gather.8.cloned.1.call-start = ((), (), s32[]{:S(2)}) async-start(), calls=%async_computation.6 | async-start | bytes 3244032 | tf_op jit(solution)/shard_map/all_gather | solution.py:27
  8.7 254.8 %all-gather.4.cloned.1.call-start = ((), (), s32[]{:S(2)}) async-start(), calls=%async_computation.4 | async-start | bytes 3244032 | tf_op jit(solution)/shard_map/all_gather | solution.py:28
  9.4 156.8 %copy-start.5 = (f32[8192]{0:T(1024)S(1)}, f32[8192]{0:T(1024)}, u32[]{:S(2)}) copy-start(f32[8192]{0:T(1024)} %param.19) | copy-start | bytes 98308
  9.4 156.8 %copy-start.3 = (bf16[2,32,512]{2,1,0:T(8,128)(2,1)S(1)}, bf16[2,32,512]{2,1,0:T(8,128)(2,1)}, u32[]{:S(2)}) copy-start(bf16[2,32,512]{2,1,0:T(8,128)(2,1)} %param.14) | copy-start | bytes 196612
  9.4 492.4 %reduce-scatter.13.cloned.1.call-start = ((), (), s32[]{:S(2)}) async-start(), calls=%async_computation.10 | async-start | bytes 4325376
  166.2 17.7 %copy-start.6 = (f32[2,512]{1,0:T(2,128)S(1)}, f32[2,512]{1,0:T(2,128)}, u32[]{:S(2)}) copy-start(f32[2,512]{1,0:T(2,128)} %param.15) | copy-start | bytes 12292
  201.9 69.8 %copy-start.4 = (bf16[512,32]{0,1:T(8,128)(2,1)S(1)}, bf16[512,32]{0,1:T(8,128)(2,1)}, u32[]{:S(2)}) copy-start(bf16[512,32]{0,1:T(8,128)(2,1)} %param.17) | copy-start | bytes 98308
  263.4 8.4 copy-start.1
  277.2 7.8 copy-start.2
  279.9 438.8 %reduce-scatter.11.cloned.1.call-start = ((), (), s32[]{:S(2)}) async-start(), calls=%async_computation.9 | async-start | bytes 1081344 | tf_op jit(solution)/shard_map/reduce_scatter | solution.py:81
  284.7 652.6 %reduce-scatter.9.cloned.1.call-start = ((), (), s32[]{:S(2)}) async-start(), calls=%async_computation.8 | async-start | bytes 2162688 | tf_op jit(solution)/shard_map/reduce_scatter | solution.py:80
  290.4 872.7 %reduce-scatter.7.cloned.1.call-start = ((), (), s32[]{:S(2)}) async-start(), calls=%async_computation.7 | async-start | bytes 6488064 | tf_op jit(solution)/shard_map/reduce_scatter | solution.py:79
  310.7 3.1 copy-start.7
  310.7 916.8 %all-reduce.4.cloned.1.call-start = ((), (), s32[]{:S(2)}) async-start(), calls=%async_computation.11 | async-start | bytes 524288 | tf_op jit(solution)/shard_map/psum | solution.py:84
Sparse Core Ops, SparseCore 0:
  9.9 90.0 all-gather.5
  102.4 79.4 all-gather.7
  184.4 78.9 all-gather.3
  280.0 221.8 reduce-scatter.12
  506.0 212.6 reduce-scatter.10
  722.9 214.4 reduce-scatter.8
  941.3 221.8 reduce-scatter.6
  1166.4 61.0 all-reduce.3
where the time goes:
time: 1240 us
  waiting for transfers between devices  947 us (76%)
  blocking collectives  168 us (14%)
  matrix products  97.6 us (8%)
  between operations  14.3 us (1%)
    reduce_scatter x1, waiting for transfers between devices, shards(): lax.psum_scatter(input_terms, 'mp', scatter_dimension=1, tiled=True)  225 us
    reduce_scatter x1, waiting for transfers between devices, shards(): lax.psum_scatter(right_down_part, 'mp', scatter_dimension=1, tiled=True)  216 us
    reduce_scatter x1, waiting for transfers between devices, shards(): lax.psum_scatter(left_gu_part, 'mp', scatter_dimension=1, tiled=True)  197 us
    unnamed x9, waiting for transfers between devices  185 us
    psum x1, blocking collectives, shards(): down_squares = lax.psum(jnp.sum(merged_down * merged_down, axis=0), 'mp')  146 us
    psum x1, waiting for transfers between devices, shards(): lax.psum((left_gu_own, right_down_own, dot_down_own, dot_gu, right_gu_par...  62.7 us
    all_gather x1, waiting for transfers between devices, shards(): lax.all_gather(out_grad, 'mp', axis=1, tiled=True)  61.5 us
  transfers between devices with their start and end apart: 8, of which 6 were waited for; matrix products, arithmetic and copies ran while one was open for 7% of the time, Pallas kernels for 0%

commit v1 on v0

v1 whole, which is shorter than its diff:
```python
import functools

import jax
import jax.numpy as jnp
from jax import lax
from jax.experimental import pallas as pl
from jax.experimental.pallas import tpu as pltpu
from jax.sharding import Mesh, PartitionSpec as P

F32, BF16 = jnp.float32, jnp.bfloat16
DP, MP = ("x", "core"), ("y", "z")
NX, NC, NY, NZ = 4, 2, 4, 8
NDP, NMP = NX * NC, NY * NZ
NT = (((1,), (1,)), ((), ()))
PAR = dict(vmem_limit_bytes=50 * 1024 * 1024)


def ring_gather(block, axis, n):
    up = [(i, (i + 1) % n) for i in range(n)]
    down = [(i, (i - 1) % n) for i in range(n)]
    behind, ahead = [block], [block]
    for _ in range(n // 2 - 1):
        behind.append(lax.ppermute(behind[-1], axis, up))
        ahead.append(lax.ppermute(ahead[-1], axis, down))
    half = block.shape[0] // 2
    far = jnp.concatenate(
        [lax.ppermute(behind[-1][:half], axis, up), lax.ppermute(ahead[-1][half:], axis, down)]
    )
    return jnp.stack(behind[:0:-1] + ahead + [far])


def place_y_first(pos_ref, block):
    y, z = pos_ref[0], pos_ref[1]
    return lax.rem(block // NZ - y + 1 + NY, NY) * NZ + lax.rem(block % NZ - z + 3 + NZ, NZ)


def place_z_first(pos_ref, block):
    y, z = pos_ref[0], pos_ref[1]
    return lax.rem(block % NZ - z + 3 + NZ, NZ) * NY + lax.rem(block // NZ - y + 1 + NY, NY)


def merge_down_body(frozen_ref, left_ref, right_ref, tile_ref, squares_ref):
    merged = frozen_ref[...].astype(F32) + 2.0 * jnp.dot(
        left_ref[...], right_ref[...], preferred_element_type=F32
    )
    tile_ref[...] = merged.astype(BF16)
    rows, cols = merged.shape
    squares = jnp.sum((merged * merged).reshape(rows // 8, 8, cols), axis=0)
    squares_ref[0] = squares[:, : cols // 2]
    squares_ref[1] = squares[:, cols // 2 :]


def merge_down(frozen, left, right):
    f, d = frozen.shape
    return pl.pallas_call(
        merge_down_body,
        grid=(d // 512,),
        in_specs=[
            pl.BlockSpec((f, 512), lambda c: (0, c)),
            pl.BlockSpec((f, 32), lambda c: (0, 0)),
            pl.BlockSpec((32, 512), lambda c: (0, c)),
        ],
        out_specs=[
            pl.BlockSpec((f, 512), lambda c: (0, c)),
            pl.BlockSpec((2, 8, 256), lambda c: (c, 0, 0)),
        ],
        out_shape=[
            jax.ShapeDtypeStruct((f, d), BF16),
            jax.ShapeDtypeStruct((d // 256, 8, 256), F32),
        ],
        compiler_params=pltpu.CompilerParams(**PAR),
        cost_estimate=pl.CostEstimate(flops=2 * f * d * 40, bytes_accessed=4 * f * d, transcendentals=0),
        name="merge_down",
    )(frozen, left, right)


def proj_body(pos_ref, x_ref, left_ref, out_ref):
    c = pl.program_id(0)

    @pl.when(c == 0)
    def _():
        out_ref[...] = jnp.zeros_like(out_ref)

    for h in range(2):
        x = x_ref[place_y_first(pos_ref, 2 * c + h)]
        for k in range(2):
            out_ref[k] += jnp.dot(x, left_ref[k, h * 256 : (h + 1) * 256], preferred_element_type=F32)


def proj_gate_up(pos, x, left):
    n, t, w = x.shape
    return pl.pallas_call(
        proj_body,
        grid_spec=pltpu.PrefetchScalarGridSpec(
            num_scalar_prefetch=1,
            grid=(n // 2,),
            in_specs=[
                pl.BlockSpec((n, t, w), lambda c, p: (0, 0, 0)),
                pl.BlockSpec((2, 2 * w, 32), lambda c, p: (0, c, 0)),
            ],
            out_specs=pl.BlockSpec((2, t, 32), lambda c, p: (0, 0, 0)),
        ),
        out_shape=jax.ShapeDtypeStruct((2, t, 32), F32),
        compiler_params=pltpu.CompilerParams(**PAR),
        cost_estimate=pl.CostEstimate(flops=n * t * w * 128, bytes_accessed=8_000_000, transcendentals=0),
        name="proj_gate_up",
    )(pos, x, left)


def grad_act_body(pos_ref, g_ref, scale_ref, tile_ref, right_ref, out_ref, rows_ref):
    c = pl.program_id(0)

    @pl.when(c == 0)
    def _():
        out_ref[...] = jnp.zeros_like(out_ref)
        rows_ref[...] = jnp.zeros_like(rows_ref)

    for h in range(2):
        g = g_ref[place_z_first(pos_ref, 2 * c + h)].astype(F32)
        g = (g * scale_ref[h]).astype(BF16)
        cols = slice(h * 256, (h + 1) * 256)
        out_ref[...] += lax.dot_general(g, tile_ref[:, cols], NT, preferred_element_type=F32)
        rows_ref[...] += lax.dot_general(g, right_ref[:, cols], NT, preferred_element_type=F32)


def grad_act_rows(pos, g, scale, tile, right):
    n, t, w = g.shape
    f, d = tile.shape
    return pl.pallas_call(
        grad_act_body,
        grid_spec=pltpu.PrefetchScalarGridSpec(
            num_scalar_prefetch=1,
            grid=(n // 2,),
            in_specs=[
                pl.BlockSpec((n, t, w), lambda c, p: (0, 0, 0)),
                pl.BlockSpec((2, 1, w), lambda c, p: (c, 0, 0)),
                pl.BlockSpec((f, 2 * w), lambda c, p: (0, c)),
                pl.BlockSpec((32, 2 * w), lambda c, p: (0, c)),
            ],
            out_specs=[
                pl.BlockSpec((t, f), lambda c, p: (0, 0)),
                pl.BlockSpec((t, 32), lambda c, p: (0, 0)),
            ],
        ),
        out_shape=[jax.ShapeDtypeStruct((t, f), F32), jax.ShapeDtypeStruct((t, 32), F32)],
        compiler_params=pltpu.CompilerParams(**PAR),
        cost_estimate=pl.CostEstimate(flops=2 * t * f * d, bytes_accessed=12_000_000, transcendentals=0),
        name="grad_act",
    )(pos, g, scale, tile, right)


def dot_down_body(pos_ref, g_ref, act_ref, tile_ref, out_ref):
    c = pl.program_id(0)
    out_pre = jnp.dot(act_ref[...], tile_ref[...], preferred_element_type=F32)
    t = out_pre.shape[0]
    for h in range(2):
        g = g_ref[place_z_first(pos_ref, 2 * c + h)].astype(F32)
        both = g * out_pre[:, h * 256 : (h + 1) * 256]
        out_ref[h] = jnp.sum(both.reshape(t // 8, 8, 256), axis=0)


def dot_down_sums(pos, g, act, tile):
    n, t, w = g.shape
    f, d = tile.shape
    return pl.pallas_call(
        dot_down_body,
        grid_spec=pltpu.PrefetchScalarGridSpec(
            num_scalar_prefetch=1,
            grid=(n // 2,),
            in_specs=[
                pl.BlockSpec((n, t, w), lambda c, p: (0, 0, 0)),
                pl.BlockSpec((t, f), lambda c, p: (0, 0)),
                pl.BlockSpec((f, 2 * w), lambda c, p: (0, c)),
            ],
            out_specs=pl.BlockSpec((2, 8, w), lambda c, p: (c, 0, 0)),
        ),
        out_shape=jax.ShapeDtypeStruct((n, 8, w), F32),
        compiler_params=pltpu.CompilerParams(**PAR),
        cost_estimate=pl.CostEstimate(flops=2 * t * f * d, bytes_accessed=12_000_000, transcendentals=0),
        name="dot_down",
    )(pos, g, act, tile)


def gate_up_body(pos_ref, x_ref, frozen_ref, left_ref, right_ref, tile_ref, pre_ref, squares_ref):
    c = pl.program_id(0)

    @pl.when(c == 0)
    def _():
        pre_ref[...] = jnp.zeros_like(pre_ref)
        squares_ref[...] = jnp.zeros_like(squares_ref)

    for h in range(2):
        x = x_ref[place_y_first(pos_ref, 2 * c + h)]
        rows = slice(h * 256, (h + 1) * 256)
        for k in range(2):
            merged = frozen_ref[k, rows].astype(F32) + 2.0 * jnp.dot(
                left_ref[k, rows], right_ref[k], preferred_element_type=F32
            )
            tile = merged.astype(BF16)
            tile_ref[k, rows] = tile
            squares_ref[k] += jnp.sum((merged * merged).reshape(32, 8, -1), axis=0)
            pre_ref[k] += jnp.dot(x, tile, preferred_element_type=F32)


def gate_up(pos, x, frozen, left, right):
    n, t, w = x.shape
    _, d, f = frozen.shape
    return pl.pallas_call(
        gate_up_body,
        grid_spec=pltpu.PrefetchScalarGridSpec(
            num_scalar_prefetch=1,
            grid=(n // 2,),
            in_specs=[
                pl.BlockSpec((n, t, w), lambda c, p: (0, 0, 0)),
                pl.BlockSpec((2, 2 * w, f), lambda c, p: (0, c, 0)),
                pl.BlockSpec((2, 2 * w, 32), lambda c, p: (0, c, 0)),
                pl.BlockSpec((2, 32, f), lambda c, p: (0, 0, 0)),
            ],
            out_specs=[
                pl.BlockSpec((2, 2 * w, f), lambda c, p: (0, c, 0)),
                pl.BlockSpec((2, t, f), lambda c, p: (0, 0, 0)),
                pl.BlockSpec((2, 8, f), lambda c, p: (0, 0, 0)),
            ],
        ),
        out_shape=[
            jax.ShapeDtypeStruct((2, d, f), BF16),
            jax.ShapeDtypeStruct((2, t, f), F32),
            jax.ShapeDtypeStruct((2, 8, f), F32),
        ],
        compiler_params=pltpu.CompilerParams(**PAR),
        cost_estimate=pl.CostEstimate(flops=4 * t * f * d, bytes_accessed=36_000_000, transcendentals=0),
        name="gate_up",
    )(pos, x, frozen, left, right)


def grad_in_body(first, grads_ref, tile_ref, a_ref, b_ref):
    for h in range(2):
        rows = slice(h * 256, (h + 1) * 256)
        out = lax.dot_general(grads_ref[0], tile_ref[0, rows], NT, preferred_element_type=F32)
        out += lax.dot_general(grads_ref[1], tile_ref[1, rows], NT, preferred_element_type=F32)
        out = out.astype(BF16)
        a_ref[0, h] = out[:first]
        b_ref[h, 0] = out[first:]


def grad_in_parts(grads, tile, first):
    _, t, f = grads.shape
    d = tile.shape[1]
    quarter = NZ // 2
    return pl.pallas_call(
        functools.partial(grad_in_body, first),
        grid=(NMP // 2,),
        in_specs=[
            pl.BlockSpec((2, t, f), lambda c: (0, 0, 0)),
            pl.BlockSpec((2, 512, f), lambda c: (0, c, 0)),
        ],
        out_specs=[
            pl.BlockSpec((1, 2, first, 256), lambda c: (c // quarter, c % quarter, 0, 0)),
            pl.BlockSpec((2, 1, t - first, 256), lambda c: (c % quarter, c // quarter, 0, 0)),
        ],
        out_shape=[
            jax.ShapeDtypeStruct((NY, NZ, first, 256), BF16),
            jax.ShapeDtypeStruct((NZ, NY, t - first, 256), BF16),
        ],
        compiler_params=pltpu.CompilerParams(**PAR),
        cost_estimate=pl.CostEstimate(flops=4 * t * f * d, bytes_accessed=20_000_000, transcendentals=0),
        name="grad_in",
    )(grads, tile)


def exchange(parts, axes):
    return lax.all_to_all(parts, axes, 0, 0, tiled=True)


def sum_parts(parts, axes):
    return jnp.sum(exchange(parts, axes).astype(F32), axis=0)


def total(parts, axes):
    own = sum_parts(parts, axes)
    return exchange(jnp.broadcast_to(own[None], parts.shape), axes)


def shards(
    inputs,
    out_grad,
    frozen_gu,
    left_gu,
    right_gu,
    magnitude_gu,
    frozen_down,
    left_down,
    right_down,
    magnitude_down,
):
    tokens, width = inputs.shape
    iy, iz = lax.axis_index("y"), lax.axis_index("z")
    pos = jnp.stack([iy, iz]).astype(jnp.int32)
    frozen_full = lax.all_gather(frozen_gu, DP, axis=1, tiled=True)

    x_blocks = ring_gather(ring_gather(inputs, "z", NZ), "y", NY).reshape(NMP, tokens, width)
    g_blocks = ring_gather(ring_gather(out_grad, "y", NY), "z", NZ).reshape(NMP, tokens, width)

    tile_down, down_squares = merge_down(frozen_down, left_down, right_down)
    down_sum = jnp.sum(sum_parts(down_squares, MP), axis=0)
    down_sums = exchange(jnp.broadcast_to(down_sum, down_squares.shape), MP)[:, :1]
    norm_down = jnp.sqrt(down_sums + 1e-06)
    scale_down = magnitude_down.reshape(NMP, 1, width) / norm_down
    grad_act, rows_down = grad_act_rows(pos, g_blocks, scale_down, tile_down, right_down)
    proj_gu = proj_gate_up(pos, x_blocks, left_gu)

    tile_gu, pre_gu, gu_squares = gate_up(pos, x_blocks, frozen_full, left_gu, right_gu)
    norm_gu = jnp.sqrt(jnp.sum(gu_squares, axis=1) + 1e-06)
    scale_gu = magnitude_gu / norm_gu
    hid_gu = pre_gu * scale_gu[:, None, :]
    sig = jax.nn.sigmoid(hid_gu[0])
    silu_gate = hid_gu[0] * sig
    act = (silu_gate * hid_gu[1]).astype(BF16)
    grad_gate = grad_act * hid_gu[1] * sig * (1.0 + hid_gu[0] * (1.0 - sig))
    grad_up = grad_act * silu_gate
    grad_hid = jnp.stack([grad_gate, grad_up])
    dot_gu = jnp.sum(grad_hid * pre_gu, axis=1)
    pre_grads = (grad_hid * scale_gu[:, None, :]).astype(BF16)

    rows_gu = jnp.einsum("ktf,krf->tkr", pre_grads, right_gu, preferred_element_type=F32)
    proj_down = jnp.dot(act, left_down, preferred_element_type=F32)
    rows = jnp.concatenate([rows_gu.reshape(tokens, 64), proj_down], axis=1)
    rows = jnp.pad(rows, ((0, 256 - tokens), (0, 32))).reshape(NMP, 8, 128)

    part_a, part_b = grad_in_parts(pre_grads, tile_gu, 128)
    half_a = sum_parts(part_a, "y").astype(BF16)
    half_b = sum_parts(part_b, "z").astype(BF16)
    grad_in = jnp.concatenate([sum_parts(half_a, "z"), sum_parts(half_b, "y")])

    rows = total(rows, MP).reshape(256, 128)[:tokens]
    own = lax.dynamic_index_in_dim(scale_down, iy * NZ + iz, 0, keepdims=False)
    own_norm = lax.dynamic_index_in_dim(norm_down, iy * NZ + iz, 0, keepdims=False)
    own_grads = (out_grad.astype(F32) * own).astype(BF16)
    rows16 = rows.astype(BF16)
    tn = (((0,), (0,)), ((), ()))
    left_gu_part = lax.dot_general(rows16[:, :64], inputs, tn, preferred_element_type=F32)
    right_down_part = lax.dot_general(rows16[:, 64:96], own_grads, tn, preferred_element_type=F32)
    dot_down = jnp.sum(sum_parts(dot_down_sums(pos, g_blocks, act, tile_down), MP), axis=0)

    right_gu_part = jnp.einsum("ktr,ktf->krf", proj_gu.astype(BF16), pre_grads, preferred_element_type=F32)
    left_down_part = lax.dot_general(rows_down.astype(BF16), act, tn, preferred_element_type=F32)
    hidden = pre_gu.shape[2]
    early = jnp.concatenate(
        [2.0 * right_gu_part.reshape(64, hidden), 2.0 * left_down_part, dot_gu, jnp.zeros((30, hidden), F32)]
    )
    early = total(early.reshape(NDP, 16, hidden), DP).reshape(128, hidden)
    late = jnp.concatenate(
        [2.0 * left_gu_part, 2.0 * right_down_part, dot_down[None], jnp.zeros((31, width), F32)]
    )
    late = total(late.reshape(NDP, 16, width), DP).reshape(128, width)
    return (
        grad_in.astype(BF16),
        early[96:98] / norm_gu,
        late[:64].reshape(2, 32, width).swapaxes(1, 2),
        early[:64].reshape(2, 32, hidden),
        late[96] / own_norm[0],
        early[64:96].T,
        late[64:96],
    )


def solution(mesh):
    fine = Mesh(mesh.devices.reshape(NX, NC, NY, NZ), ("x", "core", "y", "z"))
    in_specs = (
        P(DP, MP),
        P(DP, MP),
        P(None, DP, MP),
        P(),
        P(None, None, MP),
        P(None, MP),
        P(MP, None),
        P(MP, None),
        P(),
        P(),
    )
    out_specs = (
        P(DP, MP),
        P(None, MP),
        P(None, MP, None),
        P(None, None, MP),
        P(MP),
        P(MP, None),
        P(None, MP),
    )
    return jax.shard_map(shards, mesh=fine, in_specs=in_specs, out_specs=out_specs, check_vma=False)
```

time: 1240 us -> 388 us (0.31)
  waiting for transfers between devices: 947 us -> 81.7 us
  blocking collectives: 168 us -> 32.3 us
  starting transfers between devices: 0.54 us -> 107 us
  Pallas kernels: 0 us -> 92.8 us
  matrix products: 97.6 us -> 8.59 us
  local copies, waits for them, and re-layouts: 8.21 us -> 29.6 us
  other arithmetic: 3.07 us -> 16.8 us
    reduce_scatter x3 -> x0, waiting for transfers between devices: 638 us -> none  [the longest x1 225 us: shards(): lax.psum_scatter(input_terms, 'mp', scatter_dimension=1, tiled=True)]
    unnamed x9 -> x1, waiting for transfers between devices: 185 us -> 0.68 us
    psum x2 -> x0, blocking collectives: 168 us -> none  [the longest x1 146 us: shards(): down_squares = lax.psum(jnp.sum(merged_down * merged_down, axis=0), 'mp')]
    pallas_call x0 -> x6, Pallas kernels: none -> 92.8 us  [the longest x1 26.3 us: gate_up(): pl.pallas_call(gate_up_body, grid_spec=pltpu.PrefetchScalarGridSpec(num_s...]
    dot_general x14 -> x6, matrix products: 97.6 us -> 8.59 us  [the longest x1 1.8 us: shards(): jnp.einsum('ktr,ktf->krf', proj_gu.astype(BF16), pre_grads, preferred_ele...]
    all_to_all x0 -> x12, waiting for transfers between devices: none -> 67.8 us  [exchange(): return lax.all_to_all(parts, axes, 0, 0, tiled=True)]
    all_to_all x0 -> x12, starting transfers between devices: none -> 64.4 us  [exchange(): return lax.all_to_all(parts, axes, 0, 0, tiled=True)]
    psum x1 -> x0, waiting for transfers between devices: 62.7 us -> none  [shards(): lax.psum((left_gu_own, right_down_own, dot_down_own, dot_gu, right_gu_par...]
  transfers between devices with their start and end apart: 8 -> 37, of which waited for: 6 -> 11; matrix products, arithmetic and copies ran while one was open for 7% -> 9% of each run, Pallas kernels for 0% -> 17%
where the time goes in v1:
time: 388 us; the launch traced here: 383 us
  starting transfers between devices  107 us (28%)
  Pallas kernels  92.8 us (24%)
  waiting for transfers between devices  81.7 us (21%)
  blocking collectives  32.3 us (8%)
  local copies, waits for them, and re-layouts  29.6 us (8%)
  other arithmetic  16.8 us (4%)
  between operations  14.6 us (4%)
  matrix products  8.59 us (2%)
    all_to_all x12, waiting for transfers between devices, exchange(): return lax.all_to_all(parts, axes, 0, 0, tiled=True)  67.8 us
    all_to_all x12, starting transfers between devices, exchange(): return lax.all_to_all(parts, axes, 0, 0, tiled=True)  64.4 us
    all_to_all x1, blocking collectives, exchange(): return lax.all_to_all(parts, axes, 0, 0, tiled=True)  32.3 us
    pallas_call x1, Pallas kernels, gate_up(): pl.pallas_call(gate_up_body, grid_spec=pltpu.PrefetchScalarGridSpec(num_s...  26.3 us
    ppermute x8, starting transfers between devices, ring_gather(): ahead.append(lax.ppermute(ahead[-1], axis, down))  19.8 us
    unnamed x71, local copies, waits for them, and re-layouts  17.5 us
    pallas_call x1, Pallas kernels, grad_in_parts(): pl.pallas_call(functools.partial(grad_in_body, first), grid=(NMP // 2,),...  15.8 us
    pallas_call x1, Pallas kernels, merge_down(): pl.pallas_call(merge_down_body, grid=(d // 512,), in_specs=[pl.BlockSpec(...  14.6 us
  transfers between devices with their start and end apart: 37, of which 11 were waited for; matrix products, arithmetic and copies ran while one was open for 9% of the time, Pallas kernels for 17%

profile of v1, /device:TPU:2, one launch (start us, length us, event | category | flops | bytes accessed | tf_op | source)
XLA Modules:
  0.0 383.2 jit_solution(16195432905782185727)
XLA Ops:
  7.9 1.7 collective-permute-start
  9.6 1.7 collective-permute-start.1
  11.2 1.9 collective-permute-start.12
  13.1 3.9 %collective-permute-start.15 = (bf16[192,256]{1,0:T(8,128)(2,1)}, bf16[192,256]{1,0:T(8,128)(2,1)S(1)}, u32[]{:S(2)}, u32[]{:S(2)}) collective-permute-start(bf16[192,256]{1,0:T(8,128)(2,1)} %param.10), channel_id=1, source_target_pairs={{0,7},{1,0},{2,1},{3,2},{4,3},{5,4},{6,5},{7,6},{8,15},{9,8},{10,9... | collective-permute-start | bytes 294920 | tf_op jit(solution)/shard_map/ppermute | solution.py:24
  17.5 2.9 collective-permute-start.3
  22.4 14.6 %merge_down.1 = (bf16[512,8192]{1,0:T(8,128)(2,1)}, f32[32,8,256]{2,1,0:T(8,128)}) custom-call(bf16[512,8192]{1,0:T(8,128)(2,1)} %frozen_ref.1, bf16[512,32]{1,0:T(8,128)(2,1)S(1)} %copy.33.left_ref, bf16[32,8192]{1,0:T(8,128)(2,1)S(1)} %copy-done.5), custom_call_target="tpu_custom_call" | custom-call | flops 335544320 | bytes 16777216 | tf_op jit(solution)/shard_map/merge_down/pallas_call | solution.py:55
  37.0 6.4 %all-to-all-start = ((f32[32,8,256]{2,1,0:T(8,128)}), f32[32,8,256]{2,1,0:T(8,128)S(1)}, u32[]{:S(2)}, u32[]{:S(2)}) async-start(f32[32,8,256]{2,1,0:T(8,128)} %get-tuple-element.16), calls=%async_computation | async-start | bytes 524288 | tf_op jit(solution)/shard_map/all_to_all | solution.py:272
  43.5 1.9 collective-permute-start.13
  45.4 1.4 collective-permute-start.16
  46.8 5.7 %collective-permute-done.13 = bf16[192,256]{1,0:T(8,128)(2,1)S(1)} collective-permute-done((bf16[192,256]{1,0:T(8,128)(2,1)S(1)}, bf16[192,256]{1,0:T(8,128)(2,1)S(1)}, u32[]{:S(2)}, u32[]{:S(2)}) %collective-permute-start.13) | collective-permute-done | bytes 98336 | tf_op jit(solution)/shard_map/ppermute | solution.py:23
  52.6 3.2 collective-permute-start.17
  56.0 3.2 collective-permute-start.7
  59.5 3.3 collective-permute-start.19
  63.7 7.6 %all-to-all-start.1 = ((f32[32,8,256]{2,1,0:T(8,128)}), f32[32,8,256]{2,1,0:T(8,128)}, u32[]{:S(2)}, u32[]{:S(2)}) async-start(f32[32,8,256]{2,1,0:T(8,128)} %broadcast_in_dim.14), calls=%async_computation.1 | async-start | bytes 524288 | tf_op jit(solution)/shard_map/all_to_all | solution.py:272
  71.4 1.8 collective-permute-start.5
  73.2 1.5 collective-permute-start.8
  74.7 1.8 collective-permute-start.20
  76.5 1.5 collective-permute-start.21
  78.1 7.1 %collective-permute-done.5 = bf16[4,192,256]{2,1,0:T(8,128)(2,1)} collective-permute-done((bf16[4,192,256]{2,1,0:T(8,128)(2,1)}, bf16[4,192,256]{2,1,0:T(8,128)(2,1)}, u32[]{:S(2)}, u32[]{:S(2)}) %collective-permute-start.5) | collective-permute-done | bytes 393248 | tf_op jit(solution)/shard_map/ppermute | solution.py:23
  85.2 3.2 collective-permute-start.9
  88.5 3.1 copy.34.left_ref
  92.8 1.7 fusion.10
  95.1 1.5 collective-permute-start.22
  96.7 1.8 collective-permute-start.23
  100.5 3.3 collective-permute-start.11
  104.9 1.1 bitcast_dynamic-update-slice_fusion.5
  110.3 1.6 pad_maximum_fusion
  111.9 10.7 %proj_gate_up.1 = f32[2,192,32]{2,1,0:T(8,128)S(1)} custom-call(s32[2]{0:T(128)S(1)} %pad_add_fusion.pos_ref, bf16[32,192,256]{2,1,0:T(8,128)(2,1)S(1)} %bitcast.102, bf16[2,8192,32]{2,1,0:T(8,128)(2,1)} %copy.34.left_ref), custom_call_target="tpu_custom_call" | custom-call | flops 201326592 | bytes 8000000 | tf_op jit(solution)/shard_map/proj_gate_up/pallas_call | solution.py:92
  123.2 1.6 copy-done
  124.8 13.7 %grad_act.1 = (f32[192,512]{1,0:T(8,128)S(1)}, f32[192,32]{1,0:T(8,128)S(1)}) custom-call(s32[2]{0:T(128)S(1)} %pad_add_fusion.pos_ref, bf16[32,192,256]{2,1,0:T(8,128)(2,1)} %bitcast.104, f32[32,1,256]{2,1,0:T(1,128)S(1)} %get-tuple-element.31.scale_ref, bf16[512,8192]{1,0:T(8,128)(2,1)} %get-tuple-element.17.tile_ref, bf16[32,8192]{1,0:T(8,128)(2,1)S(1)} %copy-done.6), custom_call_target="tpu_custom_call" | custom-call | flops 1610612736 | bytes 12000000 | tf_op jit(solution)/shard_map/grad_act/pallas_call | solution.py:129
  139.9 26.3 %gate_up.1 = (bf16[2,8192,512]{2,1,0:T(8,128)(2,1)}, f32[2,192,512]{2,1,0:T(8,128)S(1)}, f32[2,8,512]{2,1,0:T(8,128)S(1)}) custom-call(s32[2]{0:T(128)S(1)} %pad_add_fusion.pos_ref, bf16[32,192,256]{2,1,0:T(8,128)(2,1)S(1)} %bitcast.103, bf16[2,8192,512]{2,1,0:T(8,128)(2,1)} %all-gather.2.cloned.1.call-done.frozen_ref, bf16[2,8192,32]{2,1,0:T(8,128)(2,1)} %copy.34.left_ref, ...), custom_call_target="tpu_custom_call" | custom-call | flops 3221225472 | bytes 36000000 | tf_op jit(solution)/shard_map/gate_up/pallas_call | solution.py:208
  167.2 1.3 broadcast_multiply_fusion
  168.5 2.1 multiply_bitcast_fusion.1
  170.8 1.7 fusion.13
  172.5 1.6 copy.37
  174.0 1.1 fusion.14
  175.2 1.6 fusion.2
  176.8 6.2 %all-to-all-start.8 = ((f32[32,8,128]{2,1,0:T(8,128)}), f32[32,8,128]{2,1,0:T(8,128)}, u32[]{:S(2)}, u32[]{:S(2)}) async-start(f32[32,8,128]{2,1,0:T(8,128)} %fusion.2), calls=%async_computation.8 | async-start | bytes 262144 | tf_op jit(solution)/shard_map/all_to_all | solution.py:272
  183.0 1.8 convolution_multiply_fusion.2
  184.8 1.8 convolution_multiply_fusion
  186.6 6.7 %all-to-all-done.8 = f32[32,8,128]{2,1,0:T(8,128)} async-done(((f32[32,8,128]{2,1,0:T(8,128)}), f32[32,8,128]{2,1,0:T(8,128)}, u32[]{:S(2)}, u32[]{:S(2)}) %all-to-all-start.8) | async-done | bytes 131104 | tf_op jit(solution)/shard_map/all_to_all | solution.py:272
  194.9 4.8 %all-to-all-start.9 = ((bf16[32,8,128]{2,1,0:T(8,128)(2,1)}), bf16[32,8,128]{2,1,0:T(8,128)(2,1)}, u32[]{:S(2)}, u32[]{:S(2)}) async-start(bf16[32,8,128]{2,1,0:T(8,128)(2,1)} %broadcast_in_dim.17), calls=%async_computation.9 | async-start | bytes 131072 | tf_op jit(solution)/shard_map/all_to_all | solution.py:272
  200.7 11.6 %dot_down.1 = f32[32,8,256]{2,1,0:T(8,128)S(1)} custom-call(s32[2]{0:T(128)S(1)} %pad_add_fusion.pos_ref, bf16[32,192,256]{2,1,0:T(8,128)(2,1)S(1)} %bitcast.105, bf16[192,512]{1,0:T(8,128)(2,1)S(1)} %copy-done.4, bf16[512,8192]{1,0:T(8,128)(2,1)} %get-tuple-element.17.tile_ref), custom_call_target="tpu_custom_call" | custom-call | flops 1610612736 | bytes 12000000 | tf_op jit(solution)/shard_map/dot_down/pallas_call | solution.py:165
  213.0 9.7 %all-to-all-start.10 = ((f32[32,8,256]{2,1,0:T(8,128)}), f32[32,8,256]{2,1,0:T(8,128)S(1)}, u32[]{:S(2)}, u32[]{:S(2)}) async-start(f32[32,8,256]{2,1,0:T(8,128)} %copy-done.7), calls=%async_computation.10 | async-start | bytes 524288 | tf_op jit(solution)/shard_map/all_to_all | solution.py:272
  222.7 1.7 maximum_maximum_fusion
  226.3 7.2 %all-to-all-done.10 = f32[32,8,256]{2,1,0:T(8,128)S(1)} async-done(((f32[32,8,256]{2,1,0:T(8,128)}), f32[32,8,256]{2,1,0:T(8,128)S(1)}, u32[]{:S(2)}, u32[]{:S(2)}) %all-to-all-start.10) | async-done | bytes 262176 | tf_op jit(solution)/shard_map/all_to_all | solution.py:272
  233.5 4.8 %all-to-all-start.6 = ((f32[8,16,512]{2,1,0:T(8,128)}), f32[8,16,512]{2,1,0:T(8,128)S(1)}, u32[]{:S(2)}, u32[]{:S(2)}) async-start(f32[8,16,512]{2,1,0:T(8,128)} %bitcast.34), calls=%async_computation.6 | async-start | bytes 524288 | tf_op jit(solution)/shard_map/all_to_all | solution.py:272
  238.4 1.1 convolution_multiply_fusion.3
  239.6 1.3 maximum_maximum_fusion.1
  240.9 3.6 all-to-all-done.6
  244.5 4.7 %all-to-all-start.11 = ((f32[8,16,256]{2,1,0:T(8,128)}), f32[8,16,256]{2,1,0:T(8,128)S(1)}, u32[]{:S(2)}, u32[]{:S(2)}) async-start(f32[8,16,256]{2,1,0:T(8,128)} %bitcast.42), calls=%async_computation.11 | async-start | bytes 262144 | tf_op jit(solution)/shard_map/all_to_all | solution.py:272
  249.2 4.7 %all-to-all-done.11 = f32[8,16,256]{2,1,0:T(8,128)S(1)} async-done(((f32[8,16,256]{2,1,0:T(8,128)}), f32[8,16,256]{2,1,0:T(8,128)S(1)}, u32[]{:S(2)}, u32[]{:S(2)}) %all-to-all-start.11) | async-done | bytes 131104 | tf_op jit(solution)/shard_map/all_to_all | solution.py:272
  254.6 4.8 %all-to-all-start.7 = ((f32[8,16,512]{2,1,0:T(8,128)}), f32[8,16,512]{2,1,0:T(8,128)S(1)}, u32[]{:S(2)}, u32[]{:S(2)}) async-start(f32[8,16,512]{2,1,0:T(8,128)} %broadcast_in_dim.16), calls=%async_computation.7 | async-start | bytes 524288 | tf_op jit(solution)/shard_map/all_to_all | solution.py:272
  259.4 6.1 %all-to-all-done.7 = f32[8,16,512]{2,1,0:T(8,128)S(1)} async-done(((f32[8,16,512]{2,1,0:T(8,128)}), f32[8,16,512]{2,1,0:T(8,128)S(1)}, u32[]{:S(2)}, u32[]{:S(2)}) %all-to-all-start.7) | async-done | bytes 262176 | tf_op jit(solution)/shard_map/all_to_all | solution.py:272
  266.2 4.7 %all-to-all-start.12 = ((f32[8,16,256]{2,1,0:T(8,128)}), f32[8,16,256]{2,1,0:T(8,128)S(1)}, u32[]{:S(2)}, u32[]{:S(2)}) async-start(f32[8,16,256]{2,1,0:T(8,128)} %broadcast_in_dim.38), calls=%async_computation.12 | async-start | bytes 262144 | tf_op jit(solution)/shard_map/all_to_all | solution.py:272
  270.9 15.8 %grad_in.1 = (bf16[4,8,128,256]{3,2,1,0:T(8,128)(2,1)}, bf16[8,4,64,256]{3,2,1,0:T(8,128)(2,1)S(1)}) custom-call(bf16[2,192,512]{2,1,0:T(8,128)(2,1)S(1)} %get-tuple-element.29.grads_ref, bf16[2,8192,512]{2,1,0:T(8,128)(2,1)} %get-tuple-element.21.tile_ref), custom_call_target="tpu_custom_call" | custom-call | flops 3221225472 | bytes 20000000 | tf_op jit(solution)/shard_map/grad_in/pallas_call | solution.py:250
  286.7 32.3 %all_to_all.65 = bf16[8,4,64,256]{3,2,1,0:T(8,128)(2,1)S(1)} all-to-all(bf16[8,4,64,256]{3,2,1,0:T(8,128)(2,1)S(1)} %get-tuple-element.23), channel_id=1, replica_groups=mesh['x'=4,'core'=2,'y'=4,'z'=8] {'z'}, dimensions={0} | all-to-all | bytes 2097152 | tf_op jit(solution)/shard_map/all_to_all | solution.py:272
  319.1 3.6 all-to-all-start.2
  323.5 24.7 %all-to-all-done.2 = bf16[4,8,128,256]{3,2,1,0:T(8,128)(2,1)S(1)} async-done(((bf16[4,8,128,256]{3,2,1,0:T(8,128)(2,1)}), bf16[4,8,128,256]{3,2,1,0:T(8,128)(2,1)S(1)}, u32[]{:S(2)}, u32[]{:S(2)}) %all-to-all-start.2) | async-done | bytes 2097184 | tf_op jit(solution)/shard_map/all_to_all | solution.py:272
  348.2 3.3 all-to-all-start.5
  351.6 1.3 reduce_sum.115
  352.8 4.7 %all-to-all-done.5 = bf16[4,64,256]{2,1,0:T(8,128)(2,1)S(1)} async-done(((bf16[4,64,256]{2,1,0:T(8,128)(2,1)}), bf16[4,64,256]{2,1,0:T(8,128)(2,1)S(1)}, u32[]{:S(2)}, u32[]{:S(2)}) %all-to-all-start.5) | async-done | bytes 131104 | tf_op jit(solution)/shard_map/all_to_all | solution.py:272
  357.5 3.5 all-to-all-start.3
  365.5 10.1 %all-to-all-done.3 = bf16[8,128,256]{2,1,0:T(8,128)(2,1)S(1)} async-done(((bf16[8,128,256]{2,1,0:T(8,128)(2,1)}), bf16[8,128,256]{2,1,0:T(8,128)(2,1)S(1)}, u32[]{:S(2)}, u32[]{:S(2)}) %all-to-all-start.3) | async-done | bytes 524320 | tf_op jit(solution)/shard_map/all_to_all | solution.py:272
  (149 shorter events, 29.3 us)
Async XLA Ops:
  7.2 132.7 %all-gather.2.cloned.1.call-start = ((), (), s32[]{:S(2)}) async-start(), calls=%async_computation.13 | async-start | bytes 18874368 | tf_op jit(solution)/shard_map/all_gather | solution.py:299
  7.9 9.2 %collective-permute-start = (bf16[192,256]{1,0:T(8,128)(2,1)}, bf16[192,256]{1,0:T(8,128)(2,1)S(1)}, u32[]{:S(2)}, u32[]{:S(2)}) collective-permute-start(bf16[192,256]{1,0:T(8,128)(2,1)} %param.11), channel_id=1, source_target_pairs={{0,8},{8,16},{16,24},{24,0},{1,9},{9,17},{17,25},{25,1},{2,10},{10... | collective-permute-start | bytes 294920 | tf_op jit(solution)/shard_map/ppermute | solution.py:23
  9.6 8.0 %collective-permute-start.1 = (bf16[192,256]{1,0:T(8,128)(2,1)}, bf16[192,256]{1,0:T(8,128)(2,1)S(1)}, u32[]{:S(2)}, u32[]{:S(2)}) collective-permute-start(bf16[192,256]{1,0:T(8,128)(2,1)} %param.11), channel_id=1, source_target_pairs={{0,24},{8,0},{16,8},{24,16},{1,25},{9,1},{17,9},{25,17},{2,26},{10... | collective-permute-start | bytes 294920 | tf_op jit(solution)/shard_map/ppermute | solution.py:24
  11.2 32.3 %collective-permute-start.12 = (bf16[192,256]{1,0:T(8,128)(2,1)}, bf16[192,256]{1,0:T(8,128)(2,1)S(1)}, u32[]{:S(2)}, u32[]{:S(2)}) collective-permute-start(bf16[192,256]{1,0:T(8,128)(2,1)} %param.10), channel_id=1, source_target_pairs={{0,1},{1,2},{2,3},{3,4},{4,5},{5,6},{6,7},{7,0},{8,9},{9,10},{10,1... | collective-permute-start | bytes 294920 | tf_op jit(solution)/shard_map/ppermute | solution.py:23
  13.1 32.2 %collective-permute-start.15 = (bf16[192,256]{1,0:T(8,128)(2,1)}, bf16[192,256]{1,0:T(8,128)(2,1)S(1)}, u32[]{:S(2)}, u32[]{:S(2)}) collective-permute-start(bf16[192,256]{1,0:T(8,128)(2,1)} %param.10), channel_id=1, source_target_pairs={{0,7},{1,0},{2,1},{3,2},{4,3},{5,4},{6,5},{7,6},{8,15},{9,8},{10,9... | collective-permute-start | bytes 294920 | tf_op jit(solution)/shard_map/ppermute | solution.py:24
  17.1 38.7 %copy-start.20 = (bf16[192,256]{1,0:T(8,128)(2,1)}, bf16[192,256]{1,0:T(8,128)(2,1)S(1)}, u32[]{:S(2)}) copy-start(bf16[192,256]{1,0:T(8,128)(2,1)S(1)} %collective-permute-done) | copy-start | bytes 294916
  17.1 29.7 %collective-permute-start.2 = (bf16[96,256]{1,0:T(8,128)(2,1)S(1)}, bf16[96,256]{1,0:T(8,128)(2,1)S(1)}, u32[]{:S(2)}, u32[]{:S(2)}) collective-permute-start(bf16[96,256]{1,0:T(8,128)(2,1)S(1)} %slice.95), channel_id=1, source_target_pairs={{0,8},{8,16},{16,24},{24,0},{1,9},{9,17},{17,25},{25,1},{2,10},{10... | collective-permute-start | bytes 147464 | tf_op jit(solution)/shard_map/ppermute | solution.py:27
  17.5 38.3 %copy-start.22 = (bf16[192,256]{1,0:T(8,128)(2,1)}, bf16[192,256]{1,0:T(8,128)(2,1)S(1)}, u32[]{:S(2)}) copy-start(bf16[192,256]{1,0:T(8,128)(2,1)S(1)} %collective-permute-done.1) | copy-start | bytes 294916
  17.5 29.3 %collective-permute-start.3 = (bf16[96,256]{1,0:T(8,128)(2,1)S(1)}, bf16[96,256]{1,0:T(8,128)(2,1)S(1)}, u32[]{:S(2)}, u32[]{:S(2)}) collective-permute-start(bf16[96,256]{1,0:T(8,128)(2,1)S(1)} %slice.96), channel_id=1, source_target_pairs={{0,24},{8,0},{16,8},{24,16},{1,25},{9,1},{17,9},{25,17},{2,26},{10... | collective-permute-start | bytes 147464 | tf_op jit(solution)/shard_map/ppermute | solution.py:27
  21.4 1.0 copy-start.5
  22.4 33.4 %copy-start.17 = (bf16[192,256]{1,0:T(8,128)(2,1)S(1)}, bf16[192,256]{1,0:T(8,128)(2,1)}, u32[]{:S(2)}) copy-start(bf16[192,256]{1,0:T(8,128)(2,1)} %param.11) | copy-start | bytes 294916
  22.4 40.5 %copy-start.24 = (bf16[192,256]{1,0:T(8,128)(2,1)S(1)}, bf16[192,256]{1,0:T(8,128)(2,1)}, u32[]{:S(2)}) copy-start(bf16[192,256]{1,0:T(8,128)(2,1)} %param.10) | copy-start | bytes 294916
  37.0 51.5 %copy-start.14 = (bf16[2,8192,32]{1,2,0:T(8,128)(2,1)S(1)}, bf16[2,8192,32]{1,2,0:T(8,128)(2,1)}, u32[]{:S(2)}) copy-start(bf16[2,8192,32]{1,2,0:T(8,128)(2,1)} %param.13) | copy-start | bytes 3145732
  37.0 25.9 %all-to-all-start = ((f32[32,8,256]{2,1,0:T(8,128)}), f32[32,8,256]{2,1,0:T(8,128)S(1)}, u32[]{:S(2)}, u32[]{:S(2)}) async-start(f32[32,8,256]{2,1,0:T(8,128)} %get-tuple-element.16), calls=%async_computation | async-start | bytes 524288 | tf_op jit(solution)/shard_map/all_to_all | solution.py:272
  43.5 9.1 %collective-permute-start.13 = (bf16[192,256]{1,0:T(8,128)(2,1)S(1)}, bf16[192,256]{1,0:T(8,128)(2,1)S(1)}, u32[]{:S(2)}, u32[]{:S(2)}) collective-permute-start(bf16[192,256]{1,0:T(8,128)(2,1)S(1)} %collective-permute-done.12), channel_id=1, source_target_pairs={{0,1},{1,2},{2,3},{3,4},{4,5},{5,6},{6,7},{7,0},{8,9},{9,10},{10,1... | collective-permute-start | bytes 294920 | tf_op jit(solution)/shard_map/ppermute | solution.py:23
  45.4 7.2 %collective-permute-start.16 = (bf16[192,256]{1,0:T(8,128)(2,1)S(1)}, bf16[192,256]{1,0:T(8,128)(2,1)S(1)}, u32[]{:S(2)}, u32[]{:S(2)}) collective-permute-start(bf16[192,256]{1,0:T(8,128)(2,1)S(1)} %collective-permute-done.15), channel_id=1, source_target_pairs={{0,7},{1,0},{2,1},{3,2},{4,3},{5,4},{6,5},{7,6},{8,15},{9,8},{10,9... | collective-permute-start | bytes 294920 | tf_op jit(solution)/shard_map/ppermute | solution.py:24
  46.8 12.7 %copy-start.18 = (bf16[1,192,256]{2,1,0:T(8,128)(2,1)}, bf16[1,192,256]{2,1,0:T(8,128)(2,1)S(1)}, u32[]{:S(2)}) copy-start(bf16[1,192,256]{2,1,0:T(8,128)(2,1)S(1)} %maximum_bitcast_fusion.2) | copy-start | bytes 294916
  52.6 6.9 %collective-permute-start.14 = (bf16[192,256]{1,0:T(8,128)(2,1)S(1)}, bf16[192,256]{1,0:T(8,128)(2,1)S(1)}, u32[]{:S(2)}, u32[]{:S(2)}) collective-permute-start(bf16[192,256]{1,0:T(8,128)(2,1)S(1)} %collective-permute-done.13), channel_id=1, source_target_pairs={{0,1},{1,2},{2,3},{3,4},{4,5},{5,6},{6,7},{7,0},{8,9},{9,10},{10,1... | collective-permute-start | bytes 294920 | tf_op jit(solution)/shard_map/ppermute | solution.py:23
  52.6 7.0 %collective-permute-start.17 = (bf16[192,256]{1,0:T(8,128)(2,1)S(1)}, bf16[192,256]{1,0:T(8,128)(2,1)S(1)}, u32[]{:S(2)}, u32[]{:S(2)}) collective-permute-start(bf16[192,256]{1,0:T(8,128)(2,1)S(1)} %collective-permute-done.16), channel_id=1, source_target_pairs={{0,7},{1,0},{2,1},{3,2},{4,3},{5,4},{6,5},{7,6},{8,15},{9,8},{10,9... | collective-permute-start | bytes 294920 | tf_op jit(solution)/shard_map/ppermute | solution.py:24
  55.9 15.5 %collective-permute-start.4 = (bf16[4,192,256]{2,1,0:T(8,128)(2,1)S(1)}, bf16[4,192,256]{2,1,0:T(8,128)(2,1)}, u32[]{:S(2)}, u32[]{:S(2)}) collective-permute-start(bf16[4,192,256]{2,1,0:T(8,128)(2,1)S(1)} %pad_maximum_fusion.2), channel_id=1, source_target_pairs={{0,1},{1,2},{2,3},{3,4},{4,5},{5,6},{6,7},{7,0},{8,9},{9,10},{10,1... | collective-permute-start | bytes 1179656 | tf_op jit(solution)/shard_map/ppermute | solution.py:23
  56.0 17.2 %collective-permute-start.7 = (bf16[4,192,256]{2,1,0:T(8,128)(2,1)S(1)}, bf16[4,192,256]{2,1,0:T(8,128)(2,1)}, u32[]{:S(2)}, u32[]{:S(2)}) collective-permute-start(bf16[4,192,256]{2,1,0:T(8,128)(2,1)S(1)} %pad_maximum_fusion.2), channel_id=1, source_target_pairs={{0,7},{1,0},{2,1},{3,2},{4,3},{5,4},{6,5},{7,6},{8,15},{9,8},{10,9... | collective-permute-start | bytes 1179656 | tf_op jit(solution)/shard_map/ppermute | solution.py:24
  59.5 15.2 %collective-permute-start.18 = (bf16[96,256]{1,0:T(8,128)(2,1)S(1)}, bf16[96,256]{1,0:T(8,128)(2,1)S(1)}, u32[]{:S(2)}, u32[]{:S(2)}) collective-permute-start(bf16[96,256]{1,0:T(8,128)(2,1)S(1)} %slice.100), channel_id=1, source_target_pairs={{0,1},{1,2},{2,3},{3,4},{4,5},{5,6},{6,7},{7,0},{8,9},{9,10},{10,1... | collective-permute-start | bytes 147464 | tf_op jit(solution)/shard_map/ppermute | solution.py:27
  59.5 15.2 %collective-permute-start.19 = (bf16[96,256]{1,0:T(8,128)(2,1)S(1)}, bf16[96,256]{1,0:T(8,128)(2,1)S(1)}, u32[]{:S(2)}, u32[]{:S(2)}) collective-permute-start(bf16[96,256]{1,0:T(8,128)(2,1)S(1)} %slice.101), channel_id=1, source_target_pairs={{0,7},{1,0},{2,1},{3,2},{4,3},{5,4},{6,5},{7,6},{8,15},{9,8},{10,9... | collective-permute-start | bytes 147464 | tf_op jit(solution)/shard_map/ppermute | solution.py:27
  63.0 29.8 %copy-start.25 = (f32[8192]{0:T(1024)S(1)}, f32[8192]{0:T(1024)}, u32[]{:S(2)}) copy-start(f32[8192]{0:T(1024)} %param.19) | copy-start | bytes 98308
  63.7 29.1 %all-to-all-start.1 = ((f32[32,8,256]{2,1,0:T(8,128)}), f32[32,8,256]{2,1,0:T(8,128)}, u32[]{:S(2)}, u32[]{:S(2)}) async-start(f32[32,8,256]{2,1,0:T(8,128)} %broadcast_in_dim.14), calls=%async_computation.1 | async-start | bytes 524288 | tf_op jit(solution)/shard_map/all_to_all | solution.py:272
  71.4 13.8 %collective-permute-start.5 = (bf16[4,192,256]{2,1,0:T(8,128)(2,1)}, bf16[4,192,256]{2,1,0:T(8,128)(2,1)}, u32[]{:S(2)}, u32[]{:S(2)}) collective-permute-start(bf16[4,192,256]{2,1,0:T(8,128)(2,1)} %collective-permute-done.4), channel_id=1, source_target_pairs={{0,1},{1,2},{2,3},{3,4},{4,5},{5,6},{6,7},{7,0},{8,9},{9,10},{10,1... | collective-permute-start | bytes 1179656 | tf_op jit(solution)/shard_map/ppermute | solution.py:23
  73.2 12.0 %collective-permute-start.8 = (bf16[4,192,256]{2,1,0:T(8,128)(2,1)}, bf16[4,192,256]{2,1,0:T(8,128)(2,1)}, u32[]{:S(2)}, u32[]{:S(2)}) collective-permute-start(bf16[4,192,256]{2,1,0:T(8,128)(2,1)} %collective-permute-done.7), channel_id=1, source_target_pairs={{0,7},{1,0},{2,1},{3,2},{4,3},{5,4},{6,5},{7,6},{8,15},{9,8},{10,9... | collective-permute-start | bytes 1179656 | tf_op jit(solution)/shard_map/ppermute | solution.py:24
  74.7 21.9 %copy-start.15 = (bf16[8,192,256]{2,1,0:T(8,128)(2,1)}, bf16[8,192,256]{2,1,0:T(8,128)(2,1)S(1)}, u32[]{:S(2)}) copy-start(bf16[8,192,256]{2,1,0:T(8,128)(2,1)S(1)} %fusion.3) | copy-start | bytes 2359300
  74.7 20.3 %collective-permute-start.20 = (bf16[8,192,256]{2,1,0:T(8,128)(2,1)S(1)}, bf16[8,192,256]{2,1,0:T(8,128)(2,1)S(1)}, u32[]{:S(2)}, u32[]{:S(2)}) collective-permute-start(bf16[8,192,256]{2,1,0:T(8,128)(2,1)S(1)} %fusion.3), channel_id=1, source_target_pairs={{0,8},{8,16},{16,24},{24,0},{1,9},{9,17},{17,25},{25,1},{2,10},{10... | collective-permute-start | bytes 2359304 | tf_op jit(solution)/shard_map/ppermute | solution.py:23
  76.5 20.1 %collective-permute-start.21 = (bf16[8,192,256]{2,1,0:T(8,128)(2,1)S(1)}, bf16[8,192,256]{2,1,0:T(8,128)(2,1)S(1)}, u32[]{:S(2)}, u32[]{:S(2)}) collective-permute-start(bf16[8,192,256]{2,1,0:T(8,128)(2,1)S(1)} %fusion.3), channel_id=1, source_target_pairs={{0,24},{8,0},{16,8},{24,16},{1,25},{9,1},{17,9},{25,17},{2,26},{10... | collective-permute-start | bytes 2359304 | tf_op jit(solution)/shard_map/ppermute | solution.py:24
  85.2 13.3 %collective-permute-start.6 = (bf16[4,192,256]{2,1,0:T(8,128)(2,1)}, bf16[4,192,256]{2,1,0:T(8,128)(2,1)}, u32[]{:S(2)}, u32[]{:S(2)}) collective-permute-start(bf16[4,192,256]{2,1,0:T(8,128)(2,1)} %collective-permute-done.5), channel_id=1, source_target_pairs={{0,1},{1,2},{2,3},{3,4},{4,5},{5,6},{6,7},{7,0},{8,9},{9,10},{10,1... | collective-permute-start | bytes 1179656 | tf_op jit(solution)/shard_map/ppermute | solution.py:23
  85.2 14.4 %collective-permute-start.9 = (bf16[4,192,256]{2,1,0:T(8,128)(2,1)}, bf16[4,192,256]{2,1,0:T(8,128)(2,1)}, u32[]{:S(2)}, u32[]{:S(2)}) collective-permute-start(bf16[4,192,256]{2,1,0:T(8,128)(2,1)} %collective-permute-done.8), channel_id=1, source_target_pairs={{0,7},{1,0},{2,1},{3,2},{4,3},{5,4},{6,5},{7,6},{8,15},{9,8},{10,9... | collective-permute-start | bytes 1179656 | tf_op jit(solution)/shard_map/ppermute | solution.py:24
  91.6 15.4 %copy-start.19 = (bf16[1,192,256]{2,1,0:T(8,128)(2,1)S(1)}, bf16[1,192,256]{2,1,0:T(8,128)(2,1)}, u32[]{:S(2)}) copy-start(bf16[1,192,256]{2,1,0:T(8,128)(2,1)} %copy-done.18) | copy-start | bytes 294916
  91.6 15.4 %copy-start.21 = (bf16[192,256]{1,0:T(8,128)(2,1)S(1)}, bf16[192,256]{1,0:T(8,128)(2,1)}, u32[]{:S(2)}) copy-start(bf16[192,256]{1,0:T(8,128)(2,1)} %copy-done.20) | copy-start | bytes 294916
  91.6 15.4 %copy-start.23 = (bf16[192,256]{1,0:T(8,128)(2,1)S(1)}, bf16[192,256]{1,0:T(8,128)(2,1)}, u32[]{:S(2)}) copy-start(bf16[192,256]{1,0:T(8,128)(2,1)} %copy-done.22) | copy-start | bytes 294916
  95.0 13.0 %copy-start.12 = (bf16[8,192,256]{2,1,0:T(8,128)(2,1)}, bf16[8,192,256]{2,1,0:T(8,128)(2,1)S(1)}, u32[]{:S(2)}) copy-start(bf16[8,192,256]{2,1,0:T(8,128)(2,1)S(1)} %collective-permute-done.20) | copy-start | bytes 2359300
  95.1 15.1 %collective-permute-start.22 = (bf16[4,192,256]{2,1,0:T(8,128)(2,1)S(1)}, bf16[4,192,256]{2,1,0:T(8,128)(2,1)S(1)}, u32[]{:S(2)}, u32[]{:S(2)}) collective-permute-start(bf16[4,192,256]{2,1,0:T(8,128)(2,1)S(1)} %slice.102), channel_id=1, source_target_pairs={{0,8},{8,16},{16,24},{24,0},{1,9},{9,17},{17,25},{25,1},{2,10},{10... | collective-permute-start | bytes 1179656 | tf_op jit(solution)/shard_map/ppermute | solution.py:27
  96.6 12.5 %copy-start.13 = (bf16[8,192,256]{2,1,0:T(8,128)(2,1)}, bf16[8,192,256]{2,1,0:T(8,128)(2,1)S(1)}, u32[]{:S(2)}) copy-start(bf16[8,192,256]{2,1,0:T(8,128)(2,1)S(1)} %collective-permute-done.21) | copy-start | bytes 2359300
  96.7 13.5 %collective-permute-start.23 = (bf16[4,192,256]{2,1,0:T(8,128)(2,1)S(1)}, bf16[4,192,256]{2,1,0:T(8,128)(2,1)S(1)}, u32[]{:S(2)}, u32[]{:S(2)}) collective-permute-start(bf16[4,192,256]{2,1,0:T(8,128)(2,1)S(1)} %slice.103), channel_id=1, source_target_pairs={{0,24},{8,0},{16,8},{24,16},{1,25},{9,1},{17,9},{25,17},{2,26},{10... | collective-permute-start | bytes 1179656 | tf_op jit(solution)/shard_map/ppermute | solution.py:27
  99.5 23.1 %collective-permute-start.10 = (bf16[2,192,256]{2,1,0:T(8,128)(2,1)S(1)}, bf16[2,192,256]{2,1,0:T(8,128)(2,1)S(1)}, u32[]{:S(2)}, u32[]{:S(2)}) collective-permute-start(bf16[2,192,256]{2,1,0:T(8,128)(2,1)S(1)} %slice.97), channel_id=1, source_target_pairs={{0,1},{1,2},{2,3},{3,4},{4,5},{5,6},{6,7},{7,0},{8,9},{9,10},{10,1... | collective-permute-start | bytes 589832 | tf_op jit(solution)/shard_map/ppermute | solution.py:27
  100.5 22.0 %collective-permute-start.11 = (bf16[2,192,256]{2,1,0:T(8,128)(2,1)S(1)}, bf16[2,192,256]{2,1,0:T(8,128)(2,1)S(1)}, u32[]{:S(2)}, u32[]{:S(2)}) collective-permute-start(bf16[2,192,256]{2,1,0:T(8,128)(2,1)S(1)} %slice.98), channel_id=1, source_target_pairs={{0,7},{1,0},{2,1},{3,2},{4,3},{5,4},{6,5},{7,6},{8,15},{9,8},{10,9... | collective-permute-start | bytes 589832 | tf_op jit(solution)/shard_map/ppermute | solution.py:27
  104.8 5.4 %copy-start.16 = (bf16[8,192,256]{2,1,0:T(8,128)(2,1)S(1)}, bf16[8,192,256]{2,1,0:T(8,128)(2,1)}, u32[]{:S(2)}) copy-start(bf16[8,192,256]{2,1,0:T(8,128)(2,1)} %copy-done.15) | copy-start | bytes 2359300
  111.8 13.0 %copy-start.6 = (bf16[32,8192]{1,0:T(8,128)(2,1)S(1)}, bf16[32,8192]{1,0:T(8,128)(2,1)}, u32[]{:S(2)}) copy-start(bf16[32,8192]{1,0:T(8,128)(2,1)} %right_ref.4) | copy-start | bytes 1572868
  122.5 0.7 copy-start.8
  123.2 1.6 copy-start
  124.8 15.1 %copy-start.10 = (bf16[2,32,512]{2,1,0:T(8,128)(2,1)S(1)}, bf16[2,32,512]{2,1,0:T(8,128)(2,1)}, u32[]{:S(2)}) copy-start(bf16[2,32,512]{2,1,0:T(8,128)(2,1)} %right_ref.5) | copy-start | bytes 196612
  138.5 0.7 copy-start.9
  139.9 27.3 %copy-start.27 = (f32[2,512]{1,0:T(2,128)S(1)}, f32[2,512]{1,0:T(2,128)}, u32[]{:S(2)}) copy-start(f32[2,512]{1,0:T(2,128)} %param.15) | copy-start | bytes 12292
  166.3 0.9 copy-start.2
  167.2 3.4 copy-start.3
  168.5 31.2 %copy-start.1 = (bf16[8,4,192,256]{3,2,1,0:T(8,128)(2,1)S(1)}, bf16[8,4,192,256]{3,2,1,0:T(8,128)(2,1)}, u32[]{:S(2)}) copy-start(bf16[8,4,192,256]{3,2,1,0:T(8,128)(2,1)} %copy-done) | copy-start | bytes 9437188
  176.8 16.5 %all-to-all-start.8 = ((f32[32,8,128]{2,1,0:T(8,128)}), f32[32,8,128]{2,1,0:T(8,128)}, u32[]{:S(2)}, u32[]{:S(2)}) async-start(f32[32,8,128]{2,1,0:T(8,128)} %fusion.2), calls=%async_computation.8 | async-start | bytes 262144 | tf_op jit(solution)/shard_map/all_to_all | solution.py:272
  194.9 18.1 %all-to-all-start.9 = ((bf16[32,8,128]{2,1,0:T(8,128)(2,1)}), bf16[32,8,128]{2,1,0:T(8,128)(2,1)}, u32[]{:S(2)}, u32[]{:S(2)}) async-start(bf16[32,8,128]{2,1,0:T(8,128)(2,1)} %broadcast_in_dim.17), calls=%async_computation.9 | async-start | bytes 131072 | tf_op jit(solution)/shard_map/all_to_all | solution.py:272
  199.7 0.9 copy-start.4
  200.6 37.7 %copy-start.26 = (f32[1,1,256]{2,1,0:T(1,128)S(1)}, f32[1,1,256]{2,1,0:T(1,128)}, u32[]{:S(2)}) copy-start(f32[1,1,256]{2,1,0:T(1,128)} %constant_dynamic-slice_fusion.1) | copy-start | bytes 3076
  212.3 0.7 copy-start.7
  213.0 20.5 %all-to-all-start.10 = ((f32[32,8,256]{2,1,0:T(8,128)}), f32[32,8,256]{2,1,0:T(8,128)S(1)}, u32[]{:S(2)}, u32[]{:S(2)}) async-start(f32[32,8,256]{2,1,0:T(8,128)} %copy-done.7), calls=%async_computation.10 | async-start | bytes 524288 | tf_op jit(solution)/shard_map/all_to_all | solution.py:272
  233.5 10.9 %all-to-all-start.6 = ((f32[8,16,512]{2,1,0:T(8,128)}), f32[8,16,512]{2,1,0:T(8,128)S(1)}, u32[]{:S(2)}, u32[]{:S(2)}) async-start(f32[8,16,512]{2,1,0:T(8,128)} %bitcast.34), calls=%async_computation.6 | async-start | bytes 524288 | tf_op jit(solution)/shard_map/all_to_all | solution.py:272
  244.5 9.4 %all-to-all-start.11 = ((f32[8,16,256]{2,1,0:T(8,128)}), f32[8,16,256]{2,1,0:T(8,128)S(1)}, u32[]{:S(2)}, u32[]{:S(2)}) async-start(f32[8,16,256]{2,1,0:T(8,128)} %bitcast.42), calls=%async_computation.11 | async-start | bytes 262144 | tf_op jit(solution)/shard_map/all_to_all | solution.py:272
  254.6 10.9 %all-to-all-start.7 = ((f32[8,16,512]{2,1,0:T(8,128)}), f32[8,16,512]{2,1,0:T(8,128)S(1)}, u32[]{:S(2)}, u32[]{:S(2)}) async-start(f32[8,16,512]{2,1,0:T(8,128)} %broadcast_in_dim.16), calls=%async_computation.7 | async-start | bytes 524288 | tf_op jit(solution)/shard_map/all_to_all | solution.py:272
  266.2 20.6 %all-to-all-start.12 = ((f32[8,16,256]{2,1,0:T(8,128)}), f32[8,16,256]{2,1,0:T(8,128)S(1)}, u32[]{:S(2)}, u32[]{:S(2)}) async-start(f32[8,16,256]{2,1,0:T(8,128)} %broadcast_in_dim.38), calls=%async_computation.12 | async-start | bytes 262144 | tf_op jit(solution)/shard_map/all_to_all | solution.py:272
  319.1 29.2 %all-to-all-start.2 = ((bf16[4,8,128,256]{3,2,1,0:T(8,128)(2,1)}), bf16[4,8,128,256]{3,2,1,0:T(8,128)(2,1)S(1)}, u32[]{:S(2)}, u32[]{:S(2)}) async-start(bf16[4,8,128,256]{3,2,1,0:T(8,128)(2,1)} %get-tuple-element.22), calls=%async_computation.2 | async-start | bytes 4194304 | tf_op jit(solution)/shard_map/all_to_all | solution.py:272
  348.2 9.3 %all-to-all-start.5 = ((bf16[4,64,256]{2,1,0:T(8,128)(2,1)}), bf16[4,64,256]{2,1,0:T(8,128)(2,1)S(1)}, u32[]{:S(2)}, u32[]{:S(2)}) async-start(bf16[4,64,256]{2,1,0:T(8,128)(2,1)} %reduce_sum.117), calls=%async_computation.5 | async-start | bytes 262144 | tf_op jit(solution)/shard_map/all_to_all | solution.py:272
  357.5 18.1 %all-to-all-start.3 = ((bf16[8,128,256]{2,1,0:T(8,128)(2,1)}), bf16[8,128,256]{2,1,0:T(8,128)(2,1)S(1)}, u32[]{:S(2)}, u32[]{:S(2)}) async-start(bf16[8,128,256]{2,1,0:T(8,128)(2,1)} %reduce_sum.115), calls=%async_computation.3 | async-start | bytes 1048576 | tf_op jit(solution)/shard_map/all_to_all | solution.py:272
  (1 other events, 0.6 us)
Sparse Core Ops, SparseCore 0:
  9.8 90.0 all-gather.1

commit v2 on v0

v2 whole, which is shorter than its diff:
```python
import functools

import jax
import jax.numpy as jnp
from jax import lax
from jax.experimental import pallas as pl
from jax.experimental.pallas import tpu as pltpu
from jax.sharding import Mesh, PartitionSpec as P

F32, BF16 = jnp.float32, jnp.bfloat16
DP, MP, CMP = ("x", "core"), ("y", "z"), ("core", "y", "z")
NX, NC, NY, NZ = 4, 2, 4, 8
NDP, NMP = NX * NC, NY * NZ
NT = (((1,), (1,)), ((), ()))
TN = (((0,), (0,)), ((), ()))
OTHER = [(0, 1), (1, 0)]
VMEM = 50 * 1024 * 1024


def step(array, axis, n, shift):
    return lax.ppermute(array, axis, [(i, (i + shift) % n) for i in range(n)])


def both_ways(a, b, axis, n):
    return step(a, axis, n, 1), step(b, axis, n, -1)


def nothing(*refs):
    pass


def after(array, *others):
    anywhere = pl.BlockSpec(memory_space=pl.ANY)
    return pl.pallas_call(
        nothing,
        in_specs=[anywhere] * (1 + len(others)),
        out_specs=anywhere,
        out_shape=jax.ShapeDtypeStruct(array.shape, array.dtype),
        input_output_aliases={0: 0},
        name="after",
    )(array, *others)


def stack_body(*refs):
    *pieces, first, second, out = refs
    for i, piece in enumerate(pieces):
        out[i] = piece[...]
    half = first.shape[0]
    out[len(pieces), :half] = first[...]
    out[len(pieces), half:] = second[...]


def stack(pieces, first, second):
    return pl.pallas_call(
        stack_body,
        out_shape=jax.ShapeDtypeStruct((len(pieces) + 1,) + pieces[0].shape, BF16),
        compiler_params=pltpu.CompilerParams(vmem_limit_bytes=VMEM),
        cost_estimate=pl.CostEstimate(flops=0, bytes_accessed=6_000_000, transcendentals=0),
        name="stack",
    )(*pieces, first, second)


def rel(a, b, shift, n):
    return lax.rem(a - b + shift + n, n)


def call(body, name, grid, in_specs, out_specs, out_shape, aliases=None):
    return pl.pallas_call(
        body,
        grid_spec=pltpu.PrefetchScalarGridSpec(
            num_scalar_prefetch=1, grid=grid, in_specs=in_specs, out_specs=out_specs
        ),
        out_shape=out_shape,
        input_output_aliases=aliases or {},
        compiler_params=pltpu.CompilerParams(vmem_limit_bytes=VMEM),
        cost_estimate=pl.CostEstimate(flops=1_000_000_000, bytes_accessed=16_000_000, transcendentals=0),
        name=name,
    )


def merge_down_body(pos_ref, frozen_ref, left_ref, right_ref, tile_ref, squares_ref):
    merged = frozen_ref[...].astype(F32) + 2.0 * lax.dot_general(
        left_ref[...], right_ref[...], TN, preferred_element_type=F32
    )
    tile_ref[...] = merged.astype(BF16)
    rows, cols = merged.shape
    squares = jnp.sum((merged * merged).reshape(rows // 8, 8, cols), axis=0)
    for i in range(cols // 128):
        squares_ref[i] = squares[:, i * 128 : (i + 1) * 128]


def merge_down(pos, frozen, left, right):
    f, d = frozen.shape[0] // NC, frozen.shape[1]
    w = d // NY
    return call(
        merge_down_body,
        "merge_down",
        (NY,),
        [
            pl.BlockSpec((f, w), lambda i, p: (p[1], i)),
            pl.BlockSpec((32, f), lambda i, p: (0, p[1])),
            pl.BlockSpec((32, w), lambda i, p: (0, i)),
        ],
        [
            pl.BlockSpec((f, w), lambda i, p: (0, i)),
            pl.BlockSpec((w // 128, 8, 128), lambda i, p: (i, 0, 0)),
        ],
        [
            jax.ShapeDtypeStruct((f, d), BF16),
            jax.ShapeDtypeStruct((d // 128, 8, 128), F32),
        ],
    )(pos, frozen, left, right)


def x_spec(t, w):
    return pl.BlockSpec((1, NZ, t, w), lambda i, p: (rel(i, p[2], 1, NY), 0, 0, 0))


def g_spec(t, w):
    return pl.BlockSpec((NZ, 1, t, w), lambda i, p: (0, rel(i, p[2], 1, NY), 0, 0))


def proj_body(pos_ref, own_ref, other_ref, left_ref, out_ref):
    @pl.when(pl.program_id(0) == 0)
    def _():
        out_ref[...] = jnp.zeros_like(out_ref)

    total = jnp.zeros(out_ref.shape, F32)
    for i in range(NZ):
        x = jnp.concatenate([own_ref[0, i], other_ref[0, i]])
        cols = slice(i * 256, (i + 1) * 256)
        left = jnp.concatenate([left_ref[0, :, cols], left_ref[1, :, cols]])
        total += lax.dot_general(x, left, NT, preferred_element_type=F32)
    out_ref[...] += total


def proj_gate_up(pos, own, other, left):
    _, _, t, w = own.shape
    return call(
        proj_body,
        "proj_gate_up",
        (NY,),
        [x_spec(t, w), x_spec(t, w), pl.BlockSpec((2, 32, NZ * w), lambda i, p: (0, 0, i))],
        pl.BlockSpec((2 * t, 64), lambda i, p: (0, 0)),
        jax.ShapeDtypeStruct((2 * t, 64), F32),
    )(pos, own, other, left)


def grad_act_body(pos_ref, own_ref, other_ref, scale_ref, tile_ref, right_ref, out_ref, rows_ref):
    @pl.when(pl.program_id(0) == 0)
    def _():
        out_ref[...] = jnp.zeros_like(out_ref)
        rows_ref[...] = jnp.zeros_like(rows_ref)

    total, rows = jnp.zeros(out_ref.shape, F32), jnp.zeros(rows_ref.shape, F32)
    for i in range(NZ):
        q = rel(i, pos_ref[3], 3, NZ)
        g = jnp.concatenate([own_ref[q, 0], other_ref[q, 0]]).astype(F32)
        g = (g * scale_ref[i]).astype(BF16)
        cols = slice(i * 256, (i + 1) * 256)
        total += lax.dot_general(g, tile_ref[:, cols], NT, preferred_element_type=F32)
        rows += lax.dot_general(g, right_ref[:, cols], NT, preferred_element_type=F32)
    out_ref[...] += total
    rows_ref[...] += rows


def grad_act_rows(pos, own, other, scale, tile, right):
    _, _, t, w = own.shape
    f, d = tile.shape
    return call(
        grad_act_body,
        "grad_act",
        (NY,),
        [
            g_spec(t, w),
            g_spec(t, w),
            pl.BlockSpec((NZ, 1, w), lambda i, p: (i, 0, 0)),
            pl.BlockSpec((f, NZ * w), lambda i, p: (0, i)),
            pl.BlockSpec((32, NZ * w), lambda i, p: (0, i)),
        ],
        [
            pl.BlockSpec((2 * t, f), lambda i, p: (0, 0)),
            pl.BlockSpec((2 * t, 32), lambda i, p: (0, 0)),
        ],
        [jax.ShapeDtypeStruct((2 * t, f), F32), jax.ShapeDtypeStruct((2 * t, 32), F32)],
    )(pos, own, other, scale, tile, right)


def dot_down_body(pos_ref, own_ref, other_ref, act_ref, tile_ref, out_ref):
    act = act_ref[...]
    for i in range(NZ):
        q = rel(i, pos_ref[3], 3, NZ)
        g = jnp.concatenate([own_ref[q, 0], other_ref[q, 0]]).astype(F32)
        out_pre = jnp.dot(act, tile_ref[:, i * 256 : (i + 1) * 256], preferred_element_type=F32)
        sums = jnp.sum(g * out_pre, axis=0, keepdims=True)
        out_ref[2 * i] = sums[:, :128]
        out_ref[2 * i + 1] = sums[:, 128:]


def dot_down_sums(pos, own, other, act, tile):
    _, _, t, w = own.shape
    f, d = tile.shape
    return call(
        dot_down_body,
        "dot_down",
        (NY,),
        [
            g_spec(t, w),
            g_spec(t, w),
            pl.BlockSpec((2 * t, f), lambda i, p: (0, 0)),
            pl.BlockSpec((f, NZ * w), lambda i, p: (0, i)),
        ],
        pl.BlockSpec((2 * NZ, 1, 128), lambda i, p: (i, 0, 0)),
        jax.ShapeDtypeStruct((2 * NMP, 1, 128), F32),
    )(pos, own, other, act, tile)


def gate_up_body(pos_ref, own_ref, other_ref, frozen_ref, left_ref, right_ref, tile_ref, pre_ref, squares_ref):
    @pl.when(pl.program_id(0) == 0)
    def _():
        pre_ref[...] = jnp.zeros_like(pre_ref)
        squares_ref[...] = jnp.zeros_like(squares_ref)

    for k in range(2):
        right = right_ref[k]
        pre, squares = jnp.zeros(pre_ref.shape[1:], F32), jnp.zeros(squares_ref.shape[1:], F32)
        for i in range(NZ):
            x = jnp.concatenate([own_ref[0, i], other_ref[0, i]])
            rows = slice(i * 256, (i + 1) * 256)
            merged = frozen_ref[k, rows].astype(F32) + 2.0 * lax.dot_general(
                left_ref[k, :, rows], right, TN, preferred_element_type=F32
            )
            tile = merged.astype(BF16)
            tile_ref[k, rows] = tile
            squares += jnp.sum((merged * merged).reshape(32, 8, -1), axis=0)
            pre += jnp.dot(x, tile, preferred_element_type=F32)
        pre_ref[k] += pre
        squares_ref[k] += squares


def gate_up(pos, own, other, frozen, left, right):
    _, _, t, w = own.shape
    _, d, f = frozen.shape
    f, rows = f // NC, NZ * w
    return call(
        gate_up_body,
        "gate_up",
        (NY,),
        [
            x_spec(t, w),
            x_spec(t, w),
            pl.BlockSpec((2, rows, f), lambda i, p: (0, i, p[1])),
            pl.BlockSpec((2, 32, rows), lambda i, p: (0, 0, i)),
            pl.BlockSpec((2, 32, f), lambda i, p: (0, 0, 0)),
        ],
        [
            pl.BlockSpec((2, rows, f), lambda i, p: (0, i, 0)),
            pl.BlockSpec((2, 2 * t, f), lambda i, p: (0, 0, 0)),
            pl.BlockSpec((2, 8, f), lambda i, p: (0, 0, 0)),
        ],
        [
            jax.ShapeDtypeStruct((2, d, f), BF16),
            jax.ShapeDtypeStruct((2, 2 * t, f), F32),
            jax.ShapeDtypeStruct((2, 8, f), F32),
        ],
    )(pos, own, other, frozen, left, right)


def grad_in_body(pos_ref, grads_ref, tile_ref, own_ref, other_ref):
    t = grads_ref.shape[1] // 2
    for i in range(NZ):
        rows = slice(i * 256, (i + 1) * 256)
        out = lax.dot_general(grads_ref[0], tile_ref[0, rows], NT, preferred_element_type=F32)
        out += lax.dot_general(grads_ref[1], tile_ref[1, rows], NT, preferred_element_type=F32)
        out = out.astype(BF16)
        own_ref[0, i] = out[:t]
        other_ref[0, i] = out[t:]


def grad_in_parts(pos, grads, tiles):
    _, t, f = grads.shape
    out = pl.BlockSpec((1, NZ, t // 2, 256), lambda i, p: (i, 0, 0, 0))
    shape = jax.ShapeDtypeStruct((NY, NZ, t // 2, 256), BF16)
    return call(
        grad_in_body,
        "grad_in",
        (NY,),
        [
            pl.BlockSpec((2, t, f), lambda i, p: (0, 0, 0)),
            pl.BlockSpec((2, NZ * 256, f), lambda i, p: (0, i, 0)),
        ],
        [out, out],
        [shape, shape],
    )(pos, grads, tiles)


def exchange(parts, axes):
    return lax.all_to_all(parts, axes, 0, 0, tiled=True)


def sum_parts(parts, axes):
    return jnp.sum(exchange(parts, axes).astype(F32), axis=0)


def gather_small(own, axes, n):
    return exchange(jnp.broadcast_to(own[None], (n,) + own.shape), axes)


def shards(
    inputs,
    out_grad,
    frozen_gu,
    left_gu,
    right_gu,
    magnitude_gu,
    frozen_down,
    left_down,
    right_down,
    magnitude_down,
):
    tokens, width = inputs.shape
    hidden = frozen_gu.shape[2] // NC
    ix, ic, iy, iz = (lax.axis_index(a) for a in ("x", "core", "y", "z"))
    pos = jnp.stack([ix, ic, iy, iz]).astype(jnp.int32)

    def half_of(array, core, axis):
        return lax.dynamic_slice_in_dim(array, core * hidden, hidden, axis)

    frozen_full = lax.all_gather(frozen_gu, DP, axis=1, tiled=True)
    tile_down, down_squares = merge_down(pos, frozen_down, left_down.T, right_down)
    down_sum = jnp.sum(sum_parts(down_squares, CMP), axis=0, keepdims=True)
    g_y = jnp.stack(
        [step(out_grad, "y", NY, 1), out_grad, step(out_grad, "y", NY, -1), step(out_grad, "y", NY, 2)]
    )
    copies = after(jnp.broadcast_to(inputs[None], (NZ, tokens, width)), down_sum)
    x_z = exchange(copies, "z")
    yr, yl = both_ways(x_z, x_z, "y", NY)
    down_sums = gather_small(jnp.broadcast_to(down_sum, (8, 128)), CMP, NC * NMP)[:, :1]
    yr = after(yr, yl, down_sums)
    yfr, yfl = both_ways(yr[: NZ // 2], yl[NZ // 2 :], "y", NY)
    x_own = stack([yr, x_z, yl], yfr, yfl)
    r1, l1 = both_ways(g_y, g_y, "z", NZ)
    r2, l2 = both_ways(r1, l1, "z", NZ)
    r3, l3 = both_ways(r2, l2, "z", NZ)
    zfr, zfl = both_ways(r3[: NY // 2], l3[NY // 2 :], "z", NZ)
    g_own = stack([r3, r2, r1, g_y, l1, l2, l3], zfr, zfl)
    x_other = lax.ppermute(x_own, "core", OTHER)
    g_other = lax.ppermute(g_own, "core", OTHER)
    right = half_of(right_gu, ic, 2)
    left_t = left_gu.swapaxes(1, 2)

    norm_down = jnp.sqrt(down_sums.reshape(NMP, 1, width) + 1e-06)
    scale_down = magnitude_down.reshape(NMP, 1, width) / norm_down
    grad_act, rows_down = grad_act_rows(pos, g_own, g_other, scale_down, tile_down, right_down)

    proj_gu = proj_gate_up(pos, x_own, x_other, left_t).astype(BF16)
    tiles, pre_gu, squares = gate_up(pos, x_own, x_other, frozen_full, left_t, right)
    norm_gu = jnp.sqrt(jnp.sum(squares, axis=1) + 1e-06)
    scale_gu = half_of(magnitude_gu, ic, 1) / norm_gu
    hid_gu = pre_gu * scale_gu[:, None, :]
    sig = jax.nn.sigmoid(hid_gu[0])
    silu_gate = hid_gu[0] * sig
    act = (silu_gate * hid_gu[1]).astype(BF16)
    grad_gate = grad_act * hid_gu[1] * sig * (1.0 + hid_gu[0] * (1.0 - sig))
    grad_up = grad_act * silu_gate
    grad_hid = jnp.stack([grad_gate, grad_up])
    dot_gu = jnp.sum(grad_hid * pre_gu, axis=1) / norm_gu
    pre_grads = (grad_hid * scale_gu[:, None, :]).astype(BF16)

    own_terms, other_terms = grad_in_parts(pos, pre_grads, tiles)
    from_other = lax.ppermute(other_terms, "core", OTHER)
    terms = (own_terms.astype(F32) + from_other.astype(F32)).astype(BF16)
    grad_in = lax.psum_scatter(lax.psum_scatter(terms, "y").astype(F32), "z")

    rows_gu = [
        lax.dot_general(pre_grads[k], right[k], NT, preferred_element_type=F32) for k in range(2)
    ]
    proj_down = jnp.dot(act, half_of(left_down, ic, 0), preferred_element_type=F32)
    rows = jnp.concatenate(rows_gu + [proj_down, jnp.zeros_like(proj_down)], axis=1)
    rows = rows.reshape(NC, NMP, tokens // NMP, 128)
    rows = jnp.where(ic == 0, rows, rows[::-1]).reshape(NC * NMP, tokens // NMP, 128)
    dots = dot_down_sums(pos, g_own, g_other, act, tile_down)
    rows = jnp.concatenate([rows, dots, jnp.zeros_like(dots)], axis=1)
    rows = gather_small(sum_parts(rows, CMP), CMP, NC * NMP)
    dots = lax.dynamic_slice_in_dim(rows[:, 6], 2 * (iy * NZ + iz), 2, 0).reshape(1, width)
    rows = lax.dynamic_slice_in_dim(rows[:, :6], ic * NMP, NMP, 0).reshape(tokens, 128).astype(BF16)
    own = iy * NZ + iz
    own_scale = lax.dynamic_index_in_dim(scale_down, own, 0, keepdims=False)
    own_norm = lax.dynamic_index_in_dim(norm_down, own, 0, keepdims=False)
    own_grads = (out_grad.astype(F32) * own_scale).astype(BF16)
    left_gu_part = lax.dot_general(rows[:, :64], inputs, TN, preferred_element_type=F32)
    right_down_part = lax.dot_general(rows[:, 64:96], own_grads, TN, preferred_element_type=F32)

    right_gu_parts = [
        lax.dot_general(proj_gu[:, 32 * k : 32 * k + 32], pre_grads[k], TN, preferred_element_type=F32)
        for k in range(2)
    ]
    left_down_part = lax.dot_general(rows_down.astype(BF16), act, TN, preferred_element_type=F32)
    mine = jnp.concatenate(
        [2.0 * p for p in right_gu_parts] + [2.0 * left_down_part, jnp.pad(dot_gu, ((0, 30), (0, 0)))]
    )
    cores = [jnp.where(ic == c, mine, 0.0) for c in range(NC)]
    sums = jnp.concatenate(
        [2.0 * left_gu_part, 2.0 * right_down_part, jnp.pad(0.5 * dots, ((0, 31), (0, 0)))] + cores
    )
    sums = gather_small(sum_parts(sums.reshape(NDP, 48, width), DP), DP, NDP).reshape(384, width)
    cores = sums[128:].reshape(NC, 128, hidden).swapaxes(0, 1).reshape(128, NC * hidden)
    return (
        grad_in.astype(BF16),
        cores[96:98],
        sums[:64].reshape(2, 32, width).swapaxes(1, 2),
        cores[:64].reshape(2, 32, NC * hidden),
        sums[96] / own_norm[0],
        cores[64:96].T,
        sums[64:96],
    )


def solution(mesh):
    fine = Mesh(mesh.devices.reshape(NX, NC, NY, NZ), ("x", "core", "y", "z"))
    in_specs = (
        P(DP, MP),
        P(DP, MP),
        P(None, DP, MP),
        P(),
        P(None, None, MP),
        P(None, MP),
        P(MP, None),
        P(MP, None),
        P(),
        P(),
    )
    out_specs = (
        P(DP, MP),
        P(None, MP),
        P(None, MP, None),
        P(None, None, MP),
        P(MP),
        P(MP, None),
        P(None, MP),
    )
    return jax.shard_map(shards, mesh=fine, in_specs=in_specs, out_specs=out_specs, check_vma=False)
```

time: 1240 us -> 285 us (0.23)
  waiting for transfers between devices: 947 us -> 90.1 us
  blocking collectives: 168 us -> 38.5 us
  matrix products: 97.6 us -> 3.55 us
  starting transfers between devices: 0.54 us -> 54.5 us
  Pallas kernels: 0 us -> 51.2 us
    reduce_scatter x3 -> x2, waiting for transfers between devices: 638 us -> 20.9 us  [shards(): grad_in = lax.psum_scatter(lax.psum_scatter(terms, 'y').astype(F32), 'z')]
    unnamed x9 -> x3, waiting for transfers between devices: 185 us -> 0.71 us
    psum x2 -> x0, blocking collectives: 168 us -> none  [the longest x1 146 us: shards(): down_squares = lax.psum(jnp.sum(merged_down * merged_down, axis=0), 'mp')]
    dot_general x14 -> x8, matrix products: 97.6 us -> 3.55 us  [the longest x2 2.34 us: shards(): lax.dot_general(pre_grads[k], right[k], NT, preferred_element_type=F32)]
    psum x1 -> x0, waiting for transfers between devices: 62.7 us -> none  [shards(): lax.psum((left_gu_own, right_down_own, dot_down_own, dot_gu, right_gu_par...]
    all_gather x3 -> x1, waiting for transfers between devices: 61.6 us -> 0.01 us  [shards(): frozen_full = lax.all_gather(frozen_gu, DP, axis=1, tiled=True)]
    pallas_call x0 -> x10, Pallas kernels: none -> 51.2 us  [the longest x1 13.6 us: gate_up(): call(gate_up_body, 'gate_up', (NY,), [x_spec(t, w), x_spec(t, w), pl.Bloc...]
    all_to_all x0 -> x2, blocking collectives: none -> 38.5 us  [exchange(): return lax.all_to_all(parts, axes, 0, 0, tiled=True)]
  transfers between devices with their start and end apart: 8 -> 26, of which waited for: 6 -> 13; matrix products, arithmetic and copies ran while one was open for 7% -> 8% of each run, Pallas kernels for 0% -> 10%
where the time goes in v2:
time: 285 us; the launch traced here: 282 us
  waiting for transfers between devices  90.1 us (32%)
  starting transfers between devices  54.5 us (19%)
  Pallas kernels  51.2 us (18%)
  blocking collectives  38.5 us (14%)
  local copies, waits for them, and re-layouts  18.7 us (7%)
  between operations  14.3 us (5%)
  other arithmetic  11.2 us (4%)
  matrix products  3.55 us (1%)
    all_to_all x2, blocking collectives, exchange(): return lax.all_to_all(parts, axes, 0, 0, tiled=True)  38.5 us
    all_to_all x5, starting transfers between devices, exchange(): return lax.all_to_all(parts, axes, 0, 0, tiled=True)  33.5 us
    all_to_all x5, waiting for transfers between devices, exchange(): return lax.all_to_all(parts, axes, 0, 0, tiled=True)  31.8 us
    ppermute x15, waiting for transfers between devices, step(): return lax.ppermute(array, axis, [(i, (i + shift) % n) for i in range(n)])  27.4 us
    reduce_scatter x2, waiting for transfers between devices, shards(): grad_in = lax.psum_scatter(lax.psum_scatter(terms, 'y').astype(F32), 'z')  20.9 us
    ppermute x15, starting transfers between devices, step(): return lax.ppermute(array, axis, [(i, (i + shift) % n) for i in range(n)])  20.1 us
    pallas_call x1, Pallas kernels, gate_up(): call(gate_up_body, 'gate_up', (NY,), [x_spec(t, w), x_spec(t, w), pl.Bloc...  13.6 us
    pallas_call x1, Pallas kernels, grad_in_parts(): call(grad_in_body, 'grad_in', (NY,), [pl.BlockSpec((2, t, f), lambda i, p...  8.14 us
  transfers between devices with their start and end apart: 26, of which 13 were waited for; matrix products, arithmetic and copies ran while one was open for 8% of the time, Pallas kernels for 10%

profile of v2, /device:TPU:2, one launch (start us, length us, event | category | flops | bytes accessed | tf_op | source)
XLA Modules:
  0.0 282.1 jit_solution(7821688515959636590)
XLA Ops:
  7.2 0.7 all-gather.2.cloned.1.call-update
  8.0 1.0 copy-done.10
  9.0 0.8 copy-done.16
  9.8 6.4 %merge_down.1 = (bf16[256,8192]{1,0:T(8,128)(2,1)}, f32[64,8,128]{2,1,0:T(8,128)S(1)}) custom-call(s32[4]{0:T(128)S(1)} %pad_add_fusion.pos_ref, bf16[512,8192]{1,0:T(8,128)(2,1)} %frozen_ref.1, bf16[32,512]{1,0:T(8,128)(2,1)S(1)} %bitcast.78, bf16[32,8192]{1,0:T(8,128)(2,1)S(1)} %copy-done.10), custom_call_target="tpu_custom_call" | custom-call | flops 1000000000 | bytes 16000000 | tf_op jit(solution)/shard_map/merge_down/pallas_call | solution.py:95
  16.2 26.4 %all_to_all.35 = f32[64,8,128]{2,1,0:T(8,128)S(1)} all-to-all(f32[64,8,128]{2,1,0:T(8,128)S(1)} %get-tuple-element.16), channel_id=1, replica_groups=mesh['x'=4,'core'=2,'y'=4,'z'=8] {'core','y','z'}, dimensions={0} | all-to-all | bytes 524288 | tf_op jit(solution)/shard_map/all_to_all | solution.py:298
  43.1 0.9 broadcast_in_dim.17.refs_0_
  44.1 3.5 %all-to-all-start.2 = ((bf16[8,192,256]{2,1,0:T(8,128)(2,1)}), bf16[8,192,256]{2,1,0:T(8,128)(2,1)S(1)}, u32[]{:S(2)}, u32[]{:S(2)}) async-start(bf16[8,192,256]{2,1,0:T(8,128)(2,1)} %after.2), calls=%async_computation.2 | async-start | bytes 1572864 | tf_op jit(solution)/shard_map/all_to_all | solution.py:298
  47.6 0.7 collective-permute-start
  48.3 2.6 collective-permute-start.1
  51.0 2.6 collective-permute-done
  53.5 0.8 collective-permute-done.1
  54.3 2.8 collective-permute-done.2
  57.1 3.2 %collective-permute-start.6 = (bf16[4,192,256]{2,1,0:T(8,128)(2,1)S(1)}, bf16[4,192,256]{2,1,0:T(8,128)(2,1)S(1)}, u32[]{:S(2)}, u32[]{:S(2)}) collective-permute-start(bf16[4,192,256]{2,1,0:T(8,128)(2,1)S(1)} %pad_maximum_fusion.1.refs_3_), channel_id=1, source_target_pairs={{0,7},{1,0},{2,1},{3,2},{4,3},{5,4},{6,5},{7,6},{8,15},{9,8},{10,9... | collective-permute-start | bytes 1179656 | tf_op jit(solution)/shard_map/ppermute | solution.py:21
  60.3 9.9 %all-to-all-done.2.refs_1_ = bf16[8,192,256]{2,1,0:T(8,128)(2,1)S(1)} async-done(((bf16[8,192,256]{2,1,0:T(8,128)(2,1)}), bf16[8,192,256]{2,1,0:T(8,128)(2,1)S(1)}, u32[]{:S(2)}, u32[]{:S(2)}) %all-to-all-start.2) | async-done | bytes 786464 | tf_op jit(solution)/shard_map/all_to_all | solution.py:298
  70.2 2.1 collective-permute-start.13
  72.3 0.7 broadcast_in_dim_broadcast_in_dim_broadcast_in_dim.2
  73.0 5.7 %all-to-all-start.1 = ((f32[64,8,128]{2,1,0:T(8,128)}), f32[64,8,128]{2,1,0:T(8,128)S(1)}, u32[]{:S(2)}, u32[]{:S(2)}) async-start(f32[64,8,128]{2,1,0:T(8,128)} %broadcast_in_dim_broadcast_in_dim_broadcast_in_dim.2), calls=%async_computation.1 | async-start | bytes 524288 | tf_op jit(solution)/shard_map/all_to_all | solution.py:298
  78.8 2.9 %collective-permute-start.7 = (bf16[4,192,256]{2,1,0:T(8,128)(2,1)S(1)}, bf16[4,192,256]{2,1,0:T(8,128)(2,1)}, u32[]{:S(2)}, u32[]{:S(2)}) collective-permute-start(bf16[4,192,256]{2,1,0:T(8,128)(2,1)S(1)} %collective-permute-done.6.refs_4_), channel_id=1, source_target_pairs={{0,7},{1,0},{2,1},{3,2},{4,3},{5,4},{6,5},{7,6},{8,15},{9,8},{10,9... | collective-permute-start | bytes 1179656 | tf_op jit(solution)/shard_map/ppermute | solution.py:21
  81.7 0.8 copy-done.12
  82.4 13.0 %collective-permute-done.7.refs_5_ = bf16[4,192,256]{2,1,0:T(8,128)(2,1)} collective-permute-done((bf16[4,192,256]{2,1,0:T(8,128)(2,1)S(1)}, bf16[4,192,256]{2,1,0:T(8,128)(2,1)}, u32[]{:S(2)}, u32[]{:S(2)}) %collective-permute-start.7) | collective-permute-done | bytes 393248 | tf_op jit(solution)/shard_map/ppermute | solution.py:21
  95.4 1.6 collective-permute-start.8
  97.4 0.6 sqrt_reduce_fusion
  98.1 0.9 copy-done.4
  99.2 1.0 slice.113
  100.2 1.8 collective-permute-start.14
  102.0 1.0 slice.114
  103.0 1.8 collective-permute-start.15
  104.8 1.5 collective-permute-done.8.refs_6_
  106.3 3.0 %collective-permute-start.10 = (bf16[2,192,256]{2,1,0:T(8,128)(2,1)S(1)}, bf16[2,192,256]{2,1,0:T(8,128)(2,1)S(1)}, u32[]{:S(2)}, u32[]{:S(2)}) collective-permute-start(bf16[2,192,256]{2,1,0:T(8,128)(2,1)S(1)} %slice.111), channel_id=1, source_target_pairs={{0,7},{1,0},{2,1},{3,2},{4,3},{5,4},{6,5},{7,6},{8,15},{9,8},{10,9... | collective-permute-start | bytes 589832 | tf_op jit(solution)/shard_map/ppermute | solution.py:21
  109.3 0.9 slice.110
  110.4 2.2 collective-permute-done.10.refs_8_
  112.5 4.7 %collective-permute-done.9.refs_7_ = bf16[2,192,256]{2,1,0:T(8,128)(2,1)S(1)} collective-permute-done((bf16[2,192,256]{2,1,0:T(8,128)(2,1)S(1)}, bf16[2,192,256]{2,1,0:T(8,128)(2,1)S(1)}, u32[]{:S(2)}, u32[]{:S(2)}) %collective-permute-start.9) | collective-permute-done | bytes 196640 | tf_op jit(solution)/shard_map/ppermute | solution.py:21
  117.2 1.0 copy-done.13
  118.2 3.2 %stack.54.own_ref = bf16[8,4,192,256]{3,2,1,0:T(8,128)(2,1)} custom-call(bf16[4,192,256]{2,1,0:T(8,128)(2,1)} %collective-permute-done.5.refs_0_, bf16[4,192,256]{2,1,0:T(8,128)(2,1)} %collective-permute-done.4.refs_1_, bf16[4,192,256]{2,1,0:T(8,128)(2,1)} %collective-permute-done.3.refs_2_, bf16[4,192,256]{2,1,0:T(8,128)(2,1)S(1)} %pad_maximum_fusion.1.refs_3_, ...), custom_call_target="tpu_custom_call" | custom-call | bytes 6000000 | tf_op jit(solution)/shard_map/stack/pallas_call | solution.py:54
  121.4 1.8 stack.55.own_ref
  123.8 3.6 %collective-permute-done.11.other_ref = bf16[8,4,192,256]{3,2,1,0:T(8,128)(2,1)} collective-permute-done((bf16[8,4,192,256]{3,2,1,0:T(8,128)(2,1)}, bf16[8,4,192,256]{3,2,1,0:T(8,128)(2,1)}, u32[]{:S(2)}, u32[]{:S(2)}) %collective-permute-start.11) | collective-permute-done | bytes 3145760 | tf_op jit(solution)/shard_map/ppermute | solution.py:348
  127.4 7.3 %grad_act.1 = (f32[384,256]{1,0:T(8,128)S(1)}, f32[384,32]{1,0:T(8,128)S(1)}) custom-call(s32[4]{0:T(128)S(1)} %pad_add_fusion.pos_ref, bf16[8,4,192,256]{3,2,1,0:T(8,128)(2,1)} %stack.54.own_ref, bf16[8,4,192,256]{3,2,1,0:T(8,128)(2,1)} %collective-permute-done.11.other_ref, f32[32,1,256]{2,1,0:T(1,128)S(1)} %div.15.scale_ref, ...), custom_call_target="tpu_custom_call" | custom-call | flops 1000000000 | bytes 16000000 | tf_op jit(solution)/shard_map/grad_act/pallas_call | solution.py:170
  134.7 0.7 copy-done.14
  135.4 13.6 %gate_up.1 = (bf16[2,8192,256]{2,1,0:T(8,128)(2,1)}, f32[2,384,256]{2,1,0:T(8,128)S(1)}, f32[2,8,256]{2,1,0:T(8,128)S(1)}) custom-call(s32[4]{0:T(128)S(1)} %pad_add_fusion.pos_ref, bf16[4,8,192,256]{3,2,1,0:T(8,128)(2,1)} %stack.55.own_ref, bf16[4,8,192,256]{3,2,1,0:T(8,128)(2,1)} %collective-permute-done.16.other_ref, ...), custom_call_target="tpu_custom_call" | custom-call | flops 1000000000 | bytes 16000000 | tf_op jit(solution)/shard_map/gate_up/pallas_call | solution.py:245
  149.5 8.1 %grad_in.1 = (bf16[4,8,192,256]{3,2,1,0:T(8,128)(2,1)S(1)}, bf16[4,8,192,256]{3,2,1,0:T(8,128)(2,1)}) custom-call(s32[4]{0:T(128)S(1)} %pad_add_fusion.pos_ref, bf16[2,384,256]{2,1,0:T(8,128)(2,1)S(1)} %get-tuple-element.28.grads_ref, bf16[2,8192,256]{2,1,0:T(8,128)(2,1)} %get-tuple-element.21.tile_ref), custom_call_target="tpu_custom_call" | custom-call | flops 1000000000 | bytes 16000000 | tf_op jit(solution)/shard_map/grad_in/pallas_call | solution.py:284
  157.8 5.7 %collective-permute-done.17 = bf16[4,8,192,256]{3,2,1,0:T(8,128)(2,1)S(1)} collective-permute-done((bf16[4,8,192,256]{3,2,1,0:T(8,128)(2,1)}, bf16[4,8,192,256]{3,2,1,0:T(8,128)(2,1)S(1)}, u32[]{:S(2)}, u32[]{:S(2)}) %collective-permute-start.17) | collective-permute-done | bytes 3145760 | tf_op jit(solution)/shard_map/ppermute | solution.py:371
  163.5 2.9 %add_convert_fusion = bf16[4,8,192,256]{3,2,1,0:T(8,128)(2,1)} fusion(bf16[4,8,192,256]{3,2,1,0:T(8,128)(2,1)S(1)} %collective-permute-done.17, bf16[4,8,192,256]{3,2,1,0:T(8,128)(2,1)S(1)} %get-tuple-element.22), kind=kLoop, calls=%fused_computation | loop fusion | flops 6291456 | bytes 9437184 | tf_op jit(solution)/shard_map/convert_element_type | solution.py:372
  166.6 1.2 fusion.3
  167.8 1.1 fusion.4
  169.1 0.8 maximum_maximum_fusion.1
  169.9 1.7 copy.25
  171.7 1.7 reshape.112
  173.3 5.7 %dot_down.1 = f32[64,1,128]{2,1,0:T(1,128)S(1)} custom-call(s32[4]{0:T(128)S(1)} %pad_add_fusion.pos_ref, bf16[8,4,192,256]{3,2,1,0:T(8,128)(2,1)S(1)} %copy-done.1, bf16[8,4,192,256]{3,2,1,0:T(8,128)(2,1)} %collective-permute-done.11.other_ref, bf16[384,256]{1,0:T(8,128)(2,1)S(1)} %get-tuple-element.29.act_ref, bf16[256,8192]{1,0:T(8,128)(2,1)} %get-tuple-element.17.tile_ref), custom_call_target="tpu_custom_call" | custom-call | flops 1000000000 | bytes 16000000 | tf_op jit(solution)/shard_map/dot_down/pallas_call | solution.py:203
  179.1 0.8 maximum_maximum_fusion
  179.9 10.5 %all-to-all-start.3 = ((f32[64,8,128]{2,1,0:T(8,128)}), f32[64,8,128]{2,1,0:T(8,128)S(1)}, u32[]{:S(2)}, u32[]{:S(2)}) async-start(f32[64,8,128]{2,1,0:T(8,128)} %maximum_maximum_fusion), calls=%async_computation.5 | async-start | bytes 524288 | tf_op jit(solution)/shard_map/all_to_all | solution.py:298
  190.7 20.9 %reduce-scatter.3.cloned.1.call-done = bf16[1,8,192,256]{3,2,1,0:T(8,128)(2,1)} async-done(((bf16[4,8,192,256]{3,2,1,0:T(8,128)(2,1)}), bf16[1,8,192,256]{3,2,1,0:T(8,128)(2,1)}) %reduce-scatter.3.cloned.1.call-update) | async-done | bytes 786448 | tf_op jit(solution)/shard_map/reduce_scatter | solution.py:373
  211.6 2.5 bitcast_convert_fusion
  214.1 5.2 %proj_gate_up.1 = f32[384,64]{1,0:T(8,128)S(1)} custom-call(s32[4]{0:T(128)S(1)} %pad_add_fusion.pos_ref, bf16[4,8,192,256]{3,2,1,0:T(8,128)(2,1)} %stack.55.own_ref, bf16[4,8,192,256]{3,2,1,0:T(8,128)(2,1)} %collective-permute-done.16.other_ref, bf16[2,32,8192]{2,1,0:T(8,128)(2,1)S(1)} %bitcast.77), custom_call_target="tpu_custom_call" | custom-call | flops 1000000000 | bytes 16000000 | tf_op jit(solution)/shard_map/proj_gate_up/pallas_call | solution.py:139
  219.7 0.7 broadcast_in_dim.38
  220.4 8.9 %all-to-all-start.4 = ((f32[64,8,128]{2,1,0:T(8,128)}), f32[64,8,128]{2,1,0:T(8,128)S(1)}, u32[]{:S(2)}, u32[]{:S(2)}) async-start(f32[64,8,128]{2,1,0:T(8,128)} %broadcast_in_dim.38), calls=%async_computation.6 | async-start | bytes 524288 | tf_op jit(solution)/shard_map/all_to_all | solution.py:298
  229.8 14.4 %all-to-all-done.4 = f32[64,8,128]{2,1,0:T(8,128)S(1)} async-done(((f32[64,8,128]{2,1,0:T(8,128)}), f32[64,8,128]{2,1,0:T(8,128)S(1)}, u32[]{:S(2)}, u32[]{:S(2)}) %all-to-all-start.4) | async-done | bytes 262176 | tf_op jit(solution)/shard_map/all_to_all | solution.py:298
  244.8 12.1 %all_to_all.36 = f32[8,48,256]{2,1,0:T(8,128)S(1)} all-to-all(f32[8,48,256]{2,1,0:T(8,128)S(1)} %bitcast.87), channel_id=1, replica_groups=mesh['x'=4,'core'=2,'y'=4,'z'=8] {'x','core'}, dimensions={0} | all-to-all | bytes 786432 | tf_op jit(solution)/shard_map/all_to_all | solution.py:298
  256.9 0.8 broadcast_in_dim.40
  257.7 4.8 %all-to-all-start.6 = ((f32[8,48,256]{2,1,0:T(8,128)}), f32[8,48,256]{2,1,0:T(8,128)S(1)}, u32[]{:S(2)}, u32[]{:S(2)}) async-start(f32[8,48,256]{2,1,0:T(8,128)} %broadcast_in_dim.40), calls=%async_computation.8 | async-start | bytes 786432 | tf_op jit(solution)/shard_map/all_to_all | solution.py:298
  262.6 7.5 %all-to-all-done.6 = f32[8,48,256]{2,1,0:T(8,128)S(1)} async-done(((f32[8,48,256]{2,1,0:T(8,128)}), f32[8,48,256]{2,1,0:T(8,128)S(1)}, u32[]{:S(2)}, u32[]{:S(2)}) %all-to-all-start.6) | async-done | bytes 393248 | tf_op jit(solution)/shard_map/all_to_all | solution.py:298
  270.7 0.6 slice.127
  272.0 0.8 reshape.118
  272.8 0.6 copy.29
  274.0 1.6 convert_bitcast_fusion
  (119 shorter events, 6.8 us)
Async XLA Ops:
  7.2 116.6 %copy-start = (bf16[2,32,512]{2,1,0:T(8,128)(2,1)S(1)}, bf16[2,32,512]{2,1,0:T(8,128)(2,1)}, u32[]{:S(2)}) copy-start(bf16[2,32,512]{2,1,0:T(8,128)(2,1)} %param.14) | copy-start | bytes 196612
  7.2 128.2 %all-gather.2.cloned.1.call-start = ((), (), s32[]{:S(2)}) async-start(), calls=%async_computation.9 | async-start | bytes 18874368 | tf_op jit(solution)/shard_map/all_gather | solution.py:329
  8.0 1.0 copy-start.10
  9.0 0.8 copy-start.16
  9.8 33.3 %copy-start.19 = (bf16[192,256]{1,0:T(8,128)(2,1)S(1)}, bf16[192,256]{1,0:T(8,128)(2,1)}, u32[]{:S(2)}) copy-start(bf16[192,256]{1,0:T(8,128)(2,1)} %param.10) | copy-start | bytes 294916
  16.2 31.5 %copy-start.21 = (bf16[192,256]{1,0:T(8,128)(2,1)S(1)}, bf16[192,256]{1,0:T(8,128)(2,1)}, u32[]{:S(2)}) copy-start(bf16[192,256]{1,0:T(8,128)(2,1)} %param.11) | copy-start | bytes 294916
  43.1 29.2 %copy-start.24 = (f32[128]{0:T(128)S(1)}, f32[128]{0:T(128)}, u32[]{:S(2)}) copy-start(f32[128]{0:T(128)} %reduce_sum.49) | copy-start | bytes 1540
  44.1 26.1 %all-to-all-start.2 = ((bf16[8,192,256]{2,1,0:T(8,128)(2,1)}), bf16[8,192,256]{2,1,0:T(8,128)(2,1)S(1)}, u32[]{:S(2)}, u32[]{:S(2)}) async-start(bf16[8,192,256]{2,1,0:T(8,128)(2,1)} %after.2), calls=%async_computation.2 | async-start | bytes 1572864 | tf_op jit(solution)/shard_map/all_to_all | solution.py:298
  47.6 5.9 %collective-permute-start = (bf16[192,256]{1,0:T(8,128)(2,1)S(1)}, bf16[192,256]{1,0:T(8,128)(2,1)S(1)}, u32[]{:S(2)}, u32[]{:S(2)}) collective-permute-start(bf16[192,256]{1,0:T(8,128)(2,1)S(1)} %copy-done.21), channel_id=1, source_target_pairs={{0,8},{8,16},{16,24},{24,0},{1,9},{9,17},{17,25},{25,1},{2,10},{10... | collective-permute-start | bytes 294920 | tf_op jit(solution)/shard_map/ppermute | solution.py:21
  48.3 6.0 %collective-permute-start.1 = (bf16[192,256]{1,0:T(8,128)(2,1)S(1)}, bf16[192,256]{1,0:T(8,128)(2,1)S(1)}, u32[]{:S(2)}, u32[]{:S(2)}) collective-permute-start(bf16[192,256]{1,0:T(8,128)(2,1)S(1)} %copy-done.21), channel_id=1, source_target_pairs={{0,24},{8,0},{16,8},{24,16},{1,25},{9,1},{17,9},{25,17},{2,26},{10... | collective-permute-start | bytes 294920 | tf_op jit(solution)/shard_map/ppermute | solution.py:21
  51.0 6.1 %collective-permute-start.2 = (bf16[192,256]{1,0:T(8,128)(2,1)S(1)}, bf16[192,256]{1,0:T(8,128)(2,1)S(1)}, u32[]{:S(2)}, u32[]{:S(2)}) collective-permute-start(bf16[192,256]{1,0:T(8,128)(2,1)S(1)} %copy-done.21), channel_id=1, source_target_pairs={{0,16},{8,24},{16,0},{24,8},{1,17},{9,25},{17,1},{25,9},{2,18},{10... | collective-permute-start | bytes 294920 | tf_op jit(solution)/shard_map/ppermute | solution.py:21
  57.1 21.6 %collective-permute-start.6 = (bf16[4,192,256]{2,1,0:T(8,128)(2,1)S(1)}, bf16[4,192,256]{2,1,0:T(8,128)(2,1)S(1)}, u32[]{:S(2)}, u32[]{:S(2)}) collective-permute-start(bf16[4,192,256]{2,1,0:T(8,128)(2,1)S(1)} %pad_maximum_fusion.1.refs_3_), channel_id=1, source_target_pairs={{0,7},{1,0},{2,1},{3,2},{4,3},{5,4},{6,5},{7,6},{8,15},{9,8},{10,9... | collective-permute-start | bytes 1179656 | tf_op jit(solution)/shard_map/ppermute | solution.py:21
  60.3 22.1 %collective-permute-start.3 = (bf16[4,192,256]{2,1,0:T(8,128)(2,1)S(1)}, bf16[4,192,256]{2,1,0:T(8,128)(2,1)}, u32[]{:S(2)}, u32[]{:S(2)}) collective-permute-start(bf16[4,192,256]{2,1,0:T(8,128)(2,1)S(1)} %pad_maximum_fusion.1.refs_3_), channel_id=1, source_target_pairs={{0,1},{1,2},{2,3},{3,4},{4,5},{5,6},{6,7},{7,0},{8,9},{9,10},{10,1... | collective-permute-start | bytes 1179656 | tf_op jit(solution)/shard_map/ppermute | solution.py:21
  70.2 27.8 %collective-permute-start.13 = (bf16[8,192,256]{2,1,0:T(8,128)(2,1)S(1)}, bf16[8,192,256]{2,1,0:T(8,128)(2,1)S(1)}, u32[]{:S(2)}, u32[]{:S(2)}) collective-permute-start(bf16[8,192,256]{2,1,0:T(8,128)(2,1)S(1)} %all-to-all-done.2.refs_1_), channel_id=1, source_target_pairs={{0,24},{8,0},{16,8},{24,16},{1,25},{9,1},{17,9},{25,17},{2,26},{10... | collective-permute-start | bytes 2359304 | tf_op jit(solution)/shard_map/ppermute | solution.py:21
  72.3 25.8 %collective-permute-start.12 = (bf16[8,192,256]{2,1,0:T(8,128)(2,1)S(1)}, bf16[8,192,256]{2,1,0:T(8,128)(2,1)S(1)}, u32[]{:S(2)}, u32[]{:S(2)}) collective-permute-start(bf16[8,192,256]{2,1,0:T(8,128)(2,1)S(1)} %all-to-all-done.2.refs_1_), channel_id=1, source_target_pairs={{0,8},{8,16},{16,24},{24,0},{1,9},{9,17},{17,25},{25,1},{2,10},{10... | collective-permute-start | bytes 2359304 | tf_op jit(solution)/shard_map/ppermute | solution.py:21
  73.0 24.4 %all-to-all-start.1 = ((f32[64,8,128]{2,1,0:T(8,128)}), f32[64,8,128]{2,1,0:T(8,128)S(1)}, u32[]{:S(2)}, u32[]{:S(2)}) async-start(f32[64,8,128]{2,1,0:T(8,128)} %broadcast_in_dim_broadcast_in_dim_broadcast_in_dim.2), calls=%async_computation.1 | async-start | bytes 524288 | tf_op jit(solution)/shard_map/all_to_all | solution.py:298
  78.7 132.8 %reduce-scatter.3.cloned.1.call-start = ((), (), s32[]{:S(2)}) async-start(), calls=%async_computation.10 | async-start | bytes 3932160 | tf_op jit(solution)/shard_map/reduce_scatter | solution.py:373
  78.8 16.6 %collective-permute-start.7 = (bf16[4,192,256]{2,1,0:T(8,128)(2,1)S(1)}, bf16[4,192,256]{2,1,0:T(8,128)(2,1)}, u32[]{:S(2)}, u32[]{:S(2)}) collective-permute-start(bf16[4,192,256]{2,1,0:T(8,128)(2,1)S(1)} %collective-permute-done.6.refs_4_), channel_id=1, source_target_pairs={{0,7},{1,0},{2,1},{3,2},{4,3},{5,4},{6,5},{7,6},{8,15},{9,8},{10,9... | collective-permute-start | bytes 1179656 | tf_op jit(solution)/shard_map/ppermute | solution.py:21
  81.7 0.8 copy-start.12
  82.4 14.6 %collective-permute-start.4 = (bf16[4,192,256]{2,1,0:T(8,128)(2,1)}, bf16[4,192,256]{2,1,0:T(8,128)(2,1)}, u32[]{:S(2)}, u32[]{:S(2)}) collective-permute-start(bf16[4,192,256]{2,1,0:T(8,128)(2,1)} %collective-permute-done.3.refs_2_), channel_id=1, source_target_pairs={{0,1},{1,2},{2,3},{3,4},{4,5},{5,6},{6,7},{7,0},{8,9},{9,10},{10,1... | collective-permute-start | bytes 1179656 | tf_op jit(solution)/shard_map/ppermute | solution.py:21
  95.4 11.0 %collective-permute-start.8 = (bf16[4,192,256]{2,1,0:T(8,128)(2,1)}, bf16[4,192,256]{2,1,0:T(8,128)(2,1)S(1)}, u32[]{:S(2)}, u32[]{:S(2)}) collective-permute-start(bf16[4,192,256]{2,1,0:T(8,128)(2,1)} %collective-permute-done.7.refs_5_), channel_id=1, source_target_pairs={{0,7},{1,0},{2,1},{3,2},{4,3},{5,4},{6,5},{7,6},{8,15},{9,8},{10,9... | collective-permute-start | bytes 1179656 | tf_op jit(solution)/shard_map/ppermute | solution.py:21
  97.0 12.3 %collective-permute-start.5 = (bf16[4,192,256]{2,1,0:T(8,128)(2,1)}, bf16[4,192,256]{2,1,0:T(8,128)(2,1)}, u32[]{:S(2)}, u32[]{:S(2)}) collective-permute-start(bf16[4,192,256]{2,1,0:T(8,128)(2,1)} %collective-permute-done.4.refs_1_), channel_id=1, source_target_pairs={{0,1},{1,2},{2,3},{3,4},{4,5},{5,6},{6,7},{7,0},{8,9},{9,10},{10,1... | collective-permute-start | bytes 1179656 | tf_op jit(solution)/shard_map/ppermute | solution.py:21
  98.1 0.9 copy-start.4
  98.1 1.2 copy-start.6
  100.2 21.2 %collective-permute-start.14 = (bf16[4,192,256]{2,1,0:T(8,128)(2,1)S(1)}, bf16[4,192,256]{2,1,0:T(8,128)(2,1)S(1)}, u32[]{:S(2)}, u32[]{:S(2)}) collective-permute-start(bf16[4,192,256]{2,1,0:T(8,128)(2,1)S(1)} %slice.113), channel_id=1, source_target_pairs={{0,8},{8,16},{16,24},{24,0},{1,9},{9,17},{17,25},{25,1},{2,10},{10... | collective-permute-start | bytes 1179656 | tf_op jit(solution)/shard_map/ppermute | solution.py:21
  103.0 18.4 %collective-permute-start.15 = (bf16[4,192,256]{2,1,0:T(8,128)(2,1)S(1)}, bf16[4,192,256]{2,1,0:T(8,128)(2,1)S(1)}, u32[]{:S(2)}, u32[]{:S(2)}) collective-permute-start(bf16[4,192,256]{2,1,0:T(8,128)(2,1)S(1)} %slice.114), channel_id=1, source_target_pairs={{0,24},{8,0},{16,8},{24,16},{1,25},{9,1},{17,9},{25,17},{2,26},{10... | collective-permute-start | bytes 1179656 | tf_op jit(solution)/shard_map/ppermute | solution.py:21
  106.3 6.2 %collective-permute-start.10 = (bf16[2,192,256]{2,1,0:T(8,128)(2,1)S(1)}, bf16[2,192,256]{2,1,0:T(8,128)(2,1)S(1)}, u32[]{:S(2)}, u32[]{:S(2)}) collective-permute-start(bf16[2,192,256]{2,1,0:T(8,128)(2,1)S(1)} %slice.111), channel_id=1, source_target_pairs={{0,7},{1,0},{2,1},{3,2},{4,3},{5,4},{6,5},{7,6},{8,15},{9,8},{10,9... | collective-permute-start | bytes 589832 | tf_op jit(solution)/shard_map/ppermute | solution.py:21
  110.2 11.2 %copy-start.5 = (bf16[8,192,256]{2,1,0:T(8,128)(2,1)S(1)}, bf16[8,192,256]{2,1,0:T(8,128)(2,1)}, u32[]{:S(2)}) copy-start(bf16[8,192,256]{2,1,0:T(8,128)(2,1)} %copy-done.4) | copy-start | bytes 2359300
  110.3 11.2 %copy-start.7 = (bf16[8,192,256]{2,1,0:T(8,128)(2,1)S(1)}, bf16[8,192,256]{2,1,0:T(8,128)(2,1)}, u32[]{:S(2)}) copy-start(bf16[8,192,256]{2,1,0:T(8,128)(2,1)} %after.3.refs_0_) | copy-start | bytes 2359300
  110.3 7.0 %collective-permute-start.9 = (bf16[2,192,256]{2,1,0:T(8,128)(2,1)S(1)}, bf16[2,192,256]{2,1,0:T(8,128)(2,1)S(1)}, u32[]{:S(2)}, u32[]{:S(2)}) collective-permute-start(bf16[2,192,256]{2,1,0:T(8,128)(2,1)S(1)} %slice.110), channel_id=1, source_target_pairs={{0,1},{1,2},{2,3},{3,4},{4,5},{5,6},{6,7},{7,0},{8,9},{9,10},{10,1... | collective-permute-start | bytes 589832 | tf_op jit(solution)/shard_map/ppermute | solution.py:21
  117.2 1.0 copy-start.13
  121.4 2.4 copy-start.23
  121.4 6.0 %copy-start.11 = (bf16[32,8192]{1,0:T(8,128)(2,1)S(1)}, bf16[32,8192]{1,0:T(8,128)(2,1)}, u32[]{:S(2)}) copy-start(bf16[32,8192]{1,0:T(8,128)(2,1)} %right_ref.3) | copy-start | bytes 1572868
  121.4 6.0 %collective-permute-start.11 = (bf16[8,4,192,256]{3,2,1,0:T(8,128)(2,1)}, bf16[8,4,192,256]{3,2,1,0:T(8,128)(2,1)}, u32[]{:S(2)}, u32[]{:S(2)}) collective-permute-start(bf16[8,4,192,256]{3,2,1,0:T(8,128)(2,1)} %stack.54.own_ref), channel_id=1, source_target_pairs={{0,32},{32,0},{1,33},{33,1},{2,34},{34,2},{3,35},{35,3},{4,36},{36... | collective-permute-start | bytes 9437192 | tf_op jit(solution)/shard_map/ppermute | solution.py:348
  123.3 12.1 %collective-permute-start.16 = (bf16[4,8,192,256]{3,2,1,0:T(8,128)(2,1)}, bf16[4,8,192,256]{3,2,1,0:T(8,128)(2,1)}, u32[]{:S(2)}, u32[]{:S(2)}) collective-permute-start(bf16[4,8,192,256]{3,2,1,0:T(8,128)(2,1)} %stack.55.own_ref), channel_id=1, source_target_pairs={{0,32},{32,0},{1,33},{33,1},{2,34},{34,2},{3,35},{35,3},{4,36},{36... | collective-permute-start | bytes 9437192 | tf_op jit(solution)/shard_map/ppermute | solution.py:347
  127.4 8.0 %copy-start.8 = (bf16[2,8192,32]{1,2,0:T(8,128)(2,1)S(1)}, bf16[2,8192,32]{1,2,0:T(8,128)(2,1)}, u32[]{:S(2)}) copy-start(bf16[2,8192,32]{1,2,0:T(8,128)(2,1)} %param.13) | copy-start | bytes 3145732
  134.7 0.7 copy-start.14
  135.4 13.6 %copy-start.25 = (f32[2,512]{1,0:T(2,128)S(1)}, f32[2,512]{1,0:T(2,128)}, u32[]{:S(2)}) copy-start(f32[2,512]{1,0:T(2,128)} %param.15) | copy-start | bytes 12292
  149.5 8.1 %copy-start.2 = (bf16[2,384,256]{2,1,0:T(8,128)(2,1)}, bf16[2,384,256]{2,1,0:T(8,128)(2,1)S(1)}, u32[]{:S(2)}) copy-start(bf16[2,384,256]{2,1,0:T(8,128)(2,1)S(1)} %get-tuple-element.28.grads_ref) | copy-start | bytes 1179652
  157.6 5.9 %collective-permute-start.17 = (bf16[4,8,192,256]{3,2,1,0:T(8,128)(2,1)}, bf16[4,8,192,256]{3,2,1,0:T(8,128)(2,1)S(1)}, u32[]{:S(2)}, u32[]{:S(2)}) collective-permute-start(bf16[4,8,192,256]{3,2,1,0:T(8,128)(2,1)} %get-tuple-element.23), channel_id=1, source_target_pairs={{0,32},{32,0},{1,33},{33,1},{2,34},{34,2},{3,35},{35,3},{4,36},{36... | collective-permute-start | bytes 9437192 | tf_op jit(solution)/shard_map/ppermute | solution.py:371
  166.4 2.5 copy-start.17
  166.4 6.9 %copy-start.1 = (bf16[8,4,192,256]{3,2,1,0:T(8,128)(2,1)S(1)}, bf16[8,4,192,256]{3,2,1,0:T(8,128)(2,1)}, u32[]{:S(2)}) copy-start(bf16[8,4,192,256]{3,2,1,0:T(8,128)(2,1)} %stack.54.own_ref) | copy-start | bytes 9437188
  173.3 5.7 %copy-start.18 = (f32[2,32,6,128]{3,2,1,0:T(8,128)S(1)}, f32[2,32,6,128]{3,2,1,0:T(8,128)}, u32[]{:S(2)}) copy-start(f32[2,32,6,128]{3,2,1,0:T(8,128)} %reshape.112) | copy-start | bytes 589828
  179.1 35.0 %copy-start.9 = (bf16[2,8192,32]{1,2,0:T(8,128)(2,1)S(1)}, bf16[2,8192,32]{1,2,0:T(8,128)(2,1)}, u32[]{:S(2)}) copy-start(bf16[2,8192,32]{1,2,0:T(8,128)(2,1)} %param.13) | copy-start | bytes 3145732
  179.9 39.7 %all-to-all-start.3 = ((f32[64,8,128]{2,1,0:T(8,128)}), f32[64,8,128]{2,1,0:T(8,128)S(1)}, u32[]{:S(2)}, u32[]{:S(2)}) async-start(f32[64,8,128]{2,1,0:T(8,128)} %maximum_maximum_fusion), calls=%async_computation.5 | async-start | bytes 524288 | tf_op jit(solution)/shard_map/all_to_all | solution.py:298
  190.4 83.6 %reduce-scatter.5.cloned.1.call-start = ((), (), s32[]{:S(2)}) async-start(), calls=%async_computation.11 | async-start | bytes 1769472 | tf_op jit(solution)/shard_map/reduce_scatter | solution.py:373
  214.1 5.3 %copy-start.3 = (bf16[2,384,256]{2,1,0:T(8,128)(2,1)S(1)}, bf16[2,384,256]{2,1,0:T(8,128)(2,1)}, u32[]{:S(2)}) copy-start(bf16[2,384,256]{2,1,0:T(8,128)(2,1)} %copy-done.2) | copy-start | bytes 1179652
  214.1 15.5 %copy-start.15 = (f32[384,32]{1,0:T(8,128)S(1)}, f32[384,32]{1,0:T(8,128)}, u32[]{:S(2)}) copy-start(f32[384,32]{1,0:T(8,128)} %copy-done.14) | copy-start | bytes 147460
  214.1 30.2 %copy-start.20 = (bf16[192,256]{1,0:T(8,128)(2,1)S(1)}, bf16[192,256]{1,0:T(8,128)(2,1)}, u32[]{:S(2)}) copy-start(bf16[192,256]{1,0:T(8,128)(2,1)} %param.10) | copy-start | bytes 294916
  219.3 25.2 %copy-start.22 = (bf16[192,256]{1,0:T(8,128)(2,1)S(1)}, bf16[192,256]{1,0:T(8,128)(2,1)}, u32[]{:S(2)}) copy-start(bf16[192,256]{1,0:T(8,128)(2,1)} %param.11) | copy-start | bytes 294916
  220.4 23.8 %all-to-all-start.4 = ((f32[64,8,128]{2,1,0:T(8,128)}), f32[64,8,128]{2,1,0:T(8,128)S(1)}, u32[]{:S(2)}, u32[]{:S(2)}) async-start(f32[64,8,128]{2,1,0:T(8,128)} %broadcast_in_dim.38), calls=%async_computation.6 | async-start | bytes 524288 | tf_op jit(solution)/shard_map/all_to_all | solution.py:298
  257.7 12.3 %all-to-all-start.6 = ((f32[8,48,256]{2,1,0:T(8,128)}), f32[8,48,256]{2,1,0:T(8,128)S(1)}, u32[]{:S(2)}, u32[]{:S(2)}) async-start(f32[8,48,256]{2,1,0:T(8,128)} %broadcast_in_dim.40), calls=%async_computation.8 | async-start | bytes 786432 | tf_op jit(solution)/shard_map/all_to_all | solution.py:298
Sparse Core Ops, SparseCore 0:
  9.9 90.0 all-gather.1
  166.5 44.9 reduce-scatter.2
  214.2 44.0 reduce-scatter.4

commit v3 on v2

--- a/solution.py
+++ b/solution.py
@@ -327,21 +327,22 @@
         return lax.dynamic_slice_in_dim(array, core * hidden, hidden, axis)
 
     frozen_full = lax.all_gather(frozen_gu, DP, axis=1, tiled=True)
-    tile_down, down_squares = merge_down(pos, frozen_down, left_down.T, right_down)
-    down_sum = jnp.sum(sum_parts(down_squares, CMP), axis=0, keepdims=True)
     g_y = jnp.stack(
         [step(out_grad, "y", NY, 1), out_grad, step(out_grad, "y", NY, -1), step(out_grad, "y", NY, 2)]
     )
-    copies = after(jnp.broadcast_to(inputs[None], (NZ, tokens, width)), down_sum)
-    x_z = exchange(copies, "z")
+    x_z = gather_small(inputs, "z", NZ)
+    tile_down, down_squares = merge_down(pos, frozen_down, left_down.T, right_down)
+    x_z = after(x_z, down_squares)
     yr, yl = both_ways(x_z, x_z, "y", NY)
+    down_sum = jnp.sum(sum_parts(after(down_squares, x_z), CMP), axis=0, keepdims=True)
+    yr = after(yr, yl, down_sum)
+    yfr, yfl = both_ways(yr[: NZ // 2], yl[NZ // 2 :], "y", NY)
     down_sums = gather_small(jnp.broadcast_to(down_sum, (8, 128)), CMP, NC * NMP)[:, :1]
-    yr = after(yr, yl, down_sums)
-    yfr, yfl = both_ways(yr[: NZ // 2], yl[NZ // 2 :], "y", NY)
     x_own = stack([yr, x_z, yl], yfr, yfl)
     r1, l1 = both_ways(g_y, g_y, "z", NZ)
     r2, l2 = both_ways(r1, l1, "z", NZ)
     r3, l3 = both_ways(r2, l2, "z", NZ)
+    r3 = after(r3, l3, down_sums)
     zfr, zfl = both_ways(r3[: NY // 2], l3[NY // 2 :], "z", NZ)
     g_own = stack([r3, r2, r1, g_y, l1, l2, l3], zfr, zfl)
     x_other = lax.ppermute(x_own, "core", OTHER)
@@ -369,8 +370,6 @@
 
     own_terms, other_terms = grad_in_parts(pos, pre_grads, tiles)
     from_other = lax.ppermute(other_terms, "core", OTHER)
-    terms = (own_terms.astype(F32) + from_other.astype(F32)).astype(BF16)
-    grad_in = lax.psum_scatter(lax.psum_scatter(terms, "y").astype(F32), "z")
 
     rows_gu = [
         lax.dot_general(pre_grads[k], right[k], NT, preferred_element_type=F32) for k in range(2)
@@ -379,10 +378,18 @@
     rows = jnp.concatenate(rows_gu + [proj_down, jnp.zeros_like(proj_down)], axis=1)
     rows = rows.reshape(NC, NMP, tokens // NMP, 128)
     rows = jnp.where(ic == 0, rows, rows[::-1]).reshape(NC * NMP, tokens // NMP, 128)
-    dots = dot_down_sums(pos, g_own, g_other, act, tile_down)
-    rows = jnp.concatenate([rows, dots, jnp.zeros_like(dots)], axis=1)
-    rows = gather_small(sum_parts(rows, CMP), CMP, NC * NMP)
-    dots = lax.dynamic_slice_in_dim(rows[:, 6], 2 * (iy * NZ + iz), 2, 0).reshape(1, width)
+    rows = jnp.pad(rows, ((0, 0), (0, 2), (0, 0)))
+    from_other = after(from_other, rows)
+    terms = (own_terms.astype(F32) + from_other.astype(F32)).astype(BF16)
+    over_y = lax.psum_scatter(terms, "y")
+    rows = sum_parts(after(rows, terms), CMP)
+    dots = dot_down_sums(pos, g_own, g_other, act, tile_down).reshape(NMP, NC, 1, 128)
+    dots = dots.swapaxes(0, 1).reshape(NC * NMP, 1, 128)
+    rows = jnp.broadcast_to(rows[None, :6], (NC * NMP, 6, 128))
+    rows = exchange(jnp.concatenate([rows, dots, jnp.zeros_like(dots)], axis=1), CMP)
+    grad_in = lax.psum_scatter(after(over_y, rows).astype(F32), "z")
+    dots = jnp.sum(rows[:, 6:7], axis=0)
+    dots = jnp.concatenate([jnp.where(ic == c, dots, 0.0) for c in range(NC)], axis=1)
     rows = lax.dynamic_slice_in_dim(rows[:, :6], ic * NMP, NMP, 0).reshape(tokens, 128).astype(BF16)
     own = iy * NZ + iz
     own_scale = lax.dynamic_index_in_dim(scale_down, own, 0, keepdims=False)
@@ -401,7 +408,7 @@
     )
     cores = [jnp.where(ic == c, mine, 0.0) for c in range(NC)]
     sums = jnp.concatenate(
-        [2.0 * left_gu_part, 2.0 * right_down_part, jnp.pad(0.5 * dots, ((0, 31), (0, 0)))] + cores
+        [2.0 * left_gu_part, 2.0 * right_down_part, jnp.pad(dots, ((0, 31), (0, 0)))] + cores
     )
     sums = gather_small(sum_parts(sums.reshape(NDP, 48, width), DP), DP, NDP).reshape(384, width)
     cores = sums[128:].reshape(NC, 128, hidden).swapaxes(0, 1).reshape(128, NC * hidden)

time: 285 us -> 267 us (0.937)
  blocking collectives: 38.5 us -> 12.1 us
  starting transfers between devices: 54.5 us -> 68.2 us
  waiting for transfers between devices: 90.1 us -> 81.9 us
  other arithmetic: 11.2 us -> 14.8 us
    all_to_all x2 -> x1, blocking collectives: 38.5 us -> 12.1 us  [exchange(): return lax.all_to_all(parts, axes, 0, 0, tiled=True)]
    reduce_scatter x2, waiting for transfers between devices: 20.9 us -> 4.95 us  [the longest x1 3.64 us: shards(): grad_in = lax.psum_scatter(after(over_y, rows).astype(F32), 'z')]
    all_to_all x5 -> x6, starting transfers between devices: 33.5 us -> 44.7 us  [exchange(): return lax.all_to_all(parts, axes, 0, 0, tiled=True)]
    ppermute x15, waiting for transfers between devices: 27.4 us -> 35.6 us  [step(): return lax.ppermute(array, axis, [(i, (i + shift) % n) for i in range(n)])]
    unnamed x54 -> x71, local copies, waits for them, and re-layouts: 5.48 us -> 7.89 us
    all_to_all x5 -> x6, waiting for transfers between devices: 31.8 us -> 32.8 us  [exchange(): return lax.all_to_all(parts, axes, 0, 0, tiled=True)]
  transfers between devices with their start and end apart: 26 -> 27, of which waited for: 13 -> 14; matrix products, arithmetic and copies ran while one was open for 8% -> 8% of each run, Pallas kernels for 10% -> 11%
where the time goes in v3:
time: 267 us; the launch traced here: 265 us
  waiting for transfers between devices  81.9 us (31%)
  starting transfers between devices  68.2 us (26%)
  Pallas kernels  51.4 us (19%)
  local copies, waits for them, and re-layouts  21 us (8%)
  other arithmetic  14.8 us (6%)
  between operations  14.3 us (5%)
  blocking collectives  12.1 us (5%)
    all_to_all x6, starting transfers between devices, exchange(): return lax.all_to_all(parts, axes, 0, 0, tiled=True)  44.7 us
    ppermute x15, waiting for transfers between devices, step(): return lax.ppermute(array, axis, [(i, (i + shift) % n) for i in range(n)])  35.6 us
    all_to_all x6, waiting for transfers between devices, exchange(): return lax.all_to_all(parts, axes, 0, 0, tiled=True)  32.8 us
    ppermute x15, starting transfers between devices, step(): return lax.ppermute(array, axis, [(i, (i + shift) % n) for i in range(n)])  22.7 us
    pallas_call x1, Pallas kernels, gate_up(): call(gate_up_body, 'gate_up', (NY,), [x_spec(t, w), x_spec(t, w), pl.Bloc...  13.5 us
    all_to_all x1, blocking collectives, exchange(): return lax.all_to_all(parts, axes, 0, 0, tiled=True)  12.1 us
    pallas_call x1, Pallas kernels, grad_in_parts(): call(grad_in_body, 'grad_in', (NY,), [pl.BlockSpec((2, t, f), lambda i, p...  8.13 us
    unnamed x71, local copies, waits for them, and re-layouts  7.89 us
  transfers between devices with their start and end apart: 27, of which 14 were waited for; matrix products, arithmetic and copies ran while one was open for 8% of the time, Pallas kernels for 11%

profile of v3, /device:TPU:2, one launch (start us, length us, event | category | flops | bytes accessed | tf_op | source)
XLA Modules:
  0.0 265.3 jit_solution(6939082212204952092)
XLA Ops:
  7.3 0.7 all-gather.2.cloned.1.call-update
  7.9 1.8 broadcast_in_dim.39
  9.8 8.5 %all-to-all-start = ((bf16[8,192,256]{2,1,0:T(8,128)(2,1)}), bf16[8,192,256]{2,1,0:T(8,128)(2,1)S(1)}, u32[]{:S(2)}, u32[]{:S(2)}) async-start(bf16[8,192,256]{2,1,0:T(8,128)(2,1)} %broadcast_in_dim.39), calls=%async_computation | async-start | bytes 1572864 | tf_op jit(solution)/shard_map/all_to_all | solution.py:298
  18.3 1.7 collective-permute-start
  19.9 1.7 collective-permute-start.1
  21.6 2.0 collective-permute-start.2
  24.2 1.1 collective-permute-done.1
  25.3 2.4 collective-permute-done.2
  27.8 3.2 %collective-permute-start.6 = (bf16[4,192,256]{2,1,0:T(8,128)(2,1)S(1)}, bf16[4,192,256]{2,1,0:T(8,128)(2,1)S(1)}, u32[]{:S(2)}, u32[]{:S(2)}) collective-permute-start(bf16[4,192,256]{2,1,0:T(8,128)(2,1)S(1)} %pad_maximum_fusion.1.refs_3_), channel_id=1, source_target_pairs={{0,7},{1,0},{2,1},{3,2},{4,3},{5,4},{6,5},{7,6},{8,15},{9,8},{10,9... | collective-permute-start | bytes 1179656 | tf_op jit(solution)/shard_map/ppermute | solution.py:21
  31.1 6.4 %merge_down.1 = (bf16[256,8192]{1,0:T(8,128)(2,1)}, f32[64,8,128]{2,1,0:T(8,128)S(1)}) custom-call(s32[4]{0:T(128)S(1)} %pad_add_fusion.pos_ref, bf16[512,8192]{1,0:T(8,128)(2,1)} %frozen_ref.1, bf16[32,512]{1,0:T(8,128)(2,1)S(1)} %bitcast.84, bf16[32,8192]{1,0:T(8,128)(2,1)S(1)} %copy-done.19), custom_call_target="tpu_custom_call" | custom-call | flops 1000000000 | bytes 16000000 | tf_op jit(solution)/shard_map/merge_down/pallas_call | solution.py:95
  37.4 0.7 copy-done.18
  38.1 3.2 %all-to-all-done.refs_0_ = bf16[8,192,256]{2,1,0:T(8,128)(2,1)S(1)} async-done(((bf16[8,192,256]{2,1,0:T(8,128)(2,1)}), bf16[8,192,256]{2,1,0:T(8,128)(2,1)S(1)}, u32[]{:S(2)}, u32[]{:S(2)}) %all-to-all-start) | async-done | bytes 786464 | tf_op jit(solution)/shard_map/all_to_all | solution.py:298
  41.4 0.9 copy-done.2
  42.3 7.1 %all-to-all-start.1 = ((f32[64,8,128]{2,1,0:T(8,128)}), f32[64,8,128]{2,1,0:T(8,128)}, u32[]{:S(2)}, u32[]{:S(2)}) async-start(f32[64,8,128]{2,1,0:T(8,128)} %after.8), calls=%async_computation.1 | async-start | bytes 524288 | tf_op jit(solution)/shard_map/all_to_all | solution.py:298
  49.4 1.6 collective-permute-start.3
  51.0 1.7 collective-permute-start.7
  52.7 2.8 %collective-permute-start.13 = (bf16[8,192,256]{2,1,0:T(8,128)(2,1)}, bf16[8,192,256]{2,1,0:T(8,128)(2,1)S(1)}, u32[]{:S(2)}, u32[]{:S(2)}) collective-permute-start(bf16[8,192,256]{2,1,0:T(8,128)(2,1)} %after.7.refs_1_), channel_id=1, source_target_pairs={{0,24},{8,0},{16,8},{24,16},{1,25},{9,1},{17,9},{25,17},{2,26},{10... | collective-permute-start | bytes 2359304 | tf_op jit(solution)/shard_map/ppermute | solution.py:21
  55.5 11.4 %collective-permute-done.3.refs_2_ = bf16[4,192,256]{2,1,0:T(8,128)(2,1)S(1)} collective-permute-done((bf16[4,192,256]{2,1,0:T(8,128)(2,1)S(1)}, bf16[4,192,256]{2,1,0:T(8,128)(2,1)S(1)}, u32[]{:S(2)}, u32[]{:S(2)}) %collective-permute-start.3) | collective-permute-done | bytes 393248 | tf_op jit(solution)/shard_map/ppermute | solution.py:21
  66.9 1.2 reduce_sum.58
  68.1 0.7 broadcast_in_dim_broadcast_in_dim_broadcast_in_dim.2
  68.8 9.6 %all-to-all-start.2 = ((f32[64,8,128]{2,1,0:T(8,128)}), f32[64,8,128]{2,1,0:T(8,128)}, u32[]{:S(2)}, u32[]{:S(2)}) async-start(f32[64,8,128]{2,1,0:T(8,128)} %broadcast_in_dim_broadcast_in_dim_broadcast_in_dim.2), calls=%async_computation.2 | async-start | bytes 524288 | tf_op jit(solution)/shard_map/all_to_all | solution.py:298
  78.5 2.8 %collective-permute-start.8 = (bf16[4,192,256]{2,1,0:T(8,128)(2,1)}, bf16[4,192,256]{2,1,0:T(8,128)(2,1)S(1)}, u32[]{:S(2)}, u32[]{:S(2)}) collective-permute-start(bf16[4,192,256]{2,1,0:T(8,128)(2,1)} %collective-permute-done.7.refs_5_), channel_id=1, source_target_pairs={{0,7},{1,0},{2,1},{3,2},{4,3},{5,4},{6,5},{7,6},{8,15},{9,8},{10,9... | collective-permute-start | bytes 1179656 | tf_op jit(solution)/shard_map/ppermute | solution.py:21
  81.3 13.4 %collective-permute-done.8.refs_1_.refs_6_ = bf16[4,192,256]{2,1,0:T(8,128)(2,1)S(1)} collective-permute-done((bf16[4,192,256]{2,1,0:T(8,128)(2,1)}, bf16[4,192,256]{2,1,0:T(8,128)(2,1)S(1)}, u32[]{:S(2)}, u32[]{:S(2)}) %collective-permute-start.8) | collective-permute-done | bytes 393248 | tf_op jit(solution)/shard_map/ppermute | solution.py:21
  94.7 0.7 slice.116
  95.5 1.6 collective-permute-start.10
  97.1 0.8 copy-done.6
  98.2 1.9 slice.117
  100.1 1.7 collective-permute-start.14
  101.8 1.8 slice.118
  103.5 1.5 collective-permute-start.15
  105.1 1.6 sqrt_reduce_fusion
  106.7 0.7 copy-done.16
  107.4 0.9 slice.115
  108.9 6.7 %collective-permute-done.9.refs_7_ = bf16[2,192,256]{2,1,0:T(8,128)(2,1)S(1)} collective-permute-done((bf16[2,192,256]{2,1,0:T(8,128)(2,1)S(1)}, bf16[2,192,256]{2,1,0:T(8,128)(2,1)S(1)}, u32[]{:S(2)}, u32[]{:S(2)}) %collective-permute-start.9) | collective-permute-done | bytes 196640 | tf_op jit(solution)/shard_map/ppermute | solution.py:21
  115.6 1.0 copy-done.15
  116.6 1.0 copy-done.17
  117.6 3.0 %stack.54.own_ref = bf16[8,4,192,256]{3,2,1,0:T(8,128)(2,1)} custom-call(bf16[4,192,256]{2,1,0:T(8,128)(2,1)S(1)} %copy-done.17, bf16[4,192,256]{2,1,0:T(8,128)(2,1)} %collective-permute-done.4.refs_1_, bf16[4,192,256]{2,1,0:T(8,128)(2,1)S(1)} %copy-done.23, bf16[4,192,256]{2,1,0:T(8,128)(2,1)S(1)} %pad_maximum_fusion.1.refs_3_, ...), custom_call_target="tpu_custom_call" | custom-call | bytes 6000000 | tf_op jit(solution)/shard_map/stack/pallas_call | solution.py:54
  120.6 1.8 stack.55.own_ref
  123.0 3.6 %collective-permute-done.11.other_ref = bf16[8,4,192,256]{3,2,1,0:T(8,128)(2,1)} collective-permute-done((bf16[8,4,192,256]{3,2,1,0:T(8,128)(2,1)}, bf16[8,4,192,256]{3,2,1,0:T(8,128)(2,1)}, u32[]{:S(2)}, u32[]{:S(2)}) %collective-permute-start.11) | collective-permute-done | bytes 3145760 | tf_op jit(solution)/shard_map/ppermute | solution.py:349
  126.6 7.2 %grad_act.1 = (f32[384,256]{1,0:T(8,128)S(1)}, f32[384,32]{1,0:T(8,128)S(1)}) custom-call(s32[4]{0:T(128)S(1)} %pad_add_fusion.pos_ref, bf16[8,4,192,256]{3,2,1,0:T(8,128)(2,1)} %stack.54.own_ref, bf16[8,4,192,256]{3,2,1,0:T(8,128)(2,1)} %collective-permute-done.11.other_ref, f32[32,1,256]{2,1,0:T(1,128)S(1)} %div.15.scale_ref, ...), custom_call_target="tpu_custom_call" | custom-call | flops 1000000000 | bytes 16000000 | tf_op jit(solution)/shard_map/grad_act/pallas_call | solution.py:170
  133.8 0.7 copy-done.24
  134.5 13.5 %gate_up.1 = (bf16[2,8192,256]{2,1,0:T(8,128)(2,1)}, f32[2,384,256]{2,1,0:T(8,128)S(1)}, f32[2,8,256]{2,1,0:T(8,128)S(1)}) custom-call(s32[4]{0:T(128)S(1)} %pad_add_fusion.pos_ref, bf16[4,8,192,256]{3,2,1,0:T(8,128)(2,1)} %stack.55.own_ref, bf16[4,8,192,256]{3,2,1,0:T(8,128)(2,1)} %collective-permute-done.16.other_ref, ...), custom_call_target="tpu_custom_call" | custom-call | flops 1000000000 | bytes 16000000 | tf_op jit(solution)/shard_map/gate_up/pallas_call | solution.py:245
  148.5 8.1 %grad_in.1 = (bf16[4,8,192,256]{3,2,1,0:T(8,128)(2,1)S(1)}, bf16[4,8,192,256]{3,2,1,0:T(8,128)(2,1)}) custom-call(s32[4]{0:T(128)S(1)} %pad_add_fusion.pos_ref, bf16[2,384,256]{2,1,0:T(8,128)(2,1)S(1)} %get-tuple-element.28.grads_ref, bf16[2,8192,256]{2,1,0:T(8,128)(2,1)} %get-tuple-element.21.tile_ref), custom_call_target="tpu_custom_call" | custom-call | flops 1000000000 | bytes 16000000 | tf_op jit(solution)/shard_map/grad_in/pallas_call | solution.py:284
  156.7 1.6 copy-done.12
  159.4 0.7 pad.12.refs_1_.refs_0_
  160.1 4.2 %collective-permute-done.17.refs_0_ = bf16[4,8,192,256]{3,2,1,0:T(8,128)(2,1)} collective-permute-done((bf16[4,8,192,256]{3,2,1,0:T(8,128)(2,1)}, bf16[4,8,192,256]{3,2,1,0:T(8,128)(2,1)}, u32[]{:S(2)}, u32[]{:S(2)}) %collective-permute-start.17) | collective-permute-done | bytes 3145760 | tf_op jit(solution)/shard_map/ppermute | solution.py:372
  164.3 4.6 %add_convert_fusion.refs_1_ = bf16[4,8,192,256]{3,2,1,0:T(8,128)(2,1)} fusion(bf16[4,8,192,256]{3,2,1,0:T(8,128)(2,1)} %after.11, bf16[4,8,192,256]{3,2,1,0:T(8,128)(2,1)S(1)} %copy-done.13), kind=kLoop, calls=%fused_computation | loop fusion | flops 6291456 | bytes 9437184 | tf_op jit(solution)/shard_map/convert_element_type | solution.py:383
  168.9 10.0 %all-to-all-start.3 = ((f32[64,8,128]{2,1,0:T(8,128)}), f32[64,8,128]{2,1,0:T(8,128)}, u32[]{:S(2)}, u32[]{:S(2)}) async-start(f32[64,8,128]{2,1,0:T(8,128)} %after.12), calls=%async_computation.4 | async-start | bytes 524288 | tf_op jit(solution)/shard_map/all_to_all | solution.py:298
  179.0 6.1 %dot_down.1 = f32[64,1,128]{2,1,0:T(1,128)S(1)} custom-call(s32[4]{0:T(128)S(1)} %pad_add_fusion.pos_ref, bf16[8,4,192,256]{3,2,1,0:T(8,128)(2,1)S(1)} %copy-done.1, bf16[8,4,192,256]{3,2,1,0:T(8,128)(2,1)} %collective-permute-done.11.other_ref, bf16[384,256]{1,0:T(8,128)(2,1)S(1)} %get-tuple-element.29.act_ref, bf16[256,8192]{1,0:T(8,128)(2,1)} %get-tuple-element.17.tile_ref), custom_call_target="tpu_custom_call" | custom-call | flops 1000000000 | bytes 16000000 | tf_op jit(solution)/shard_map/dot_down/pallas_call | solution.py:203
  185.1 7.8 %all-to-all-done.3 = f32[64,8,128]{2,1,0:T(8,128)} async-done(((f32[64,8,128]{2,1,0:T(8,128)}), f32[64,8,128]{2,1,0:T(8,128)}, u32[]{:S(2)}, u32[]{:S(2)}) %all-to-all-start.3) | async-done | bytes 262176 | tf_op jit(solution)/shard_map/all_to_all | solution.py:298
  192.9 1.0 reduce_sum.60
  193.9 0.8 maximum_maximum_fusion
  194.8 4.8 %all-to-all-start.4 = ((f32[64,8,128]{2,1,0:T(8,128)}), f32[64,8,128]{2,1,0:T(8,128)S(1)}, u32[]{:S(2)}, u32[]{:S(2)}) async-start(f32[64,8,128]{2,1,0:T(8,128)} %maximum_maximum_fusion), calls=%async_computation.5 | async-start | bytes 524288 | tf_op jit(solution)/shard_map/all_to_all | solution.py:298
  199.6 14.3 %all-to-all-done.4.refs_1_ = f32[64,8,128]{2,1,0:T(8,128)S(1)} async-done(((f32[64,8,128]{2,1,0:T(8,128)}), f32[64,8,128]{2,1,0:T(8,128)S(1)}, u32[]{:S(2)}, u32[]{:S(2)}) %all-to-all-start.4) | async-done | bytes 262176 | tf_op jit(solution)/shard_map/all_to_all | solution.py:298
  213.9 1.3 reduce-scatter.3.cloned.1.call-done
  215.2 2.4 convert_element_type.53
  217.7 5.2 %proj_gate_up.1 = f32[384,64]{1,0:T(8,128)S(1)} custom-call(s32[4]{0:T(128)S(1)} %pad_add_fusion.pos_ref, bf16[4,8,192,256]{3,2,1,0:T(8,128)(2,1)} %stack.55.own_ref, bf16[4,8,192,256]{3,2,1,0:T(8,128)(2,1)} %collective-permute-done.16.other_ref, bf16[2,32,8192]{2,1,0:T(8,128)(2,1)S(1)} %bitcast.82), custom_call_target="tpu_custom_call" | custom-call | flops 1000000000 | bytes 16000000 | tf_op jit(solution)/shard_map/proj_gate_up/pallas_call | solution.py:139
  224.3 12.1 %all_to_all.35 = f32[8,48,256]{2,1,0:T(8,128)S(1)} all-to-all(f32[8,48,256]{2,1,0:T(8,128)S(1)} %bitcast.94), channel_id=1, replica_groups=mesh['x'=4,'core'=2,'y'=4,'z'=8] {'x','core'}, dimensions={0} | all-to-all | bytes 786432 | tf_op jit(solution)/shard_map/all_to_all | solution.py:298
  236.4 0.8 broadcast_in_dim.46
  237.2 4.8 %all-to-all-start.6 = ((f32[8,48,256]{2,1,0:T(8,128)}), f32[8,48,256]{2,1,0:T(8,128)S(1)}, u32[]{:S(2)}, u32[]{:S(2)}) async-start(f32[8,48,256]{2,1,0:T(8,128)} %broadcast_in_dim.46), calls=%async_computation.8 | async-start | bytes 786432 | tf_op jit(solution)/shard_map/all_to_all | solution.py:298
  242.1 7.5 %all-to-all-done.6 = f32[8,48,256]{2,1,0:T(8,128)S(1)} async-done(((f32[8,48,256]{2,1,0:T(8,128)}), f32[8,48,256]{2,1,0:T(8,128)S(1)}, u32[]{:S(2)}, u32[]{:S(2)}) %all-to-all-start.6) | async-done | bytes 393248 | tf_op jit(solution)/shard_map/all_to_all | solution.py:298
  251.6 0.8 reshape.130
  253.5 3.6 %reduce-scatter.5.cloned.1.call-done = f32[1,192,256]{2,1,0:T(8,128)} async-done(((f32[8,192,256]{2,1,0:T(8,128)}), f32[1,192,256]{2,1,0:T(8,128)}) %reduce-scatter.5.cloned.1.call-update) | async-done | bytes 196624 | tf_op jit(solution)/shard_map/reduce_scatter | solution.py:390
  257.2 1.6 convert_bitcast_fusion
  (145 shorter events, 8.5 us)
Async XLA Ops:
  7.2 115.8 %copy-start = (bf16[2,32,512]{2,1,0:T(8,128)(2,1)S(1)}, bf16[2,32,512]{2,1,0:T(8,128)(2,1)}, u32[]{:S(2)}) copy-start(bf16[2,32,512]{2,1,0:T(8,128)(2,1)} %param.14) | copy-start | bytes 196612
  7.2 11.1 %copy-start.30 = (bf16[192,256]{1,0:T(8,128)(2,1)S(1)}, bf16[192,256]{1,0:T(8,128)(2,1)}, u32[]{:S(2)}) copy-start(bf16[192,256]{1,0:T(8,128)(2,1)} %param.11) | copy-start | bytes 294916
  7.2 23.9 %copy-start.26 = (bf16[512,32]{0,1:T(8,128)(2,1)S(1)}, bf16[512,32]{0,1:T(8,128)(2,1)}, u32[]{:S(2)}) copy-start(bf16[512,32]{0,1:T(8,128)(2,1)} %param.17) | copy-start | bytes 98308
  7.2 23.9 %copy-start.19 = (bf16[32,8192]{1,0:T(8,128)(2,1)S(1)}, bf16[32,8192]{1,0:T(8,128)(2,1)}, u32[]{:S(2)}) copy-start(bf16[32,8192]{1,0:T(8,128)(2,1)} %right_ref.3) | copy-start | bytes 1572868
  7.2 127.3 %all-gather.2.cloned.1.call-start = ((), (), s32[]{:S(2)}) async-start(), calls=%async_computation.9 | async-start | bytes 18874368 | tf_op jit(solution)/shard_map/all_gather | solution.py:329
  9.8 31.6 %all-to-all-start = ((bf16[8,192,256]{2,1,0:T(8,128)(2,1)}), bf16[8,192,256]{2,1,0:T(8,128)(2,1)S(1)}, u32[]{:S(2)}, u32[]{:S(2)}) async-start(bf16[8,192,256]{2,1,0:T(8,128)(2,1)} %broadcast_in_dim.39), calls=%async_computation | async-start | bytes 1572864 | tf_op jit(solution)/shard_map/all_to_all | solution.py:298
  18.3 5.9 %collective-permute-start = (bf16[192,256]{1,0:T(8,128)(2,1)S(1)}, bf16[192,256]{1,0:T(8,128)(2,1)S(1)}, u32[]{:S(2)}, u32[]{:S(2)}) collective-permute-start(bf16[192,256]{1,0:T(8,128)(2,1)S(1)} %copy-done.30), channel_id=1, source_target_pairs={{0,8},{8,16},{16,24},{24,0},{1,9},{9,17},{17,25},{25,1},{2,10},{10... | collective-permute-start | bytes 294920 | tf_op jit(solution)/shard_map/ppermute | solution.py:21
  19.9 5.3 %collective-permute-start.1 = (bf16[192,256]{1,0:T(8,128)(2,1)S(1)}, bf16[192,256]{1,0:T(8,128)(2,1)S(1)}, u32[]{:S(2)}, u32[]{:S(2)}) collective-permute-start(bf16[192,256]{1,0:T(8,128)(2,1)S(1)} %copy-done.30), channel_id=1, source_target_pairs={{0,24},{8,0},{16,8},{24,16},{1,25},{9,1},{17,9},{25,17},{2,26},{10... | collective-permute-start | bytes 294920 | tf_op jit(solution)/shard_map/ppermute | solution.py:21
  21.6 6.1 %collective-permute-start.2 = (bf16[192,256]{1,0:T(8,128)(2,1)S(1)}, bf16[192,256]{1,0:T(8,128)(2,1)S(1)}, u32[]{:S(2)}, u32[]{:S(2)}) collective-permute-start(bf16[192,256]{1,0:T(8,128)(2,1)S(1)} %copy-done.30), channel_id=1, source_target_pairs={{0,16},{8,24},{16,0},{24,8},{1,17},{9,25},{17,1},{25,9},{2,18},{10... | collective-permute-start | bytes 294920 | tf_op jit(solution)/shard_map/ppermute | solution.py:21
  27.8 23.2 %collective-permute-start.6 = (bf16[4,192,256]{2,1,0:T(8,128)(2,1)S(1)}, bf16[4,192,256]{2,1,0:T(8,128)(2,1)S(1)}, u32[]{:S(2)}, u32[]{:S(2)}) collective-permute-start(bf16[4,192,256]{2,1,0:T(8,128)(2,1)S(1)} %pad_maximum_fusion.1.refs_3_), channel_id=1, source_target_pairs={{0,7},{1,0},{2,1},{3,2},{4,3},{5,4},{6,5},{7,6},{8,15},{9,8},{10,9... | collective-permute-start | bytes 1179656 | tf_op jit(solution)/shard_map/ppermute | solution.py:21
  37.4 0.7 copy-start.18
  41.4 0.9 copy-start.2
  42.3 24.6 %all-to-all-start.1 = ((f32[64,8,128]{2,1,0:T(8,128)}), f32[64,8,128]{2,1,0:T(8,128)}, u32[]{:S(2)}, u32[]{:S(2)}) async-start(f32[64,8,128]{2,1,0:T(8,128)} %after.8), calls=%async_computation.1 | async-start | bytes 524288 | tf_op jit(solution)/shard_map/all_to_all | solution.py:298
  49.4 17.5 %collective-permute-start.3 = (bf16[4,192,256]{2,1,0:T(8,128)(2,1)S(1)}, bf16[4,192,256]{2,1,0:T(8,128)(2,1)S(1)}, u32[]{:S(2)}, u32[]{:S(2)}) collective-permute-start(bf16[4,192,256]{2,1,0:T(8,128)(2,1)S(1)} %pad_maximum_fusion.1.refs_3_), channel_id=1, source_target_pairs={{0,1},{1,2},{2,3},{3,4},{4,5},{5,6},{6,7},{7,0},{8,9},{9,10},{10,1... | collective-permute-start | bytes 1179656 | tf_op jit(solution)/shard_map/ppermute | solution.py:21
  51.0 27.5 %copy-start.20 = (bf16[4,192,256]{2,1,0:T(8,128)(2,1)}, bf16[4,192,256]{2,1,0:T(8,128)(2,1)S(1)}, u32[]{:S(2)}) copy-start(bf16[4,192,256]{2,1,0:T(8,128)(2,1)S(1)} %collective-permute-done.6.refs_4_) | copy-start | bytes 1179652
  51.0 27.5 %collective-permute-start.7 = (bf16[4,192,256]{2,1,0:T(8,128)(2,1)S(1)}, bf16[4,192,256]{2,1,0:T(8,128)(2,1)}, u32[]{:S(2)}, u32[]{:S(2)}) collective-permute-start(bf16[4,192,256]{2,1,0:T(8,128)(2,1)S(1)} %collective-permute-done.6.refs_4_), channel_id=1, source_target_pairs={{0,7},{1,0},{2,1},{3,2},{4,3},{5,4},{6,5},{7,6},{8,15},{9,8},{10,9... | collective-permute-start | bytes 1179656 | tf_op jit(solution)/shard_map/ppermute | solution.py:21
  52.7 44.3 %collective-permute-start.13 = (bf16[8,192,256]{2,1,0:T(8,128)(2,1)}, bf16[8,192,256]{2,1,0:T(8,128)(2,1)S(1)}, u32[]{:S(2)}, u32[]{:S(2)}) collective-permute-start(bf16[8,192,256]{2,1,0:T(8,128)(2,1)} %after.7.refs_1_), channel_id=1, source_target_pairs={{0,24},{8,0},{16,8},{24,16},{1,25},{9,1},{17,9},{25,17},{2,26},{10... | collective-permute-start | bytes 2359304 | tf_op jit(solution)/shard_map/ppermute | solution.py:21
  55.5 41.6 %collective-permute-start.12 = (bf16[8,192,256]{2,1,0:T(8,128)(2,1)}, bf16[8,192,256]{2,1,0:T(8,128)(2,1)S(1)}, u32[]{:S(2)}, u32[]{:S(2)}) collective-permute-start(bf16[8,192,256]{2,1,0:T(8,128)(2,1)} %after.7.refs_1_), channel_id=1, source_target_pairs={{0,8},{8,16},{16,24},{24,0},{1,9},{9,17},{17,25},{25,1},{2,10},{10... | collective-permute-start | bytes 2359304 | tf_op jit(solution)/shard_map/ppermute | solution.py:21
  66.9 14.4 %copy-start.22 = (bf16[4,192,256]{2,1,0:T(8,128)(2,1)}, bf16[4,192,256]{2,1,0:T(8,128)(2,1)S(1)}, u32[]{:S(2)}) copy-start(bf16[4,192,256]{2,1,0:T(8,128)(2,1)S(1)} %collective-permute-done.3.refs_2_) | copy-start | bytes 1179652
  66.9 14.4 %collective-permute-start.4 = (bf16[4,192,256]{2,1,0:T(8,128)(2,1)S(1)}, bf16[4,192,256]{2,1,0:T(8,128)(2,1)}, u32[]{:S(2)}, u32[]{:S(2)}) collective-permute-start(bf16[4,192,256]{2,1,0:T(8,128)(2,1)S(1)} %collective-permute-done.3.refs_2_), channel_id=1, source_target_pairs={{0,1},{1,2},{2,3},{3,4},{4,5},{5,6},{6,7},{7,0},{8,9},{9,10},{10,1... | collective-permute-start | bytes 1179656 | tf_op jit(solution)/shard_map/ppermute | solution.py:21
  68.1 29.0 %copy-start.33 = (f32[128]{0:T(128)}, f32[128]{0:T(128)S(1)}, u32[]{:S(2)}) copy-start(f32[128]{0:T(128)S(1)} %reduce_sum.58) | copy-start | bytes 1540
  68.8 36.2 %all-to-all-start.2 = ((f32[64,8,128]{2,1,0:T(8,128)}), f32[64,8,128]{2,1,0:T(8,128)}, u32[]{:S(2)}, u32[]{:S(2)}) async-start(f32[64,8,128]{2,1,0:T(8,128)} %broadcast_in_dim_broadcast_in_dim_broadcast_in_dim.2), calls=%async_computation.2 | async-start | bytes 524288 | tf_op jit(solution)/shard_map/all_to_all | solution.py:298
  78.5 136.7 %reduce-scatter.3.cloned.1.call-start = ((), (), s32[]{:S(2)}) async-start(), calls=%async_computation.10 | async-start | bytes 3932160 | tf_op jit(solution)/shard_map/reduce_scatter | solution.py:384
  78.5 16.2 %collective-permute-start.8 = (bf16[4,192,256]{2,1,0:T(8,128)(2,1)}, bf16[4,192,256]{2,1,0:T(8,128)(2,1)S(1)}, u32[]{:S(2)}, u32[]{:S(2)}) collective-permute-start(bf16[4,192,256]{2,1,0:T(8,128)(2,1)} %collective-permute-done.7.refs_5_), channel_id=1, source_target_pairs={{0,7},{1,0},{2,1},{3,2},{4,3},{5,4},{6,5},{7,6},{8,15},{9,8},{10,9... | collective-permute-start | bytes 1179656 | tf_op jit(solution)/shard_map/ppermute | solution.py:21
  81.3 25.4 %collective-permute-start.5 = (bf16[4,192,256]{2,1,0:T(8,128)(2,1)}, bf16[4,192,256]{2,1,0:T(8,128)(2,1)S(1)}, u32[]{:S(2)}, u32[]{:S(2)}) collective-permute-start(bf16[4,192,256]{2,1,0:T(8,128)(2,1)} %collective-permute-done.4.refs_1_), channel_id=1, source_target_pairs={{0,1},{1,2},{2,3},{3,4},{4,5},{5,6},{6,7},{7,0},{8,9},{9,10},{10,1... | collective-permute-start | bytes 1179656 | tf_op jit(solution)/shard_map/ppermute | solution.py:21
  94.7 12.0 %copy-start.14 = (bf16[4,192,256]{2,1,0:T(8,128)(2,1)}, bf16[4,192,256]{2,1,0:T(8,128)(2,1)S(1)}, u32[]{:S(2)}) copy-start(bf16[4,192,256]{2,1,0:T(8,128)(2,1)S(1)} %collective-permute-done.8.refs_1_.refs_6_) | copy-start | bytes 1179652
  95.5 13.5 %collective-permute-start.10 = (bf16[2,192,256]{2,1,0:T(8,128)(2,1)}, bf16[2,192,256]{2,1,0:T(8,128)(2,1)}, u32[]{:S(2)}, u32[]{:S(2)}) collective-permute-start(bf16[2,192,256]{2,1,0:T(8,128)(2,1)} %slice.116), channel_id=1, source_target_pairs={{0,7},{1,0},{2,1},{3,2},{4,3},{5,4},{6,5},{7,6},{8,15},{9,8},{10,9... | collective-permute-start | bytes 589832 | tf_op jit(solution)/shard_map/ppermute | solution.py:21
  97.1 0.9 copy-start.6
  97.1 1.1 copy-start.8
  98.2 17.4 %copy-start.21 = (bf16[4,192,256]{2,1,0:T(8,128)(2,1)S(1)}, bf16[4,192,256]{2,1,0:T(8,128)(2,1)}, u32[]{:S(2)}) copy-start(bf16[4,192,256]{2,1,0:T(8,128)(2,1)} %copy-done.20) | copy-start | bytes 1179652
  98.2 17.4 %copy-start.23 = (bf16[4,192,256]{2,1,0:T(8,128)(2,1)S(1)}, bf16[4,192,256]{2,1,0:T(8,128)(2,1)}, u32[]{:S(2)}) copy-start(bf16[4,192,256]{2,1,0:T(8,128)(2,1)} %copy-done.22) | copy-start | bytes 1179652
  100.1 20.5 %collective-permute-start.14 = (bf16[4,192,256]{2,1,0:T(8,128)(2,1)}, bf16[4,192,256]{2,1,0:T(8,128)(2,1)S(1)}, u32[]{:S(2)}, u32[]{:S(2)}) collective-permute-start(bf16[4,192,256]{2,1,0:T(8,128)(2,1)} %slice.117), channel_id=1, source_target_pairs={{0,8},{8,16},{16,24},{24,0},{1,9},{9,17},{17,25},{25,1},{2,10},{10... | collective-permute-start | bytes 1179656 | tf_op jit(solution)/shard_map/ppermute | solution.py:21
  103.5 17.1 %collective-permute-start.15 = (bf16[4,192,256]{2,1,0:T(8,128)(2,1)}, bf16[4,192,256]{2,1,0:T(8,128)(2,1)S(1)}, u32[]{:S(2)}, u32[]{:S(2)}) collective-permute-start(bf16[4,192,256]{2,1,0:T(8,128)(2,1)} %slice.118), channel_id=1, source_target_pairs={{0,24},{8,0},{16,8},{24,16},{1,25},{9,1},{17,9},{25,17},{2,26},{10... | collective-permute-start | bytes 1179656 | tf_op jit(solution)/shard_map/ppermute | solution.py:21
  106.7 0.8 copy-start.16
  108.4 12.2 %copy-start.3 = (bf16[8,192,256]{2,1,0:T(8,128)(2,1)S(1)}, bf16[8,192,256]{2,1,0:T(8,128)(2,1)}, u32[]{:S(2)}) copy-start(bf16[8,192,256]{2,1,0:T(8,128)(2,1)} %after.7.refs_1_) | copy-start | bytes 2359300
  108.4 12.2 %copy-start.7 = (bf16[8,192,256]{2,1,0:T(8,128)(2,1)S(1)}, bf16[8,192,256]{2,1,0:T(8,128)(2,1)}, u32[]{:S(2)}) copy-start(bf16[8,192,256]{2,1,0:T(8,128)(2,1)} %copy-done.6) | copy-start | bytes 2359300
  108.4 12.2 %copy-start.9 = (bf16[8,192,256]{2,1,0:T(8,128)(2,1)S(1)}, bf16[8,192,256]{2,1,0:T(8,128)(2,1)}, u32[]{:S(2)}) copy-start(bf16[8,192,256]{2,1,0:T(8,128)(2,1)} %after.10.refs_0_) | copy-start | bytes 2359300
  108.4 7.2 %collective-permute-start.9 = (bf16[2,192,256]{2,1,0:T(8,128)(2,1)S(1)}, bf16[2,192,256]{2,1,0:T(8,128)(2,1)S(1)}, u32[]{:S(2)}, u32[]{:S(2)}) collective-permute-start(bf16[2,192,256]{2,1,0:T(8,128)(2,1)S(1)} %slice.115), channel_id=1, source_target_pairs={{0,1},{1,2},{2,3},{3,4},{4,5},{5,6},{6,7},{7,0},{8,9},{9,10},{10,1... | collective-permute-start | bytes 589832 | tf_op jit(solution)/shard_map/ppermute | solution.py:21
  115.6 1.0 copy-start.15
  116.6 1.0 copy-start.17
  120.6 2.4 copy-start.32
  120.6 6.0 %collective-permute-start.11 = (bf16[8,4,192,256]{3,2,1,0:T(8,128)(2,1)}, bf16[8,4,192,256]{3,2,1,0:T(8,128)(2,1)}, u32[]{:S(2)}, u32[]{:S(2)}) collective-permute-start(bf16[8,4,192,256]{3,2,1,0:T(8,128)(2,1)} %stack.54.own_ref), channel_id=1, source_target_pairs={{0,32},{32,0},{1,33},{33,1},{2,34},{34,2},{3,35},{35,3},{4,36},{36... | collective-permute-start | bytes 9437192 | tf_op jit(solution)/shard_map/ppermute | solution.py:349
  122.4 12.1 %collective-permute-start.16 = (bf16[4,8,192,256]{3,2,1,0:T(8,128)(2,1)}, bf16[4,8,192,256]{3,2,1,0:T(8,128)(2,1)}, u32[]{:S(2)}, u32[]{:S(2)}) collective-permute-start(bf16[4,8,192,256]{3,2,1,0:T(8,128)(2,1)} %stack.55.own_ref), channel_id=1, source_target_pairs={{0,32},{32,0},{1,33},{33,1},{2,34},{34,2},{3,35},{35,3},{4,36},{36... | collective-permute-start | bytes 9437192 | tf_op jit(solution)/shard_map/ppermute | solution.py:348
  126.6 7.9 %copy-start.10 = (bf16[2,8192,32]{1,2,0:T(8,128)(2,1)S(1)}, bf16[2,8192,32]{1,2,0:T(8,128)(2,1)}, u32[]{:S(2)}) copy-start(bf16[2,8192,32]{1,2,0:T(8,128)(2,1)} %param.13) | copy-start | bytes 3145732
  133.8 0.7 copy-start.24
  134.5 13.5 %copy-start.34 = (f32[2,512]{1,0:T(2,128)S(1)}, f32[2,512]{1,0:T(2,128)}, u32[]{:S(2)}) copy-start(f32[2,512]{1,0:T(2,128)} %param.15) | copy-start | bytes 12292
  148.5 10.1 %copy-start.4 = (bf16[2,384,256]{2,1,0:T(8,128)(2,1)}, bf16[2,384,256]{2,1,0:T(8,128)(2,1)S(1)}, u32[]{:S(2)}) copy-start(bf16[2,384,256]{2,1,0:T(8,128)(2,1)S(1)} %get-tuple-element.28.grads_ref) | copy-start | bytes 1179652
  156.6 1.6 copy-start.12
  158.3 6.0 %collective-permute-start.17 = (bf16[4,8,192,256]{3,2,1,0:T(8,128)(2,1)}, bf16[4,8,192,256]{3,2,1,0:T(8,128)(2,1)}, u32[]{:S(2)}, u32[]{:S(2)}) collective-permute-start(bf16[4,8,192,256]{3,2,1,0:T(8,128)(2,1)} %get-tuple-element.23), channel_id=1, source_target_pairs={{0,32},{32,0},{1,33},{33,1},{2,34},{34,2},{3,35},{35,3},{4,36},{36... | collective-permute-start | bytes 9437192 | tf_op jit(solution)/shard_map/ppermute | solution.py:372
  160.1 4.2 %copy-start.13 = (bf16[4,8,192,256]{3,2,1,0:T(8,128)(2,1)S(1)}, bf16[4,8,192,256]{3,2,1,0:T(8,128)(2,1)}, u32[]{:S(2)}) copy-start(bf16[4,8,192,256]{3,2,1,0:T(8,128)(2,1)} %copy-done.12) | copy-start | bytes 9437188
  168.9 10.1 %copy-start.1 = (bf16[8,4,192,256]{3,2,1,0:T(8,128)(2,1)S(1)}, bf16[8,4,192,256]{3,2,1,0:T(8,128)(2,1)}, u32[]{:S(2)}) copy-start(bf16[8,4,192,256]{3,2,1,0:T(8,128)(2,1)} %stack.54.own_ref) | copy-start | bytes 9437188
  168.9 23.9 %all-to-all-start.3 = ((f32[64,8,128]{2,1,0:T(8,128)}), f32[64,8,128]{2,1,0:T(8,128)}, u32[]{:S(2)}, u32[]{:S(2)}) async-start(f32[64,8,128]{2,1,0:T(8,128)} %after.12), calls=%async_computation.4 | async-start | bytes 524288 | tf_op jit(solution)/shard_map/all_to_all | solution.py:298
  194.8 22.9 %copy-start.11 = (bf16[2,8192,32]{1,2,0:T(8,128)(2,1)S(1)}, bf16[2,8192,32]{1,2,0:T(8,128)(2,1)}, u32[]{:S(2)}) copy-start(bf16[2,8192,32]{1,2,0:T(8,128)(2,1)} %param.13) | copy-start | bytes 3145732
  194.8 19.1 %all-to-all-start.4 = ((f32[64,8,128]{2,1,0:T(8,128)}), f32[64,8,128]{2,1,0:T(8,128)S(1)}, u32[]{:S(2)}, u32[]{:S(2)}) async-start(f32[64,8,128]{2,1,0:T(8,128)} %maximum_maximum_fusion), calls=%async_computation.5 | async-start | bytes 524288 | tf_op jit(solution)/shard_map/all_to_all | solution.py:298
  199.5 57.7 %reduce-scatter.5.cloned.1.call-start = ((), (), s32[]{:S(2)}) async-start(), calls=%async_computation.11 | async-start | bytes 1769472 | tf_op jit(solution)/shard_map/reduce_scatter | solution.py:390
  213.9 1.3 copy-start.27
  217.7 5.3 %copy-start.5 = (bf16[2,384,256]{2,1,0:T(8,128)(2,1)S(1)}, bf16[2,384,256]{2,1,0:T(8,128)(2,1)}, u32[]{:S(2)}) copy-start(bf16[2,384,256]{2,1,0:T(8,128)(2,1)} %copy-done.4) | copy-start | bytes 1179652
  217.7 5.8 %copy-start.25 = (f32[384,32]{1,0:T(8,128)S(1)}, f32[384,32]{1,0:T(8,128)}, u32[]{:S(2)}) copy-start(f32[384,32]{1,0:T(8,128)} %copy-done.24) | copy-start | bytes 147460
  217.7 6.0 %copy-start.28 = (f32[64,8,128]{2,1,0:T(8,128)S(1)}, f32[64,8,128]{2,1,0:T(8,128)}, u32[]{:S(2)}) copy-start(f32[64,8,128]{2,1,0:T(8,128)} %copy-done.27) | copy-start | bytes 786436
  217.7 6.2 %copy-start.29 = (bf16[192,256]{1,0:T(8,128)(2,1)S(1)}, bf16[192,256]{1,0:T(8,128)(2,1)}, u32[]{:S(2)}) copy-start(bf16[192,256]{1,0:T(8,128)(2,1)} %param.10) | copy-start | bytes 294916
  217.7 6.3 %copy-start.31 = (bf16[192,256]{1,0:T(8,128)(2,1)S(1)}, bf16[192,256]{1,0:T(8,128)(2,1)}, u32[]{:S(2)}) copy-start(bf16[192,256]{1,0:T(8,128)(2,1)} %param.11) | copy-start | bytes 294916
  237.2 12.3 %all-to-all-start.6 = ((f32[8,48,256]{2,1,0:T(8,128)}), f32[8,48,256]{2,1,0:T(8,128)S(1)}, u32[]{:S(2)}, u32[]{:S(2)}) async-start(f32[8,48,256]{2,1,0:T(8,128)} %broadcast_in_dim.46), calls=%async_computation.8 | async-start | bytes 786432 | tf_op jit(solution)/shard_map/all_to_all | solution.py:298
Sparse Core Ops, SparseCore 0:
  9.9 90.0 all-gather.1
  169.1 46.0 reduce-scatter.2
  217.8 39.3 reduce-scatter.4

commit v4 on v3

--- a/solution.py
+++ b/solution.py
@@ -120,7 +120,7 @@
     return pl.BlockSpec((NZ, 1, t, w), lambda i, p: (0, rel(i, p[2], 1, NY), 0, 0))
 
 
-def proj_body(pos_ref, own_ref, other_ref, left_ref, out_ref):
+def proj_body(pos_ref, own_ref, other_ref, left_ref, _, out_ref):
     @pl.when(pl.program_id(0) == 0)
     def _():
         out_ref[...] = jnp.zeros_like(out_ref)
@@ -134,19 +134,24 @@
     out_ref[...] += total
 
 
-def proj_gate_up(pos, own, other, left):
+def proj_gate_up(pos, own, other, left, before):
     _, _, t, w = own.shape
     return call(
         proj_body,
         "proj_gate_up",
         (NY,),
-        [x_spec(t, w), x_spec(t, w), pl.BlockSpec((2, 32, NZ * w), lambda i, p: (0, 0, i))],
+        [
+            x_spec(t, w),
+            x_spec(t, w),
+            pl.BlockSpec((2, 32, NZ * w), lambda i, p: (0, 0, i)),
+            pl.BlockSpec(memory_space=pl.ANY),
+        ],
         pl.BlockSpec((2 * t, 64), lambda i, p: (0, 0)),
         jax.ShapeDtypeStruct((2 * t, 64), F32),
-    )(pos, own, other, left)
-
-
-def grad_act_body(pos_ref, own_ref, other_ref, scale_ref, tile_ref, right_ref, out_ref, rows_ref):
+    )(pos, own, other, left, before)
+
+
+def grad_act_body(pos_ref, own_ref, other_ref, scale_ref, tile_ref, right_ref, _, out_ref, rows_ref):
     @pl.when(pl.program_id(0) == 0)
     def _():
         out_ref[...] = jnp.zeros_like(out_ref)
@@ -164,7 +169,7 @@
     rows_ref[...] += rows
 
 
-def grad_act_rows(pos, own, other, scale, tile, right):
+def grad_act_rows(pos, own, other, scale, tile, right, before):
     _, _, t, w = own.shape
     f, d = tile.shape
     return call(
@@ -177,13 +182,14 @@
             pl.BlockSpec((NZ, 1, w), lambda i, p: (i, 0, 0)),
             pl.BlockSpec((f, NZ * w), lambda i, p: (0, i)),
             pl.BlockSpec((32, NZ * w), lambda i, p: (0, i)),
+            pl.BlockSpec(memory_space=pl.ANY),
         ],
         [
             pl.BlockSpec((2 * t, f), lambda i, p: (0, 0)),
             pl.BlockSpec((2 * t, 32), lambda i, p: (0, 0)),
         ],
         [jax.ShapeDtypeStruct((2 * t, f), F32), jax.ShapeDtypeStruct((2 * t, 32), F32)],
-    )(pos, own, other, scale, tile, right)
+    )(pos, own, other, scale, tile, right, before)
 
 
 def dot_down_body(pos_ref, own_ref, other_ref, act_ref, tile_ref, out_ref):
@@ -215,7 +221,9 @@
     )(pos, own, other, act, tile)
 
 
-def gate_up_body(pos_ref, own_ref, other_ref, frozen_ref, left_ref, right_ref, tile_ref, pre_ref, squares_ref):
+def gate_up_body(
+    pos_ref, own_ref, other_ref, frozen_ref, left_ref, right_ref, _, tile_ref, pre_ref, squares_ref
+):
     @pl.when(pl.program_id(0) == 0)
     def _():
         pre_ref[...] = jnp.zeros_like(pre_ref)
@@ -238,7 +246,7 @@
         squares_ref[k] += squares
 
 
-def gate_up(pos, own, other, frozen, left, right):
+def gate_up(pos, own, other, frozen, left, right, before):
     _, _, t, w = own.shape
     _, d, f = frozen.shape
     f, rows = f // NC, NZ * w
@@ -252,6 +260,7 @@
             pl.BlockSpec((2, rows, f), lambda i, p: (0, i, p[1])),
             pl.BlockSpec((2, 32, rows), lambda i, p: (0, 0, i)),
             pl.BlockSpec((2, 32, f), lambda i, p: (0, 0, 0)),
+            pl.BlockSpec(memory_space=pl.ANY),
         ],
         [
             pl.BlockSpec((2, rows, f), lambda i, p: (0, i, 0)),
@@ -263,35 +272,36 @@
             jax.ShapeDtypeStruct((2, 2 * t, f), F32),
             jax.ShapeDtypeStruct((2, 8, f), F32),
         ],
-    )(pos, own, other, frozen, left, right)
-
-
-def grad_in_body(pos_ref, grads_ref, tile_ref, own_ref, other_ref):
-    t = grads_ref.shape[1] // 2
+    )(pos, own, other, frozen, left, right, before)
+
+
+def grad_in_body(pos_ref, grads_ref, tile_ref, *refs):
+    *from_ref, out_ref = refs
     for i in range(NZ):
         rows = slice(i * 256, (i + 1) * 256)
         out = lax.dot_general(grads_ref[0], tile_ref[0, rows], NT, preferred_element_type=F32)
         out += lax.dot_general(grads_ref[1], tile_ref[1, rows], NT, preferred_element_type=F32)
-        out = out.astype(BF16)
-        own_ref[0, i] = out[:t]
-        other_ref[0, i] = out[t:]
-
-
-def grad_in_parts(pos, grads, tiles):
+        if from_ref:
+            out += from_ref[0][i, 0].astype(F32)
+        out_ref[i, 0] = out.astype(BF16)
+
+
+def grad_in_terms(pos, grads, tiles, half, *from_other):
     _, t, f = grads.shape
-    out = pl.BlockSpec((1, NZ, t // 2, 256), lambda i, p: (i, 0, 0, 0))
-    shape = jax.ShapeDtypeStruct((NY, NZ, t // 2, 256), BF16)
+    t = t // 2
+    out = pl.BlockSpec((NZ, 1, t, 256), lambda i, p: (0, i, 0, 0))
     return call(
         grad_in_body,
         "grad_in",
         (NY,),
         [
-            pl.BlockSpec((2, t, f), lambda i, p: (0, 0, 0)),
+            pl.BlockSpec((2, t, f), lambda i, p: (0, half, 0)),
             pl.BlockSpec((2, NZ * 256, f), lambda i, p: (0, i, 0)),
-        ],
-        [out, out],
-        [shape, shape],
-    )(pos, grads, tiles)
+        ]
+        + [out] * len(from_other),
+        out,
+        jax.ShapeDtypeStruct((NZ, NY, t, 256), BF16),
+    )(pos, grads, tiles, *from_other)
 
 
 def exchange(parts, axes):
@@ -334,28 +344,29 @@
     tile_down, down_squares = merge_down(pos, frozen_down, left_down.T, right_down)
     x_z = after(x_z, down_squares)
     yr, yl = both_ways(x_z, x_z, "y", NY)
-    down_sum = jnp.sum(sum_parts(after(down_squares, x_z), CMP), axis=0, keepdims=True)
-    yr = after(yr, yl, down_sum)
     yfr, yfl = both_ways(yr[: NZ // 2], yl[NZ // 2 :], "y", NY)
-    down_sums = gather_small(jnp.broadcast_to(down_sum, (8, 128)), CMP, NC * NMP)[:, :1]
     x_own = stack([yr, x_z, yl], yfr, yfl)
     r1, l1 = both_ways(g_y, g_y, "z", NZ)
+    down_sum = jnp.sum(sum_parts(after(down_squares, r1, l1), CMP), axis=0, keepdims=True)
     r2, l2 = both_ways(r1, l1, "z", NZ)
+    r2, l2 = after(r2, down_sum), after(l2, down_sum)
+    down_sums = gather_small(jnp.broadcast_to(down_sum, (8, 128)), CMP, NC * NMP)[:, :1]
     r3, l3 = both_ways(r2, l2, "z", NZ)
-    r3 = after(r3, l3, down_sums)
+    r3, l3 = after(r3, down_sums), after(l3, down_sums)
     zfr, zfl = both_ways(r3[: NY // 2], l3[NY // 2 :], "z", NZ)
-    g_own = stack([r3, r2, r1, g_y, l1, l2, l3], zfr, zfl)
     x_other = lax.ppermute(x_own, "core", OTHER)
-    g_other = lax.ppermute(g_own, "core", OTHER)
     right = half_of(right_gu, ic, 2)
     left_t = left_gu.swapaxes(1, 2)
 
     norm_down = jnp.sqrt(down_sums.reshape(NMP, 1, width) + 1e-06)
     scale_down = magnitude_down.reshape(NMP, 1, width) / norm_down
-    grad_act, rows_down = grad_act_rows(pos, g_own, g_other, scale_down, tile_down, right_down)
-
-    proj_gu = proj_gate_up(pos, x_own, x_other, left_t).astype(BF16)
-    tiles, pre_gu, squares = gate_up(pos, x_own, x_other, frozen_full, left_t, right)
+
+    tiles, pre_gu, squares = gate_up(pos, x_own, x_other, frozen_full, left_t, right, down_sums)
+    g_own = stack([r3, r2, r1, g_y, l1, l2, l3], after(zfr, squares), zfl)
+    g_other = lax.ppermute(g_own, "core", OTHER)
+    proj_gu = proj_gate_up(pos, x_own, x_other, left_t, g_own)
+    grad_act, rows_down = grad_act_rows(pos, g_own, g_other, scale_down, tile_down, right_down, proj_gu)
+    proj_gu = proj_gu.astype(BF16)
     norm_gu = jnp.sqrt(jnp.sum(squares, axis=1) + 1e-06)
     scale_gu = half_of(magnitude_gu, ic, 1) / norm_gu
     hid_gu = pre_gu * scale_gu[:, None, :]
@@ -368,7 +379,7 @@
     dot_gu = jnp.sum(grad_hid * pre_gu, axis=1) / norm_gu
     pre_grads = (grad_hid * scale_gu[:, None, :]).astype(BF16)
 
-    own_terms, other_terms = grad_in_parts(pos, pre_grads, tiles)
+    other_terms = grad_in_terms(pos, pre_grads, tiles, 1)
     from_other = lax.ppermute(other_terms, "core", OTHER)
 
     rows_gu = [
@@ -379,15 +390,21 @@
     rows = rows.reshape(NC, NMP, tokens // NMP, 128)
     rows = jnp.where(ic == 0, rows, rows[::-1]).reshape(NC * NMP, tokens // NMP, 128)
     rows = jnp.pad(rows, ((0, 0), (0, 2), (0, 0)))
-    from_other = after(from_other, rows)
-    terms = (own_terms.astype(F32) + from_other.astype(F32)).astype(BF16)
-    over_y = lax.psum_scatter(terms, "y")
+    dots = dot_down_sums(pos, g_own, g_other, after(act, other_terms), tile_down).reshape(NMP, NC, 1, 128)
+    dots = dots.swapaxes(0, 1).reshape(NC * NMP, 1, 128)
+    terms = grad_in_terms(pos, pre_grads, tiles, 0, after(from_other, rows, dots))
+    over_z = lax.psum_scatter(terms, "z")
     rows = sum_parts(after(rows, terms), CMP)
-    dots = dot_down_sums(pos, g_own, g_other, act, tile_down).reshape(NMP, NC, 1, 128)
-    dots = dots.swapaxes(0, 1).reshape(NC * NMP, 1, 128)
     rows = jnp.broadcast_to(rows[None, :6], (NC * NMP, 6, 128))
     rows = exchange(jnp.concatenate([rows, dots, jnp.zeros_like(dots)], axis=1), CMP)
-    grad_in = lax.psum_scatter(after(over_y, rows).astype(F32), "z")
+    right_gu_parts = [
+        lax.dot_general(proj_gu[:, 32 * k : 32 * k + 32], pre_grads[k], TN, preferred_element_type=F32)
+        for k in range(2)
+    ]
+    left_down_part = lax.dot_general(rows_down.astype(BF16), act, TN, preferred_element_type=F32)
+    mine = jnp.concatenate(
+        [2.0 * p for p in right_gu_parts] + [2.0 * left_down_part, jnp.pad(dot_gu, ((0, 30), (0, 0)))]
+    )
     dots = jnp.sum(rows[:, 6:7], axis=0)
     dots = jnp.concatenate([jnp.where(ic == c, dots, 0.0) for c in range(NC)], axis=1)
     rows = lax.dynamic_slice_in_dim(rows[:, :6], ic * NMP, NMP, 0).reshape(tokens, 128).astype(BF16)
@@ -398,19 +415,17 @@
     left_gu_part = lax.dot_general(rows[:, :64], inputs, TN, preferred_element_type=F32)
     right_down_part = lax.dot_general(rows[:, 64:96], own_grads, TN, preferred_element_type=F32)
 
-    right_gu_parts = [
-        lax.dot_general(proj_gu[:, 32 * k : 32 * k + 32], pre_grads[k], TN, preferred_element_type=F32)
-        for k in range(2)
-    ]
-    left_down_part = lax.dot_general(rows_down.astype(BF16), act, TN, preferred_element_type=F32)
-    mine = jnp.concatenate(
-        [2.0 * p for p in right_gu_parts] + [2.0 * left_down_part, jnp.pad(dot_gu, ((0, 30), (0, 0)))]
-    )
     cores = [jnp.where(ic == c, mine, 0.0) for c in range(NC)]
     sums = jnp.concatenate(
         [2.0 * left_gu_part, 2.0 * right_down_part, jnp.pad(dots, ((0, 31), (0, 0)))] + cores
     )
-    sums = gather_small(sum_parts(sums.reshape(NDP, 48, width), DP), DP, NDP).reshape(384, width)
+    sums = sum_parts(sums.reshape(NDP, 48, width), DP)
+    over_z = after(over_z, sums)
+    over_z = jnp.roll(over_z, 1 - iy, 0)
+    grad_in = over_z[1].astype(F32)
+    for p in (0, 2, 3):
+        grad_in += step(over_z[p], "y", NY, p - 1).astype(F32)
+    sums = gather_small(sums, DP, NDP).reshape(384, width)
     cores = sums[128:].reshape(NC, 128, hidden).swapaxes(0, 1).reshape(128, NC * hidden)
     return (
         grad_in.astype(BF16),

time: 267 us -> 310 us (1.16)
  waiting for transfers between devices: 81.9 us -> 120 us
  local copies, waits for them, and re-layouts: 21 us -> 30.3 us
  other arithmetic: 14.8 us -> 6.54 us
  Pallas kernels: 51.4 us -> 58.6 us
  starting transfers between devices: 68.2 us -> 64.1 us
    all_to_all x6, waiting for transfers between devices: 32.8 us -> 76.7 us  [exchange(): return lax.all_to_all(parts, axes, 0, 0, tiled=True)]
    unnamed x71 -> x89, local copies, waits for them, and re-layouts: 7.89 us -> 18.5 us
    all_to_all x6, starting transfers between devices: 44.7 us -> 36.9 us  [exchange(): return lax.all_to_all(parts, axes, 0, 0, tiled=True)]
    pallas_call x1 -> x2, Pallas kernels: 8.13 us -> 15.9 us  [grad_in_terms(): call(grad_in_body, 'grad_in', (NY,), [pl.BlockSpec((2, t, f), lambda i, p...]
    convert_element_type x3 -> x1, other arithmetic: 7.08 us -> 0.01 us  [shards(): proj_gu = proj_gu.astype(BF16)]
    ppermute x15 -> x18, waiting for transfers between devices: 35.6 us -> 41.8 us  [step(): return lax.ppermute(array, axis, [(i, (i + shift) % n) for i in range(n)])]
    reduce_scatter x2 -> x1, waiting for transfers between devices: 4.95 us -> 0.02 us  [shards(): over_z = lax.psum_scatter(terms, 'z')]
    ppermute x15 -> x18, starting transfers between devices: 22.7 us -> 27 us  [step(): return lax.ppermute(array, axis, [(i, (i + shift) % n) for i in range(n)])]
  transfers between devices with their start and end apart: 27 -> 29, of which waited for: 14 -> 15; matrix products, arithmetic and copies ran while one was open for 8% -> 6% of each run, Pallas kernels for 11% -> 11%
where the time goes in v4:
time: 310 us; the launch traced here: 309 us
  waiting for transfers between devices  120 us (39%)
  starting transfers between devices  64.1 us (21%)
  Pallas kernels  58.6 us (19%)
  local copies, waits for them, and re-layouts  30.3 us (10%)
  between operations  14.6 us (5%)
  blocking collectives  12.3 us (4%)
  other arithmetic  6.54 us (2%)
    all_to_all x6, waiting for transfers between devices, exchange(): return lax.all_to_all(parts, axes, 0, 0, tiled=True)  76.7 us
    ppermute x18, waiting for transfers between devices, step(): return lax.ppermute(array, axis, [(i, (i + shift) % n) for i in range(n)])  41.8 us
    all_to_all x6, starting transfers between devices, exchange(): return lax.all_to_all(parts, axes, 0, 0, tiled=True)  36.9 us
    ppermute x18, starting transfers between devices, step(): return lax.ppermute(array, axis, [(i, (i + shift) % n) for i in range(n)])  27 us
    unnamed x89, local copies, waits for them, and re-layouts  18.5 us
    pallas_call x2, Pallas kernels, grad_in_terms(): call(grad_in_body, 'grad_in', (NY,), [pl.BlockSpec((2, t, f), lambda i, p...  15.9 us
    pallas_call x1, Pallas kernels, gate_up(): call(gate_up_body, 'gate_up', (NY,), [x_spec(t, w), x_spec(t, w), pl.Bloc...  13.5 us
    all_to_all x1, blocking collectives, exchange(): return lax.all_to_all(parts, axes, 0, 0, tiled=True)  12.3 us
  transfers between devices with their start and end apart: 29, of which 15 were waited for; matrix products, arithmetic and copies ran while one was open for 6% of the time, Pallas kernels for 11%

profile of v4, /device:TPU:2, one launch (start us, length us, event | category | flops | bytes accessed | tf_op | source)
XLA Modules:
  0.0 308.9 jit_solution(3198492256850171038)
XLA Ops:
  7.9 1.9 broadcast_in_dim.40
  9.8 8.5 %all-to-all-start.2 = ((bf16[8,192,256]{2,1,0:T(8,128)(2,1)}), bf16[8,192,256]{2,1,0:T(8,128)(2,1)S(1)}, u32[]{:S(2)}, u32[]{:S(2)}) async-start(bf16[8,192,256]{2,1,0:T(8,128)(2,1)} %broadcast_in_dim.40), calls=%async_computation.2 | async-start | bytes 1572864 | tf_op jit(solution)/shard_map/all_to_all | solution.py:308
  18.3 6.3 %merge_down.1 = (bf16[256,8192]{1,0:T(8,128)(2,1)}, f32[64,8,128]{2,1,0:T(8,128)S(1)}) custom-call(s32[4]{0:T(128)S(1)} %pad_add_fusion.pos_ref, bf16[512,8192]{1,0:T(8,128)(2,1)} %frozen_ref.1, bf16[32,512]{1,0:T(8,128)(2,1)S(1)} %bitcast.93, bf16[32,8192]{1,0:T(8,128)(2,1)S(1)} %copy-done.15), custom_call_target="tpu_custom_call" | custom-call | flops 1000000000 | bytes 16000000 | tf_op jit(solution)/shard_map/merge_down/pallas_call | solution.py:95
  25.4 16.0 %all-to-all-done.2.refs_0_ = bf16[8,192,256]{2,1,0:T(8,128)(2,1)S(1)} async-done(((bf16[8,192,256]{2,1,0:T(8,128)(2,1)}), bf16[8,192,256]{2,1,0:T(8,128)(2,1)S(1)}, u32[]{:S(2)}, u32[]{:S(2)}) %all-to-all-start.2) | async-done | bytes 786464 | tf_op jit(solution)/shard_map/all_to_all | solution.py:308
  41.4 0.9 copy-done.5
  42.3 1.6 collective-permute-start.10
  43.9 1.7 collective-permute-start.11
  45.5 17.7 %collective-permute-done.10.refs_0_ = bf16[8,192,256]{2,1,0:T(8,128)(2,1)S(1)} collective-permute-done((bf16[8,192,256]{2,1,0:T(8,128)(2,1)}, bf16[8,192,256]{2,1,0:T(8,128)(2,1)S(1)}, u32[]{:S(2)}, u32[]{:S(2)}) %collective-permute-start.10) | collective-permute-done | bytes 786464 | tf_op jit(solution)/shard_map/ppermute | solution.py:21
  63.7 3.0 collective-permute-start.13
  66.7 8.1 %collective-permute-done.12.refs_3_ = bf16[4,192,256]{2,1,0:T(8,128)(2,1)S(1)} collective-permute-done((bf16[4,192,256]{2,1,0:T(8,128)(2,1)S(1)}, bf16[4,192,256]{2,1,0:T(8,128)(2,1)S(1)}, u32[]{:S(2)}, u32[]{:S(2)}) %collective-permute-start.12) | collective-permute-done | bytes 393248 | tf_op jit(solution)/shard_map/ppermute | solution.py:21
  74.8 1.2 copy-done.6
  76.0 1.8 stack.54.own_ref
  78.3 2.7 collective-permute-start.1
  81.0 1.3 collective-permute-start.2
  82.3 2.0 collective-permute-done
  84.3 1.4 collective-permute-done.1
  85.7 1.9 collective-permute-done.2
  87.7 3.2 %collective-permute-start.5 = (bf16[4,192,256]{2,1,0:T(8,128)(2,1)S(1)}, bf16[4,192,256]{2,1,0:T(8,128)(2,1)S(1)}, u32[]{:S(2)}, u32[]{:S(2)}) collective-permute-start(bf16[4,192,256]{2,1,0:T(8,128)(2,1)S(1)} %pad_maximum_fusion.1.refs_3_), channel_id=1, source_target_pairs={{0,7},{1,0},{2,1},{3,2},{4,3},{5,4},{6,5},{7,6},{8,15},{9,8},{10,9... | collective-permute-start | bytes 1179656 | tf_op jit(solution)/shard_map/ppermute | solution.py:21
  91.7 7.8 %collective-permute-done.3.refs_1_.refs_2_ = bf16[4,192,256]{2,1,0:T(8,128)(2,1)S(1)} collective-permute-done((bf16[4,192,256]{2,1,0:T(8,128)(2,1)S(1)}, bf16[4,192,256]{2,1,0:T(8,128)(2,1)S(1)}, u32[]{:S(2)}, u32[]{:S(2)}) %collective-permute-start.3) | collective-permute-done | bytes 393248 | tf_op jit(solution)/shard_map/ppermute | solution.py:21
  100.2 0.8 copy-done.22
  101.0 5.2 %all-to-all-start = ((f32[64,8,128]{2,1,0:T(8,128)}), f32[64,8,128]{2,1,0:T(8,128)S(1)}, u32[]{:S(2)}, u32[]{:S(2)}) async-start(f32[64,8,128]{2,1,0:T(8,128)} %after.11), calls=%async_computation | async-start | bytes 524288 | tf_op jit(solution)/shard_map/all_to_all | solution.py:308
  106.2 1.6 collective-permute-start.4
  107.8 1.7 collective-permute-start.7
  109.5 11.1 %all-to-all-done = f32[64,8,128]{2,1,0:T(8,128)S(1)} async-done(((f32[64,8,128]{2,1,0:T(8,128)}), f32[64,8,128]{2,1,0:T(8,128)S(1)}, u32[]{:S(2)}, u32[]{:S(2)}) %all-to-all-start) | async-done | bytes 262176 | tf_op jit(solution)/shard_map/all_to_all | solution.py:308
  121.4 5.7 %all-to-all-start.1 = ((f32[64,8,128]{2,1,0:T(8,128)}), f32[64,8,128]{2,1,0:T(8,128)}, u32[]{:S(2)}, u32[]{:S(2)}) async-start(f32[64,8,128]{2,1,0:T(8,128)} %broadcast_in_dim_broadcast_in_dim_broadcast_in_dim.2), calls=%async_computation.1 | async-start | bytes 524288 | tf_op jit(solution)/shard_map/all_to_all | solution.py:308
  127.8 1.4 collective-permute-start.6
  130.0 1.9 collective-permute-start.8
  131.8 9.4 %all-to-all-done.1 = f32[64,8,128]{2,1,0:T(8,128)} async-done(((f32[64,8,128]{2,1,0:T(8,128)}), f32[64,8,128]{2,1,0:T(8,128)}, u32[]{:S(2)}, u32[]{:S(2)}) %all-to-all-start.1) | async-done | bytes 262176 | tf_op jit(solution)/shard_map/all_to_all | solution.py:308
  141.2 2.2 sqrt_reduce_fusion
  143.5 1.1 collective-permute-done.6.refs_0_
  145.3 1.6 slice.131
  147.7 1.6 slice.134
  149.3 3.2 %collective-permute-start.15 = (bf16[2,192,256]{2,1,0:T(8,128)(2,1)}, bf16[2,192,256]{2,1,0:T(8,128)(2,1)}, u32[]{:S(2)}, u32[]{:S(2)}) collective-permute-start(bf16[2,192,256]{2,1,0:T(8,128)(2,1)} %slice.134), channel_id=1, source_target_pairs={{0,7},{1,0},{2,1},{3,2},{4,3},{5,4},{6,5},{7,6},{8,15},{9,8},{10,9... | collective-permute-start | bytes 589832 | tf_op jit(solution)/shard_map/ppermute | solution.py:21
  152.6 0.7 copy-done.30
  153.3 13.5 %gate_up.1 = (bf16[2,8192,256]{2,1,0:T(8,128)(2,1)}, f32[2,384,256]{2,1,0:T(8,128)S(1)}, f32[2,8,256]{2,1,0:T(8,128)S(1)}) custom-call(s32[4]{0:T(128)S(1)} %pad_add_fusion.pos_ref, bf16[4,8,192,256]{3,2,1,0:T(8,128)(2,1)} %stack.54.own_ref, bf16[4,8,192,256]{3,2,1,0:T(8,128)(2,1)} %collective-permute-done.14.other_ref, ...), custom_call_target="tpu_custom_call" | custom-call | flops 1000000000 | bytes 16000000 | tf_op jit(solution)/shard_map/gate_up/pallas_call | solution.py:253
  168.1 1.0 copy-done.19
  169.1 1.0 copy-done.21
  170.1 1.0 copy-done.23
  171.1 1.0 copy-done.25
  172.1 1.0 copy-done.27
  173.1 0.9 copy-done.29
  174.1 2.8 stack.55._.own_ref
  177.0 5.2 %proj_gate_up.1._ = f32[384,64]{1,0:T(8,128)S(1)} custom-call(s32[4]{0:T(128)S(1)} %pad_add_fusion.pos_ref, bf16[4,8,192,256]{3,2,1,0:T(8,128)(2,1)} %stack.54.own_ref, bf16[4,8,192,256]{3,2,1,0:T(8,128)(2,1)} %collective-permute-done.14.other_ref, bf16[2,32,8192]{2,1,0:T(8,128)(2,1)S(1)} %bitcast.91, bf16[8,4,192,256]{3,2,1,0:T(8,128)(2,1)} %stack.55._.own_ref), custom_call_target="tpu_custom_call" | custom-call | flops 1000000000 | bytes 16000000 | tf_op jit(solution)/shard_map/proj_gate_up/pallas_call | solution.py:139
  182.9 7.2 %grad_act.1 = (f32[384,256]{1,0:T(8,128)S(1)}, f32[384,32]{1,0:T(8,128)S(1)}) custom-call(s32[4]{0:T(128)S(1)} %pad_add_fusion.pos_ref, bf16[8,4,192,256]{3,2,1,0:T(8,128)(2,1)} %stack.55._.own_ref, bf16[8,4,192,256]{3,2,1,0:T(8,128)(2,1)} %collective-permute-done.16.other_ref, f32[32,1,256]{2,1,0:T(1,128)S(1)} %div.15.scale_ref, ...), custom_call_target="tpu_custom_call" | custom-call | flops 1000000000 | bytes 16000000 | tf_op jit(solution)/shard_map/grad_act/pallas_call | solution.py:175
  190.8 7.7 %grad_in.2.refs_1_ = bf16[8,4,192,256]{3,2,1,0:T(8,128)(2,1)} custom-call(s32[4]{0:T(128)S(1)} %pad_add_fusion.pos_ref, bf16[2,384,256]{2,1,0:T(8,128)(2,1)S(1)} %get-tuple-element.24.grads_ref, bf16[2,8192,256]{2,1,0:T(8,128)(2,1)} %get-tuple-element.19.tile_ref), custom_call_target="tpu_custom_call" | custom-call | flops 1000000000 | bytes 16000000 | tf_op jit(solution)/shard_map/grad_in/pallas_call | solution.py:293
  198.9 1.3 convolution_multiply_fusion.1
  200.5 0.9 copy-done.8
  201.4 5.7 %dot_down.1 = f32[64,1,128]{2,1,0:T(1,128)S(1)} custom-call(s32[4]{0:T(128)S(1)} %pad_add_fusion.pos_ref, bf16[8,4,192,256]{3,2,1,0:T(8,128)(2,1)S(1)} %copy-done.1, bf16[8,4,192,256]{3,2,1,0:T(8,128)(2,1)} %collective-permute-done.16.other_ref, bf16[384,256]{1,0:T(8,128)(2,1)S(1)} %copy-done.8, bf16[256,8192]{1,0:T(8,128)(2,1)} %get-tuple-element.16.tile_ref), custom_call_target="tpu_custom_call" | custom-call | flops 1000000000 | bytes 16000000 | tf_op jit(solution)/shard_map/dot_down/pallas_call | solution.py:209
  209.1 1.0 copy-done.4
  210.1 8.2 %grad_in.3.refs_1_ = bf16[8,4,192,256]{3,2,1,0:T(8,128)(2,1)} custom-call(s32[4]{0:T(128)S(1)} %pad_add_fusion.pos_ref, bf16[2,384,256]{2,1,0:T(8,128)(2,1)S(1)} %copy-done.4, bf16[2,8192,256]{2,1,0:T(8,128)(2,1)} %get-tuple-element.19.tile_ref, bf16[8,4,192,256]{3,2,1,0:T(8,128)(2,1)} %after.19.refs_0_), custom_call_target="tpu_custom_call" | custom-call | flops 1000000000 | bytes 16000000 | tf_op jit(solution)/shard_map/grad_in/pallas_call | solution.py:293
  218.4 8.2 %all-to-all-start.3 = ((f32[64,8,128]{2,1,0:T(8,128)}), f32[64,8,128]{2,1,0:T(8,128)S(1)}, u32[]{:S(2)}, u32[]{:S(2)}) async-start(f32[64,8,128]{2,1,0:T(8,128)} %after.20), calls=%async_computation.4 | async-start | bytes 524288 | tf_op jit(solution)/shard_map/all_to_all | solution.py:308
  226.7 16.0 %all-to-all-done.3 = f32[64,8,128]{2,1,0:T(8,128)S(1)} async-done(((f32[64,8,128]{2,1,0:T(8,128)}), f32[64,8,128]{2,1,0:T(8,128)S(1)}, u32[]{:S(2)}, u32[]{:S(2)}) %all-to-all-start.3) | async-done | bytes 262176 | tf_op jit(solution)/shard_map/all_to_all | solution.py:308
  242.7 0.8 maximum_maximum_fusion
  243.5 4.6 %all-to-all-start.4 = ((f32[64,8,128]{2,1,0:T(8,128)}), f32[64,8,128]{2,1,0:T(8,128)S(1)}, u32[]{:S(2)}, u32[]{:S(2)}) async-start(f32[64,8,128]{2,1,0:T(8,128)} %maximum_maximum_fusion), calls=%async_computation.5 | async-start | bytes 524288 | tf_op jit(solution)/shard_map/all_to_all | solution.py:308
  248.6 16.8 %all-to-all-done.4 = f32[64,8,128]{2,1,0:T(8,128)S(1)} async-done(((f32[64,8,128]{2,1,0:T(8,128)}), f32[64,8,128]{2,1,0:T(8,128)S(1)}, u32[]{:S(2)}, u32[]{:S(2)}) %all-to-all-start.4) | async-done | bytes 262176 | tf_op jit(solution)/shard_map/all_to_all | solution.py:308
  266.1 12.3 %all_to_all.35 = f32[8,48,256]{2,1,0:T(8,128)S(1)} all-to-all(f32[8,48,256]{2,1,0:T(8,128)S(1)} %bitcast.103), channel_id=1, replica_groups=mesh['x'=4,'core'=2,'y'=4,'z'=8] {'x','core'}, dimensions={0} | all-to-all | bytes 786432 | tf_op jit(solution)/shard_map/all_to_all | solution.py:308
  278.5 0.8 broadcast_in_dim.46
  279.3 4.8 %all-to-all-start.6 = ((f32[8,48,256]{2,1,0:T(8,128)}), f32[8,48,256]{2,1,0:T(8,128)S(1)}, u32[]{:S(2)}, u32[]{:S(2)}) async-start(f32[8,48,256]{2,1,0:T(8,128)} %broadcast_in_dim.46), calls=%async_computation.7 | async-start | bytes 786432 | tf_op jit(solution)/shard_map/all_to_all | solution.py:308
  284.1 7.5 %all-to-all-done.6 = f32[8,48,256]{2,1,0:T(8,128)S(1)} async-done(((f32[8,48,256]{2,1,0:T(8,128)}), f32[8,48,256]{2,1,0:T(8,128)S(1)}, u32[]{:S(2)}, u32[]{:S(2)}) %all-to-all-start.6) | async-done | bytes 393248 | tf_op jit(solution)/shard_map/all_to_all | solution.py:308
  291.7 1.2 fusion.2
  292.9 1.0 collective-permute-start.18
  293.9 1.1 collective-permute-start.19
  297.6 0.8 reshape.131
  299.6 1.8 collective-permute-done.19
  (171 shorter events, 19.2 us)
Async XLA Ops:
  7.2 145.4 %copy-start = (bf16[2,32,512]{2,1,0:T(8,128)(2,1)S(1)}, bf16[2,32,512]{2,1,0:T(8,128)(2,1)}, u32[]{:S(2)}) copy-start(bf16[2,32,512]{2,1,0:T(8,128)(2,1)} %param.14) | copy-start | bytes 196612
  7.2 11.1 %copy-start.32 = (bf16[512,32]{0,1:T(8,128)(2,1)S(1)}, bf16[512,32]{0,1:T(8,128)(2,1)}, u32[]{:S(2)}) copy-start(bf16[512,32]{0,1:T(8,128)(2,1)} %param.17) | copy-start | bytes 98308
  7.2 11.1 %copy-start.15 = (bf16[32,8192]{1,0:T(8,128)(2,1)S(1)}, bf16[32,8192]{1,0:T(8,128)(2,1)}, u32[]{:S(2)}) copy-start(bf16[32,8192]{1,0:T(8,128)(2,1)} %right_ref.3) | copy-start | bytes 1572868
  7.2 145.3 %all-gather.2.cloned.1.call-start = ((), (), s32[]{:S(2)}) async-start(), calls=%async_computation.8 | async-start | bytes 18874368 | tf_op jit(solution)/shard_map/all_gather | solution.py:339
  9.8 31.6 %all-to-all-start.2 = ((bf16[8,192,256]{2,1,0:T(8,128)(2,1)}), bf16[8,192,256]{2,1,0:T(8,128)(2,1)S(1)}, u32[]{:S(2)}, u32[]{:S(2)}) async-start(bf16[8,192,256]{2,1,0:T(8,128)(2,1)} %broadcast_in_dim.40), calls=%async_computation.2 | async-start | bytes 1572864 | tf_op jit(solution)/shard_map/all_to_all | solution.py:308
  41.4 0.9 copy-start.5
  42.3 20.9 %collective-permute-start.10 = (bf16[8,192,256]{2,1,0:T(8,128)(2,1)}, bf16[8,192,256]{2,1,0:T(8,128)(2,1)S(1)}, u32[]{:S(2)}, u32[]{:S(2)}) collective-permute-start(bf16[8,192,256]{2,1,0:T(8,128)(2,1)} %after.16.refs_1_), channel_id=1, source_target_pairs={{0,8},{8,16},{16,24},{24,0},{1,9},{9,17},{17,25},{25,1},{2,10},{10... | collective-permute-start | bytes 2359304 | tf_op jit(solution)/shard_map/ppermute | solution.py:21
  43.9 19.8 %collective-permute-start.11 = (bf16[8,192,256]{2,1,0:T(8,128)(2,1)}, bf16[8,192,256]{2,1,0:T(8,128)(2,1)S(1)}, u32[]{:S(2)}, u32[]{:S(2)}) collective-permute-start(bf16[8,192,256]{2,1,0:T(8,128)(2,1)} %after.16.refs_1_), channel_id=1, source_target_pairs={{0,24},{8,0},{16,8},{24,16},{1,25},{9,1},{17,9},{25,17},{2,26},{10... | collective-permute-start | bytes 2359304 | tf_op jit(solution)/shard_map/ppermute | solution.py:21
  63.2 11.5 %collective-permute-start.12 = (bf16[4,192,256]{2,1,0:T(8,128)(2,1)S(1)}, bf16[4,192,256]{2,1,0:T(8,128)(2,1)S(1)}, u32[]{:S(2)}, u32[]{:S(2)}) collective-permute-start(bf16[4,192,256]{2,1,0:T(8,128)(2,1)S(1)} %slice.132), channel_id=1, source_target_pairs={{0,8},{8,16},{16,24},{24,0},{1,9},{9,17},{17,25},{25,1},{2,10},{10... | collective-permute-start | bytes 1179656 | tf_op jit(solution)/shard_map/ppermute | solution.py:21
  63.6 14.2 %copy-start.37 = (bf16[192,256]{1,0:T(8,128)(2,1)S(1)}, bf16[192,256]{1,0:T(8,128)(2,1)}, u32[]{:S(2)}) copy-start(bf16[192,256]{1,0:T(8,128)(2,1)} %param.11) | copy-start | bytes 294916
  63.7 11.1 %collective-permute-start.13 = (bf16[4,192,256]{2,1,0:T(8,128)(2,1)S(1)}, bf16[4,192,256]{2,1,0:T(8,128)(2,1)S(1)}, u32[]{:S(2)}, u32[]{:S(2)}) collective-permute-start(bf16[4,192,256]{2,1,0:T(8,128)(2,1)S(1)} %slice.133), channel_id=1, source_target_pairs={{0,24},{8,0},{16,8},{24,16},{1,25},{9,1},{17,9},{25,17},{2,26},{10... | collective-permute-start | bytes 1179656 | tf_op jit(solution)/shard_map/ppermute | solution.py:21
  74.8 1.2 copy-start.6
  77.8 74.7 %collective-permute-start.14 = (bf16[4,8,192,256]{3,2,1,0:T(8,128)(2,1)}, bf16[4,8,192,256]{3,2,1,0:T(8,128)(2,1)}, u32[]{:S(2)}, u32[]{:S(2)}) collective-permute-start(bf16[4,8,192,256]{3,2,1,0:T(8,128)(2,1)} %stack.54.own_ref), channel_id=1, source_target_pairs={{0,32},{32,0},{1,33},{33,1},{2,34},{34,2},{3,35},{35,3},{4,36},{36... | collective-permute-start | bytes 9437192 | tf_op jit(solution)/shard_map/ppermute | solution.py:357
  77.8 6.5 %collective-permute-start = (bf16[192,256]{1,0:T(8,128)(2,1)S(1)}, bf16[192,256]{1,0:T(8,128)(2,1)S(1)}, u32[]{:S(2)}, u32[]{:S(2)}) collective-permute-start(bf16[192,256]{1,0:T(8,128)(2,1)S(1)} %copy-done.37), channel_id=1, source_target_pairs={{0,8},{8,16},{16,24},{24,0},{1,9},{9,17},{17,25},{25,1},{2,10},{10... | collective-permute-start | bytes 294920 | tf_op jit(solution)/shard_map/ppermute | solution.py:21
  78.3 7.4 %collective-permute-start.1 = (bf16[192,256]{1,0:T(8,128)(2,1)S(1)}, bf16[192,256]{1,0:T(8,128)(2,1)S(1)}, u32[]{:S(2)}, u32[]{:S(2)}) collective-permute-start(bf16[192,256]{1,0:T(8,128)(2,1)S(1)} %copy-done.37), channel_id=1, source_target_pairs={{0,24},{8,0},{16,8},{24,16},{1,25},{9,1},{17,9},{25,17},{2,26},{10... | collective-permute-start | bytes 294920 | tf_op jit(solution)/shard_map/ppermute | solution.py:21
  81.0 6.6 %collective-permute-start.2 = (bf16[192,256]{1,0:T(8,128)(2,1)S(1)}, bf16[192,256]{1,0:T(8,128)(2,1)S(1)}, u32[]{:S(2)}, u32[]{:S(2)}) collective-permute-start(bf16[192,256]{1,0:T(8,128)(2,1)S(1)} %copy-done.37), channel_id=1, source_target_pairs={{0,16},{8,24},{16,0},{24,8},{1,17},{9,25},{17,1},{25,9},{2,18},{10... | collective-permute-start | bytes 294920 | tf_op jit(solution)/shard_map/ppermute | solution.py:21
  87.7 11.8 %collective-permute-start.3 = (bf16[4,192,256]{2,1,0:T(8,128)(2,1)S(1)}, bf16[4,192,256]{2,1,0:T(8,128)(2,1)S(1)}, u32[]{:S(2)}, u32[]{:S(2)}) collective-permute-start(bf16[4,192,256]{2,1,0:T(8,128)(2,1)S(1)} %pad_maximum_fusion.1.refs_3_), channel_id=1, source_target_pairs={{0,1},{1,2},{2,3},{3,4},{4,5},{5,6},{6,7},{7,0},{8,9},{9,10},{10,1... | collective-permute-start | bytes 1179656 | tf_op jit(solution)/shard_map/ppermute | solution.py:21
  87.7 11.7 %collective-permute-start.5 = (bf16[4,192,256]{2,1,0:T(8,128)(2,1)S(1)}, bf16[4,192,256]{2,1,0:T(8,128)(2,1)S(1)}, u32[]{:S(2)}, u32[]{:S(2)}) collective-permute-start(bf16[4,192,256]{2,1,0:T(8,128)(2,1)S(1)} %pad_maximum_fusion.1.refs_3_), channel_id=1, source_target_pairs={{0,7},{1,0},{2,1},{3,2},{4,3},{5,4},{6,5},{7,6},{8,15},{9,8},{10,9... | collective-permute-start | bytes 1179656 | tf_op jit(solution)/shard_map/ppermute | solution.py:21
  100.2 0.8 copy-start.22
  101.0 51.6 %copy-start.9 = (bf16[2,8192,32]{1,2,0:T(8,128)(2,1)S(1)}, bf16[2,8192,32]{1,2,0:T(8,128)(2,1)}, u32[]{:S(2)}) copy-start(bf16[2,8192,32]{1,2,0:T(8,128)(2,1)} %param.13) | copy-start | bytes 3145732
  101.0 19.5 %all-to-all-start = ((f32[64,8,128]{2,1,0:T(8,128)}), f32[64,8,128]{2,1,0:T(8,128)S(1)}, u32[]{:S(2)}, u32[]{:S(2)}) async-start(f32[64,8,128]{2,1,0:T(8,128)} %after.11), calls=%async_computation | async-start | bytes 524288 | tf_op jit(solution)/shard_map/all_to_all | solution.py:308
  106.2 20.9 %collective-permute-start.4 = (bf16[4,192,256]{2,1,0:T(8,128)(2,1)}, bf16[4,192,256]{2,1,0:T(8,128)(2,1)S(1)}, u32[]{:S(2)}, u32[]{:S(2)}) collective-permute-start(bf16[4,192,256]{2,1,0:T(8,128)(2,1)} %copy-done.20), channel_id=1, source_target_pairs={{0,1},{1,2},{2,3},{3,4},{4,5},{5,6},{6,7},{7,0},{8,9},{9,10},{10,1... | collective-permute-start | bytes 1179656 | tf_op jit(solution)/shard_map/ppermute | solution.py:21
  107.8 21.4 %collective-permute-start.7 = (bf16[4,192,256]{2,1,0:T(8,128)(2,1)}, bf16[4,192,256]{2,1,0:T(8,128)(2,1)S(1)}, u32[]{:S(2)}, u32[]{:S(2)}) collective-permute-start(bf16[4,192,256]{2,1,0:T(8,128)(2,1)} %copy-done.22), channel_id=1, source_target_pairs={{0,7},{1,0},{2,1},{3,2},{4,3},{5,4},{6,5},{7,6},{8,15},{9,8},{10,9... | collective-permute-start | bytes 1179656 | tf_op jit(solution)/shard_map/ppermute | solution.py:21
  120.6 6.5 %copy-start.42 = (f32[128]{0:T(128)}, f32[128]{0:T(128)S(1)}, u32[]{:S(2)}) copy-start(f32[128]{0:T(128)S(1)} %reduce_sum.58) | copy-start | bytes 1540
  121.4 19.9 %all-to-all-start.1 = ((f32[64,8,128]{2,1,0:T(8,128)}), f32[64,8,128]{2,1,0:T(8,128)}, u32[]{:S(2)}, u32[]{:S(2)}) async-start(f32[64,8,128]{2,1,0:T(8,128)} %broadcast_in_dim_broadcast_in_dim_broadcast_in_dim.2), calls=%async_computation.1 | async-start | bytes 524288 | tf_op jit(solution)/shard_map/all_to_all | solution.py:308
  127.0 164.6 %reduce-scatter.2.cloned.1.call-start = ((), (), s32[]{:S(2)}) async-start(), calls=%async_computation.9 | async-start | bytes 3538944 | tf_op jit(solution)/shard_map/reduce_scatter | solution.py:396
  127.8 16.7 %collective-permute-start.6 = (bf16[4,192,256]{2,1,0:T(8,128)(2,1)}, bf16[4,192,256]{2,1,0:T(8,128)(2,1)S(1)}, u32[]{:S(2)}, u32[]{:S(2)}) collective-permute-start(bf16[4,192,256]{2,1,0:T(8,128)(2,1)} %after.12.refs_1_), channel_id=1, source_target_pairs={{0,1},{1,2},{2,3},{3,4},{4,5},{5,6},{6,7},{7,0},{8,9},{9,10},{10,1... | collective-permute-start | bytes 1179656 | tf_op jit(solution)/shard_map/ppermute | solution.py:21
  130.0 16.9 %collective-permute-start.8 = (bf16[4,192,256]{2,1,0:T(8,128)(2,1)}, bf16[4,192,256]{2,1,0:T(8,128)(2,1)S(1)}, u32[]{:S(2)}, u32[]{:S(2)}) collective-permute-start(bf16[4,192,256]{2,1,0:T(8,128)(2,1)} %after.14.refs_5_), channel_id=1, source_target_pairs={{0,7},{1,0},{2,1},{3,2},{4,3},{5,4},{6,5},{7,6},{8,15},{9,8},{10,9... | collective-permute-start | bytes 1179656 | tf_op jit(solution)/shard_map/ppermute | solution.py:21
  146.9 20.6 %collective-permute-start.9 = (bf16[2,192,256]{2,1,0:T(8,128)(2,1)}, bf16[2,192,256]{2,1,0:T(8,128)(2,1)S(1)}, u32[]{:S(2)}, u32[]{:S(2)}) collective-permute-start(bf16[2,192,256]{2,1,0:T(8,128)(2,1)} %slice.131), channel_id=1, source_target_pairs={{0,1},{1,2},{2,3},{3,4},{4,5},{5,6},{6,7},{7,0},{8,9},{9,10},{10,1... | collective-permute-start | bytes 589832 | tf_op jit(solution)/shard_map/ppermute | solution.py:21
  146.9 0.8 copy-start.12
  149.3 18.8 %collective-permute-start.15 = (bf16[2,192,256]{2,1,0:T(8,128)(2,1)}, bf16[2,192,256]{2,1,0:T(8,128)(2,1)}, u32[]{:S(2)}, u32[]{:S(2)}) collective-permute-start(bf16[2,192,256]{2,1,0:T(8,128)(2,1)} %slice.134), channel_id=1, source_target_pairs={{0,7},{1,0},{2,1},{3,2},{4,3},{5,4},{6,5},{7,6},{8,15},{9,8},{10,9... | collective-permute-start | bytes 589832 | tf_op jit(solution)/shard_map/ppermute | solution.py:21
  152.6 0.8 copy-start.30
  153.3 14.8 %copy-start.11 = (bf16[4,192,256]{2,1,0:T(8,128)(2,1)S(1)}, bf16[4,192,256]{2,1,0:T(8,128)(2,1)}, u32[]{:S(2)}) copy-start(bf16[4,192,256]{2,1,0:T(8,128)(2,1)} %after.13.refs_0_) | copy-start | bytes 1179652
  153.3 14.8 %copy-start.13 = (bf16[4,192,256]{2,1,0:T(8,128)(2,1)S(1)}, bf16[4,192,256]{2,1,0:T(8,128)(2,1)}, u32[]{:S(2)}) copy-start(bf16[4,192,256]{2,1,0:T(8,128)(2,1)} %after.15.refs_6_) | copy-start | bytes 1179652
  168.1 1.0 copy-start.19
  169.1 1.0 copy-start.21
  170.1 1.0 copy-start.23
  171.1 1.0 copy-start.25
  172.1 1.0 copy-start.27
  173.1 0.9 copy-start.29
  174.0 2.8 copy-start.41
  174.1 2.9 copy-start.34
  176.9 6.0 %collective-permute-start.16 = (bf16[8,4,192,256]{3,2,1,0:T(8,128)(2,1)}, bf16[8,4,192,256]{3,2,1,0:T(8,128)(2,1)}, u32[]{:S(2)}, u32[]{:S(2)}) collective-permute-start(bf16[8,4,192,256]{3,2,1,0:T(8,128)(2,1)} %stack.55._.own_ref), channel_id=1, source_target_pairs={{0,32},{32,0},{1,33},{33,1},{2,34},{34,2},{3,35},{35,3},{4,36},{36... | collective-permute-start | bytes 9437192 | tf_op jit(solution)/shard_map/ppermute | solution.py:366
  176.9 5.3 %copy-start.43 = (f32[2,512]{1,0:T(2,128)S(1)}, f32[2,512]{1,0:T(2,128)}, u32[]{:S(2)}) copy-start(f32[2,512]{1,0:T(2,128)} %param.15) | copy-start | bytes 12292
  182.2 7.9 %copy-start.16 = (f32[384,64]{1,0:T(8,128)}, f32[384,64]{1,0:T(8,128)S(1)}, u32[]{:S(2)}) copy-start(f32[384,64]{1,0:T(8,128)S(1)} %proj_gate_up.1._) | copy-start | bytes 294916
  190.4 8.5 %copy-start.7 = (bf16[384,256]{1,0:T(8,128)(2,1)}, bf16[384,256]{1,0:T(8,128)(2,1)S(1)}, u32[]{:S(2)}) copy-start(bf16[384,256]{1,0:T(8,128)(2,1)S(1)} %get-tuple-element.25.refs_0_) | copy-start | bytes 589828
  190.5 7.9 %copy-start.2 = (bf16[2,384,256]{2,1,0:T(8,128)(2,1)}, bf16[2,384,256]{2,1,0:T(8,128)(2,1)S(1)}, u32[]{:S(2)}) copy-start(bf16[2,384,256]{2,1,0:T(8,128)(2,1)S(1)} %get-tuple-element.24.grads_ref) | copy-start | bytes 1179652
  198.5 2.0 copy-start.1
  198.5 10.6 %collective-permute-start.17 = (bf16[8,4,192,256]{3,2,1,0:T(8,128)(2,1)}, bf16[8,4,192,256]{3,2,1,0:T(8,128)(2,1)}, u32[]{:S(2)}, u32[]{:S(2)}) collective-permute-start(bf16[8,4,192,256]{3,2,1,0:T(8,128)(2,1)} %grad_in.2.refs_1_), channel_id=1, source_target_pairs={{0,32},{32,0},{1,33},{33,1},{2,34},{34,2},{3,35},{35,3},{4,36},{36... | collective-permute-start | bytes 9437192 | tf_op jit(solution)/shard_map/ppermute | solution.py:383
  200.5 0.9 copy-start.8
  201.4 6.3 %copy-start.3 = (bf16[2,384,256]{2,1,0:T(8,128)(2,1)S(1)}, bf16[2,384,256]{2,1,0:T(8,128)(2,1)}, u32[]{:S(2)}) copy-start(bf16[2,384,256]{2,1,0:T(8,128)(2,1)} %copy-done.2) | copy-start | bytes 1179652
  209.1 1.0 copy-start.4
  218.3 8.3 %copy-start.17 = (f32[384,64]{1,0:T(8,128)S(1)}, f32[384,64]{1,0:T(8,128)}, u32[]{:S(2)}) copy-start(f32[384,64]{1,0:T(8,128)} %copy-done.16) | copy-start | bytes 294916
  218.3 24.4 %copy-start.39 = (f32[32,2,1,128]{3,0,1,2:T(8,128)S(1)}, f32[32,2,1,128]{3,0,1,2:T(8,128)}, u32[]{:S(2)}) copy-start(f32[32,2,1,128]{3,0,1,2:T(8,128)} %copy.35) | copy-start | bytes 98308
  218.4 47.2 %copy-start.36 = (bf16[192,256]{1,0:T(8,128)(2,1)S(1)}, bf16[192,256]{1,0:T(8,128)(2,1)}, u32[]{:S(2)}) copy-start(bf16[192,256]{1,0:T(8,128)(2,1)} %param.10) | copy-start | bytes 294916
  218.4 47.4 %copy-start.38 = (bf16[192,256]{1,0:T(8,128)(2,1)S(1)}, bf16[192,256]{1,0:T(8,128)(2,1)}, u32[]{:S(2)}) copy-start(bf16[192,256]{1,0:T(8,128)(2,1)} %param.11) | copy-start | bytes 294916
  218.4 24.2 %all-to-all-start.3 = ((f32[64,8,128]{2,1,0:T(8,128)}), f32[64,8,128]{2,1,0:T(8,128)S(1)}, u32[]{:S(2)}, u32[]{:S(2)}) async-start(f32[64,8,128]{2,1,0:T(8,128)} %after.20), calls=%async_computation.4 | async-start | bytes 524288 | tf_op jit(solution)/shard_map/all_to_all | solution.py:308
  226.7 57.4 %copy-start.40 = (f32[64,128]{1,0:T(8,128)S(1)}, f32[64,128]{1,0:T(8,128)}, u32[]{:S(2)}) copy-start(f32[64,128]{1,0:T(8,128)} %get-tuple-element.29) | copy-start | bytes 98308
  243.5 21.9 %all-to-all-start.4 = ((f32[64,8,128]{2,1,0:T(8,128)}), f32[64,8,128]{2,1,0:T(8,128)S(1)}, u32[]{:S(2)}, u32[]{:S(2)}) async-start(f32[64,8,128]{2,1,0:T(8,128)} %maximum_maximum_fusion), calls=%async_computation.5 | async-start | bytes 524288 | tf_op jit(solution)/shard_map/all_to_all | solution.py:308
  278.5 13.2 %copy-start.35 = (f32[48,256]{1,0:T(8,128)}, f32[48,256]{1,0:T(8,128)S(1)}, u32[]{:S(2)}) copy-start(f32[48,256]{1,0:T(8,128)S(1)} %reduce_sum.63.refs_1_) | copy-start | bytes 147460
  279.3 12.3 %all-to-all-start.6 = ((f32[8,48,256]{2,1,0:T(8,128)}), f32[8,48,256]{2,1,0:T(8,128)S(1)}, u32[]{:S(2)}, u32[]{:S(2)}) async-start(f32[8,48,256]{2,1,0:T(8,128)} %broadcast_in_dim.46), calls=%async_computation.7 | async-start | bytes 786432 | tf_op jit(solution)/shard_map/all_to_all | solution.py:308
  292.9 6.7 %collective-permute-start.18 = (bf16[192,256]{1,0:T(8,128)(2,1)S(1)}, bf16[192,256]{1,0:T(8,128)(2,1)S(1)}, u32[]{:S(2)}, u32[]{:S(2)}) collective-permute-start(bf16[192,256]{1,0:T(8,128)(2,1)S(1)} %get-tuple-element.26), channel_id=1, source_target_pairs={{0,24},{8,0},{16,8},{24,16},{1,25},{9,1},{17,9},{25,17},{2,26},{10... | collective-permute-start | bytes 294920 | tf_op jit(solution)/shard_map/ppermute | solution.py:21
  293.9 7.5 %collective-permute-start.19 = (bf16[192,256]{1,0:T(8,128)(2,1)S(1)}, bf16[192,256]{1,0:T(8,128)(2,1)S(1)}, u32[]{:S(2)}, u32[]{:S(2)}) collective-permute-start(bf16[192,256]{1,0:T(8,128)(2,1)S(1)} %get-tuple-element.27), channel_id=1, source_target_pairs={{0,8},{8,16},{16,24},{24,0},{1,9},{9,17},{17,25},{25,1},{2,10},{10... | collective-permute-start | bytes 294920 | tf_op jit(solution)/shard_map/ppermute | solution.py:21
  295.0 6.4 %collective-permute-start.20 = (bf16[192,256]{1,0:T(8,128)(2,1)S(1)}, bf16[192,256]{1,0:T(8,128)(2,1)S(1)}, u32[]{:S(2)}, u32[]{:S(2)}) collective-permute-start(bf16[192,256]{1,0:T(8,128)(2,1)S(1)} %get-tuple-element.28), channel_id=1, source_target_pairs={{0,16},{8,24},{16,0},{24,8},{1,17},{9,25},{17,1},{25,9},{2,18},{10... | collective-permute-start | bytes 294920 | tf_op jit(solution)/shard_map/ppermute | solution.py:21
  (9 other events, 6.4 us)
Sparse Core Ops, SparseCore 0:
  9.9 90.0 all-gather.1
  218.5 54.0 reduce-scatter.1

commit v5 on v4

--- a/solution.py
+++ b/solution.py
@@ -275,33 +275,32 @@
     )(pos, own, other, frozen, left, right, before)
 
 
-def grad_in_body(pos_ref, grads_ref, tile_ref, *refs):
-    *from_ref, out_ref = refs
+def grad_in_body(pos_ref, grads_ref, tile_ref, own_ref, other_ref):
+    t = grads_ref.shape[1] // 2
     for i in range(NZ):
         rows = slice(i * 256, (i + 1) * 256)
         out = lax.dot_general(grads_ref[0], tile_ref[0, rows], NT, preferred_element_type=F32)
         out += lax.dot_general(grads_ref[1], tile_ref[1, rows], NT, preferred_element_type=F32)
-        if from_ref:
-            out += from_ref[0][i, 0].astype(F32)
-        out_ref[i, 0] = out.astype(BF16)
-
-
-def grad_in_terms(pos, grads, tiles, half, *from_other):
+        out = out.astype(BF16)
+        own_ref[i, 0] = out[:t]
+        other_ref[i, 0] = out[t:]
+
+
+def grad_in_parts(pos, grads, tiles):
     _, t, f = grads.shape
-    t = t // 2
-    out = pl.BlockSpec((NZ, 1, t, 256), lambda i, p: (0, i, 0, 0))
+    out = pl.BlockSpec((NZ, 1, t // 2, 256), lambda i, p: (0, i, 0, 0))
+    shape = jax.ShapeDtypeStruct((NZ, NY, t // 2, 256), BF16)
     return call(
         grad_in_body,
         "grad_in",
         (NY,),
         [
-            pl.BlockSpec((2, t, f), lambda i, p: (0, half, 0)),
+            pl.BlockSpec((2, t, f), lambda i, p: (0, 0, 0)),
             pl.BlockSpec((2, NZ * 256, f), lambda i, p: (0, i, 0)),
-        ]
-        + [out] * len(from_other),
-        out,
-        jax.ShapeDtypeStruct((NZ, NY, t, 256), BF16),
-    )(pos, grads, tiles, *from_other)
+        ],
+        [out, out],
+        [shape, shape],
+    )(pos, grads, tiles)
 
 
 def exchange(parts, axes):
@@ -354,7 +353,9 @@
     r3, l3 = both_ways(r2, l2, "z", NZ)
     r3, l3 = after(r3, down_sums), after(l3, down_sums)
     zfr, zfl = both_ways(r3[: NY // 2], l3[NY // 2 :], "z", NZ)
+    g_own = stack([r3, r2, r1, g_y, l1, l2, l3], zfr, zfl)
     x_other = lax.ppermute(x_own, "core", OTHER)
+    g_other = lax.ppermute(g_own, "core", OTHER)
     right = half_of(right_gu, ic, 2)
     left_t = left_gu.swapaxes(1, 2)
 
@@ -362,11 +363,7 @@
     scale_down = magnitude_down.reshape(NMP, 1, width) / norm_down
 
     tiles, pre_gu, squares = gate_up(pos, x_own, x_other, frozen_full, left_t, right, down_sums)
-    g_own = stack([r3, r2, r1, g_y, l1, l2, l3], after(zfr, squares), zfl)
-    g_other = lax.ppermute(g_own, "core", OTHER)
-    proj_gu = proj_gate_up(pos, x_own, x_other, left_t, g_own)
-    grad_act, rows_down = grad_act_rows(pos, g_own, g_other, scale_down, tile_down, right_down, proj_gu)
-    proj_gu = proj_gu.astype(BF16)
+    grad_act, rows_down = grad_act_rows(pos, g_own, g_other, scale_down, tile_down, right_down, squares)
     norm_gu = jnp.sqrt(jnp.sum(squares, axis=1) + 1e-06)
     scale_gu = half_of(magnitude_gu, ic, 1) / norm_gu
     hid_gu = pre_gu * scale_gu[:, None, :]
@@ -379,7 +376,7 @@
     dot_gu = jnp.sum(grad_hid * pre_gu, axis=1) / norm_gu
     pre_grads = (grad_hid * scale_gu[:, None, :]).astype(BF16)
 
-    other_terms = grad_in_terms(pos, pre_grads, tiles, 1)
+    own_terms, other_terms = grad_in_parts(pos, pre_grads, tiles)
     from_other = lax.ppermute(other_terms, "core", OTHER)
 
     rows_gu = [
@@ -390,13 +387,16 @@
     rows = rows.reshape(NC, NMP, tokens // NMP, 128)
     rows = jnp.where(ic == 0, rows, rows[::-1]).reshape(NC * NMP, tokens // NMP, 128)
     rows = jnp.pad(rows, ((0, 0), (0, 2), (0, 0)))
-    dots = dot_down_sums(pos, g_own, g_other, after(act, other_terms), tile_down).reshape(NMP, NC, 1, 128)
+    from_other = after(from_other, rows)
+    terms = (own_terms.astype(F32) + from_other.astype(F32)).astype(BF16)
+    over_z = lax.psum_scatter(terms, "z")
+    rows = sum_parts(rows, CMP)
+    dots = dot_down_sums(pos, g_own, g_other, act, tile_down).reshape(NMP, NC, 1, 128)
     dots = dots.swapaxes(0, 1).reshape(NC * NMP, 1, 128)
-    terms = grad_in_terms(pos, pre_grads, tiles, 0, after(from_other, rows, dots))
-    over_z = lax.psum_scatter(terms, "z")
-    rows = sum_parts(after(rows, terms), CMP)
+    rows_sum = rows
     rows = jnp.broadcast_to(rows[None, :6], (NC * NMP, 6, 128))
     rows = exchange(jnp.concatenate([rows, dots, jnp.zeros_like(dots)], axis=1), CMP)
+    proj_gu = proj_gate_up(pos, x_own, x_other, left_t, rows_sum).astype(BF16)
     right_gu_parts = [
         lax.dot_general(proj_gu[:, 32 * k : 32 * k + 32], pre_grads[k], TN, preferred_element_type=F32)
         for k in range(2)
@@ -420,12 +420,10 @@
         [2.0 * left_gu_part, 2.0 * right_down_part, jnp.pad(dots, ((0, 31), (0, 0)))] + cores
     )
     sums = sum_parts(sums.reshape(NDP, 48, width), DP)
-    over_z = after(over_z, sums)
-    over_z = jnp.roll(over_z, 1 - iy, 0)
-    grad_in = over_z[1].astype(F32)
-    for p in (0, 2, 3):
-        grad_in += step(over_z[p], "y", NY, p - 1).astype(F32)
-    sums = gather_small(sums, DP, NDP).reshape(384, width)
+    over_z = jnp.roll(after(over_z, sums), 1 - iy, 0)
+    sent = [step(over_z[p], "y", NY, p - 1) for p in (0, 2, 3)]
+    grad_in = over_z[1].astype(F32) + sum(r.astype(F32) for r in sent)
+    sums = after(gather_small(sums, DP, NDP), *sent).reshape(384, width)
     cores = sums[128:].reshape(NC, 128, hidden).swapaxes(0, 1).reshape(128, NC * hidden)
     return (
         grad_in.astype(BF16),

time: 310 us -> 254 us (0.82)
  waiting for transfers between devices: 120 us -> 69 us
  blocking collectives: 12.3 us -> 0 us
  starting transfers between devices: 64.1 us -> 73 us
  other arithmetic: 6.54 us -> 14.8 us
  Pallas kernels: 58.6 us -> 52.8 us
  local copies, waits for them, and re-layouts: 30.3 us -> 25.6 us
    all_to_all x6 -> x7, waiting for transfers between devices: 76.7 us -> 41.1 us  [exchange(): return lax.all_to_all(parts, axes, 0, 0, tiled=True)]
    ppermute x18, waiting for transfers between devices: 41.8 us -> 23.2 us  [step(): return lax.ppermute(array, axis, [(i, (i + shift) % n) for i in range(n)])]
    all_to_all x1 -> x0, blocking collectives: 12.3 us -> none  [exchange(): return lax.all_to_all(parts, axes, 0, 0, tiled=True)]
    all_to_all x6 -> x7, starting transfers between devices: 36.9 us -> 46.5 us  [exchange(): return lax.all_to_all(parts, axes, 0, 0, tiled=True)]
    unnamed x89 -> x69, local copies, waits for them, and re-layouts: 18.5 us -> 10.5 us
    pallas_call x2 -> x1, Pallas kernels: 15.9 us -> 8.29 us  [grad_in_parts(): call(grad_in_body, 'grad_in', (NY,), [pl.BlockSpec((2, t, f), lambda i, p...]
    convert_element_type x1 -> x2, other arithmetic: 0.01 us -> 4.62 us  [the longest x1 4.61 us: shards(): terms = (own_terms.astype(F32) + from_other.astype(F32)).astype(BF16)]
    ppermute x1, waiting for transfers between devices: 0.01 us -> 3.98 us  [shards(): from_other = lax.ppermute(other_terms, 'core', OTHER)]
  transfers between devices with their start and end apart: 29 -> 30, of which waited for: 15 -> 16; matrix products, arithmetic and copies ran while one was open for 6% -> 7% of each run, Pallas kernels for 11% -> 15%
where the time goes in v5:
time: 254 us; the launch traced here: 253 us
  starting transfers between devices  73 us (29%)
  waiting for transfers between devices  69 us (27%)
  Pallas kernels  52.8 us (21%)
  local copies, waits for them, and re-layouts  25.6 us (10%)
  other arithmetic  14.8 us (6%)
  between operations  14.6 us (6%)
  matrix products  2.83 us (1%)
    all_to_all x7, starting transfers between devices, exchange(): return lax.all_to_all(parts, axes, 0, 0, tiled=True)  46.5 us
    all_to_all x7, waiting for transfers between devices, exchange(): return lax.all_to_all(parts, axes, 0, 0, tiled=True)  41.1 us
    ppermute x18, starting transfers between devices, step(): return lax.ppermute(array, axis, [(i, (i + shift) % n) for i in range(n)])  25.8 us
    ppermute x18, waiting for transfers between devices, step(): return lax.ppermute(array, axis, [(i, (i + shift) % n) for i in range(n)])  23.2 us
    pallas_call x1, Pallas kernels, gate_up(): call(gate_up_body, 'gate_up', (NY,), [x_spec(t, w), x_spec(t, w), pl.Bloc...  13.5 us
    unnamed x69, local copies, waits for them, and re-layouts  10.5 us
    pallas_call x1, Pallas kernels, grad_in_parts(): call(grad_in_body, 'grad_in', (NY,), [pl.BlockSpec((2, t, f), lambda i, p...  8.29 us
    pallas_call x1, Pallas kernels, grad_act_rows(): call(grad_act_body, 'grad_act', (NY,), [g_spec(t, w), g_spec(t, w), pl.Bl...  7.24 us
  transfers between devices with their start and end apart: 30, of which 16 were waited for; matrix products, arithmetic and copies ran while one was open for 7% of the time, Pallas kernels for 15%

profile of v5, /device:TPU:2, one launch (start us, length us, event | category | flops | bytes accessed | tf_op | source)
XLA Modules:
  0.0 252.6 jit_solution(2800141065456110023)
XLA Ops:
  7.9 1.8 broadcast_in_dim.40
  9.8 8.5 %all-to-all-start.2 = ((bf16[8,192,256]{2,1,0:T(8,128)(2,1)}), bf16[8,192,256]{2,1,0:T(8,128)(2,1)S(1)}, u32[]{:S(2)}, u32[]{:S(2)}) async-start(bf16[8,192,256]{2,1,0:T(8,128)(2,1)} %broadcast_in_dim.40), calls=%async_computation.2 | async-start | bytes 1572864 | tf_op jit(solution)/shard_map/all_to_all | solution.py:307
  18.3 1.7 collective-permute-start
  19.9 1.7 collective-permute-start.1
  21.6 2.0 collective-permute-start.2
  24.2 1.1 collective-permute-done.1
  25.3 2.4 collective-permute-done.2
  28.5 1.9 collective-permute-start.3
  30.4 1.3 collective-permute-start.5
  31.7 6.4 %merge_down.1 = (bf16[256,8192]{1,0:T(8,128)(2,1)}, f32[64,8,128]{2,1,0:T(8,128)S(1)}) custom-call(s32[4]{0:T(128)S(1)} %pad_add_fusion.pos_ref, bf16[512,8192]{1,0:T(8,128)(2,1)} %frozen_ref.1, bf16[32,512]{1,0:T(8,128)(2,1)S(1)} %bitcast.95, bf16[32,8192]{1,0:T(8,128)(2,1)S(1)} %copy-done.15), custom_call_target="tpu_custom_call" | custom-call | flops 1000000000 | bytes 16000000 | tf_op jit(solution)/shard_map/merge_down/pallas_call | solution.py:95
  38.8 2.6 %all-to-all-done.2.refs_0_ = bf16[8,192,256]{2,1,0:T(8,128)(2,1)S(1)} async-done(((bf16[8,192,256]{2,1,0:T(8,128)(2,1)}), bf16[8,192,256]{2,1,0:T(8,128)(2,1)S(1)}, u32[]{:S(2)}, u32[]{:S(2)}) %all-to-all-start.2) | async-done | bytes 786464 | tf_op jit(solution)/shard_map/all_to_all | solution.py:307
  41.5 0.9 copy-done.2
  42.4 1.6 collective-permute-start.12
  43.9 1.7 collective-permute-start.13
  45.6 1.6 collective-permute-done.3.refs_1_.refs_2_
  47.2 8.2 %all-to-all-start = ((f32[64,8,128]{2,1,0:T(8,128)}), f32[64,8,128]{2,1,0:T(8,128)S(1)}, u32[]{:S(2)}, u32[]{:S(2)}) async-start(f32[64,8,128]{2,1,0:T(8,128)} %after.9), calls=%async_computation | async-start | bytes 524288 | tf_op jit(solution)/shard_map/all_to_all | solution.py:307
  55.4 2.9 %collective-permute-start.7 = (bf16[4,192,256]{2,1,0:T(8,128)(2,1)}, bf16[4,192,256]{2,1,0:T(8,128)(2,1)}, u32[]{:S(2)}, u32[]{:S(2)}) collective-permute-start(bf16[4,192,256]{2,1,0:T(8,128)(2,1)} %collective-permute-done.5.refs_2_.refs_4_), channel_id=1, source_target_pairs={{0,7},{1,0},{2,1},{3,2},{4,3},{5,4},{6,5},{7,6},{8,15},{9,8},{10,9... | collective-permute-start | bytes 1179656 | tf_op jit(solution)/shard_map/ppermute | solution.py:21
  58.3 6.7 %collective-permute-done.12.refs_0_ = bf16[8,192,256]{2,1,0:T(8,128)(2,1)S(1)} collective-permute-done((bf16[8,192,256]{2,1,0:T(8,128)(2,1)}, bf16[8,192,256]{2,1,0:T(8,128)(2,1)S(1)}, u32[]{:S(2)}, u32[]{:S(2)}) %collective-permute-start.12) | collective-permute-done | bytes 786464 | tf_op jit(solution)/shard_map/ppermute | solution.py:21
  66.5 0.8 slice.134
  67.3 2.5 collective-permute-start.15
  70.6 4.6 %all-to-all-start.1 = ((f32[64,8,128]{2,1,0:T(8,128)}), f32[64,8,128]{2,1,0:T(8,128)S(1)}, u32[]{:S(2)}, u32[]{:S(2)}) async-start(f32[64,8,128]{2,1,0:T(8,128)} %broadcast_in_dim_broadcast_in_dim_broadcast_in_dim.2), calls=%async_computation.1 | async-start | bytes 524288 | tf_op jit(solution)/shard_map/all_to_all | solution.py:307
  75.3 3.0 %collective-permute-start.8 = (bf16[4,192,256]{2,1,0:T(8,128)(2,1)}, bf16[4,192,256]{2,1,0:T(8,128)(2,1)S(1)}, u32[]{:S(2)}, u32[]{:S(2)}) collective-permute-start(bf16[4,192,256]{2,1,0:T(8,128)(2,1)} %after.12.refs_5_), channel_id=1, source_target_pairs={{0,7},{1,0},{2,1},{3,2},{4,3},{5,4},{6,5},{7,6},{8,15},{9,8},{10,9... | collective-permute-start | bytes 1179656 | tf_op jit(solution)/shard_map/ppermute | solution.py:21
  78.4 1.1 copy-done.17
  79.5 3.0 %stack.55.own_ref = bf16[4,8,192,256]{3,2,1,0:T(8,128)(2,1)} custom-call(bf16[8,192,256]{2,1,0:T(8,128)(2,1)S(1)} %collective-permute-done.12.refs_0_, bf16[8,192,256]{2,1,0:T(8,128)(2,1)S(1)} %copy-done.3, bf16[8,192,256]{2,1,0:T(8,128)(2,1)S(1)} %copy-done.17, bf16[4,192,256]{2,1,0:T(8,128)(2,1)} %collective-permute-done.14.refs_3_, ...), custom_call_target="tpu_custom_call" | custom-call | bytes 6000000 | tf_op jit(solution)/shard_map/stack/pallas_call | solution.py:54
  82.5 7.1 %all-to-all-done.1 = f32[64,8,128]{2,1,0:T(8,128)S(1)} async-done(((f32[64,8,128]{2,1,0:T(8,128)}), f32[64,8,128]{2,1,0:T(8,128)S(1)}, u32[]{:S(2)}, u32[]{:S(2)}) %all-to-all-start.1) | async-done | bytes 262176 | tf_op jit(solution)/shard_map/all_to_all | solution.py:307
  89.6 1.3 sqrt_reduce_fusion
  90.9 0.9 collective-permute-done.8.refs_0_
  92.5 0.9 slice.132
  93.5 1.7 collective-permute-start.10
  95.9 0.9 slice.131
  97.4 2.9 %collective-permute-done.10.refs_8_ = bf16[2,192,256]{2,1,0:T(8,128)(2,1)S(1)} collective-permute-done((bf16[2,192,256]{2,1,0:T(8,128)(2,1)S(1)}, bf16[2,192,256]{2,1,0:T(8,128)(2,1)S(1)}, u32[]{:S(2)}, u32[]{:S(2)}) %collective-permute-start.10) | collective-permute-done | bytes 196640 | tf_op jit(solution)/shard_map/ppermute | solution.py:21
  100.3 4.4 %collective-permute-done.9.refs_7_ = bf16[2,192,256]{2,1,0:T(8,128)(2,1)S(1)} collective-permute-done((bf16[2,192,256]{2,1,0:T(8,128)(2,1)S(1)}, bf16[2,192,256]{2,1,0:T(8,128)(2,1)S(1)}, u32[]{:S(2)}, u32[]{:S(2)}) %collective-permute-start.9) | collective-permute-done | bytes 196640 | tf_op jit(solution)/shard_map/ppermute | solution.py:21
  104.7 1.0 copy-done.11
  105.7 1.0 copy-done.13
  106.7 3.3 %stack.54.own_ref = bf16[8,4,192,256]{3,2,1,0:T(8,128)(2,1)} custom-call(bf16[4,192,256]{2,1,0:T(8,128)(2,1)S(1)} %copy-done.13, bf16[4,192,256]{2,1,0:T(8,128)(2,1)} %after.10.refs_1_, bf16[4,192,256]{2,1,0:T(8,128)(2,1)} %collective-permute-done.3.refs_1_.refs_2_, bf16[4,192,256]{2,1,0:T(8,128)(2,1)} %pad_maximum_fusion.1.refs_3_, ...), custom_call_target="tpu_custom_call" | custom-call | bytes 6000000 | tf_op jit(solution)/shard_map/stack/pallas_call | solution.py:54
  110.1 13.5 %gate_up.1 = (bf16[2,8192,256]{2,1,0:T(8,128)(2,1)}, f32[2,384,256]{2,1,0:T(8,128)S(1)}, f32[2,8,256]{2,1,0:T(8,128)S(1)}) custom-call(s32[4]{0:T(128)S(1)} %pad_add_fusion.pos_ref, bf16[4,8,192,256]{3,2,1,0:T(8,128)(2,1)} %stack.55.own_ref, bf16[4,8,192,256]{3,2,1,0:T(8,128)(2,1)} %collective-permute-done.16.other_ref, ...), custom_call_target="tpu_custom_call" | custom-call | flops 1000000000 | bytes 16000000 | tf_op jit(solution)/shard_map/gate_up/pallas_call | solution.py:253
  123.8 7.2 %grad_act.1 = (f32[384,256]{1,0:T(8,128)S(1)}, f32[384,32]{1,0:T(8,128)S(1)}) custom-call(s32[4]{0:T(128)S(1)} %pad_add_fusion.pos_ref, bf16[8,4,192,256]{3,2,1,0:T(8,128)(2,1)} %stack.54.own_ref, bf16[8,4,192,256]{3,2,1,0:T(8,128)(2,1)} %collective-permute-done.11.other_ref, f32[32,1,256]{2,1,0:T(1,128)S(1)} %div.15.scale_ref, ...), custom_call_target="tpu_custom_call" | custom-call | flops 1000000000 | bytes 16000000 | tf_op jit(solution)/shard_map/grad_act/pallas_call | solution.py:175
  131.5 8.3 %grad_in.1 = (bf16[8,4,192,256]{3,2,1,0:T(8,128)(2,1)S(1)}, bf16[8,4,192,256]{3,2,1,0:T(8,128)(2,1)}) custom-call(s32[4]{0:T(128)S(1)} %pad_add_fusion.pos_ref, bf16[2,384,256]{2,1,0:T(8,128)(2,1)S(1)} %get-tuple-element.28.grads_ref, bf16[2,8192,256]{2,1,0:T(8,128)(2,1)} %get-tuple-element.21.tile_ref), custom_call_target="tpu_custom_call" | custom-call | flops 1000000000 | bytes 16000000 | tf_op jit(solution)/shard_map/grad_in/pallas_call | solution.py:293
  139.8 1.6 copy-done.8
  143.5 4.0 %collective-permute-done.17.refs_0_ = bf16[8,4,192,256]{3,2,1,0:T(8,128)(2,1)} collective-permute-done((bf16[8,4,192,256]{3,2,1,0:T(8,128)(2,1)}, bf16[8,4,192,256]{3,2,1,0:T(8,128)(2,1)}, u32[]{:S(2)}, u32[]{:S(2)}) %collective-permute-start.17) | collective-permute-done | bytes 3145760 | tf_op jit(solution)/shard_map/ppermute | solution.py:380
  147.5 4.6 %add_convert_fusion = bf16[8,4,192,256]{3,2,1,0:T(8,128)(2,1)} fusion(bf16[8,4,192,256]{3,2,1,0:T(8,128)(2,1)} %after.15, bf16[8,4,192,256]{3,2,1,0:T(8,128)(2,1)S(1)} %copy-done.9), kind=kLoop, calls=%fused_computation | loop fusion | flops 6291456 | bytes 9437184 | tf_op jit(solution)/shard_map/convert_element_type | solution.py:391
  152.7 10.9 %all-to-all-start.3 = ((f32[64,8,128]{2,1,0:T(8,128)}), f32[64,8,128]{2,1,0:T(8,128)}, u32[]{:S(2)}, u32[]{:S(2)}) async-start(f32[64,8,128]{2,1,0:T(8,128)} %pad.12.refs_1_), calls=%async_computation.4 | async-start | bytes 524288 | tf_op jit(solution)/shard_map/all_to_all | solution.py:307
  163.7 5.8 %dot_down.1 = f32[64,1,128]{2,1,0:T(1,128)S(1)} custom-call(s32[4]{0:T(128)S(1)} %pad_add_fusion.pos_ref, bf16[8,4,192,256]{3,2,1,0:T(8,128)(2,1)S(1)} %copy-done.1, bf16[8,4,192,256]{3,2,1,0:T(8,128)(2,1)} %collective-permute-done.11.other_ref, bf16[384,256]{1,0:T(8,128)(2,1)S(1)} %get-tuple-element.29.act_ref, bf16[256,8192]{1,0:T(8,128)(2,1)} %get-tuple-element.17.tile_ref), custom_call_target="tpu_custom_call" | custom-call | flops 1000000000 | bytes 16000000 | tf_op jit(solution)/shard_map/dot_down/pallas_call | solution.py:209
  169.8 10.1 %all-to-all-done.3 = f32[64,8,128]{2,1,0:T(8,128)} async-done(((f32[64,8,128]{2,1,0:T(8,128)}), f32[64,8,128]{2,1,0:T(8,128)}, u32[]{:S(2)}, u32[]{:S(2)}) %all-to-all-start.3) | async-done | bytes 262176 | tf_op jit(solution)/shard_map/all_to_all | solution.py:307
  179.9 1.0 reduce_sum.60._
  180.9 0.8 maximum_maximum_fusion
  181.7 4.6 %all-to-all-start.4 = ((f32[64,8,128]{2,1,0:T(8,128)}), f32[64,8,128]{2,1,0:T(8,128)S(1)}, u32[]{:S(2)}, u32[]{:S(2)}) async-start(f32[64,8,128]{2,1,0:T(8,128)} %maximum_maximum_fusion), calls=%async_computation.5 | async-start | bytes 524288 | tf_op jit(solution)/shard_map/all_to_all | solution.py:307
  186.4 1.2 copy-done.7
  187.6 5.2 %proj_gate_up.1 = f32[384,64]{1,0:T(8,128)S(1)} custom-call(s32[4]{0:T(128)S(1)} %pad_add_fusion.pos_ref, bf16[4,8,192,256]{3,2,1,0:T(8,128)(2,1)} %stack.55.own_ref, bf16[4,8,192,256]{3,2,1,0:T(8,128)(2,1)} %collective-permute-done.16.other_ref, bf16[2,32,8192]{2,1,0:T(8,128)(2,1)S(1)} %bitcast.93, f32[8,128]{1,0:T(8,128)S(1)} %reduce_sum.60._), custom_call_target="tpu_custom_call" | custom-call | flops 1000000000 | bytes 16000000 | tf_op jit(solution)/shard_map/proj_gate_up/pallas_call | solution.py:139
  193.4 10.2 %all-to-all-done.4 = f32[64,8,128]{2,1,0:T(8,128)S(1)} async-done(((f32[64,8,128]{2,1,0:T(8,128)}), f32[64,8,128]{2,1,0:T(8,128)S(1)}, u32[]{:S(2)}, u32[]{:S(2)}) %all-to-all-start.4) | async-done | bytes 262176 | tf_op jit(solution)/shard_map/all_to_all | solution.py:307
  203.7 0.8 fusion
  204.6 0.9 fusion.1
  207.4 4.9 %all-to-all-start.5 = ((f32[8,48,256]{2,1,0:T(8,128)}), f32[8,48,256]{2,1,0:T(8,128)S(1)}, u32[]{:S(2)}, u32[]{:S(2)}) async-start(f32[8,48,256]{2,1,0:T(8,128)} %bitcast.30), calls=%async_computation.6 | async-start | bytes 786432 | tf_op jit(solution)/shard_map/all_to_all | solution.py:307
  212.3 7.5 %all-to-all-done.5 = f32[8,48,256]{2,1,0:T(8,128)S(1)} async-done(((f32[8,48,256]{2,1,0:T(8,128)}), f32[8,48,256]{2,1,0:T(8,128)S(1)}, u32[]{:S(2)}, u32[]{:S(2)}) %all-to-all-start.5) | async-done | bytes 393248 | tf_op jit(solution)/shard_map/all_to_all | solution.py:307
  220.6 4.8 %all-to-all-start.6 = ((f32[8,48,256]{2,1,0:T(8,128)}), f32[8,48,256]{2,1,0:T(8,128)S(1)}, u32[]{:S(2)}, u32[]{:S(2)}) async-start(f32[8,48,256]{2,1,0:T(8,128)} %broadcast_in_dim.46), calls=%async_computation.7 | async-start | bytes 786432 | tf_op jit(solution)/shard_map/all_to_all | solution.py:307
  225.4 1.2 fusion.2
  226.6 1.0 collective-permute-start.18
  227.6 1.1 collective-permute-start.19
  229.4 3.5 %all-to-all-done.6.refs_0_ = f32[8,48,256]{2,1,0:T(8,128)S(1)} async-done(((f32[8,48,256]{2,1,0:T(8,128)}), f32[8,48,256]{2,1,0:T(8,128)S(1)}, u32[]{:S(2)}, u32[]{:S(2)}) %all-to-all-start.6) | async-done | bytes 393248 | tf_op jit(solution)/shard_map/all_to_all | solution.py:307
  232.9 2.6 %collective-permute-done.19.refs_2_ = bf16[192,256]{1,0:T(8,128)(2,1)S(1)} collective-permute-done((bf16[192,256]{1,0:T(8,128)(2,1)S(1)}, bf16[192,256]{1,0:T(8,128)(2,1)S(1)}, u32[]{:S(2)}, u32[]{:S(2)}) %collective-permute-start.19) | collective-permute-done | bytes 98336 | tf_op jit(solution)/shard_map/ppermute | solution.py:21
  237.5 1.0 slice.149
  239.1 1.5 slice.151
  240.6 1.4 slice.155
  244.1 1.7 fusion.4
  (150 shorter events, 19.6 us)
Async XLA Ops:
  7.2 102.8 %copy-start = (bf16[2,32,512]{2,1,0:T(8,128)(2,1)S(1)}, bf16[2,32,512]{2,1,0:T(8,128)(2,1)}, u32[]{:S(2)}) copy-start(bf16[2,32,512]{2,1,0:T(8,128)(2,1)} %param.14) | copy-start | bytes 196612
  7.2 11.1 %copy-start.25 = (bf16[192,256]{1,0:T(8,128)(2,1)S(1)}, bf16[192,256]{1,0:T(8,128)(2,1)}, u32[]{:S(2)}) copy-start(bf16[192,256]{1,0:T(8,128)(2,1)} %param.11) | copy-start | bytes 294916
  7.2 24.5 %copy-start.21 = (bf16[512,32]{0,1:T(8,128)(2,1)S(1)}, bf16[512,32]{0,1:T(8,128)(2,1)}, u32[]{:S(2)}) copy-start(bf16[512,32]{0,1:T(8,128)(2,1)} %param.17) | copy-start | bytes 98308
  7.2 24.5 %copy-start.15 = (bf16[32,8192]{1,0:T(8,128)(2,1)S(1)}, bf16[32,8192]{1,0:T(8,128)(2,1)}, u32[]{:S(2)}) copy-start(bf16[32,8192]{1,0:T(8,128)(2,1)} %right_ref.3) | copy-start | bytes 1572868
  7.2 102.9 %all-gather.2.cloned.1.call-start = ((), (), s32[]{:S(2)}) async-start(), calls=%async_computation.8 | async-start | bytes 18874368 | tf_op jit(solution)/shard_map/all_gather | solution.py:338
  9.8 31.7 %all-to-all-start.2 = ((bf16[8,192,256]{2,1,0:T(8,128)(2,1)}), bf16[8,192,256]{2,1,0:T(8,128)(2,1)S(1)}, u32[]{:S(2)}, u32[]{:S(2)}) async-start(bf16[8,192,256]{2,1,0:T(8,128)(2,1)} %broadcast_in_dim.40), calls=%async_computation.2 | async-start | bytes 1572864 | tf_op jit(solution)/shard_map/all_to_all | solution.py:307
  18.3 5.9 %collective-permute-start = (bf16[192,256]{1,0:T(8,128)(2,1)S(1)}, bf16[192,256]{1,0:T(8,128)(2,1)S(1)}, u32[]{:S(2)}, u32[]{:S(2)}) collective-permute-start(bf16[192,256]{1,0:T(8,128)(2,1)S(1)} %copy-done.25), channel_id=1, source_target_pairs={{0,8},{8,16},{16,24},{24,0},{1,9},{9,17},{17,25},{25,1},{2,10},{10... | collective-permute-start | bytes 294920 | tf_op jit(solution)/shard_map/ppermute | solution.py:21
  19.9 5.3 %collective-permute-start.1 = (bf16[192,256]{1,0:T(8,128)(2,1)S(1)}, bf16[192,256]{1,0:T(8,128)(2,1)S(1)}, u32[]{:S(2)}, u32[]{:S(2)}) collective-permute-start(bf16[192,256]{1,0:T(8,128)(2,1)S(1)} %copy-done.25), channel_id=1, source_target_pairs={{0,24},{8,0},{16,8},{24,16},{1,25},{9,1},{17,9},{25,17},{2,26},{10... | collective-permute-start | bytes 294920 | tf_op jit(solution)/shard_map/ppermute | solution.py:21
  21.6 6.1 %collective-permute-start.2 = (bf16[192,256]{1,0:T(8,128)(2,1)S(1)}, bf16[192,256]{1,0:T(8,128)(2,1)S(1)}, u32[]{:S(2)}, u32[]{:S(2)}) collective-permute-start(bf16[192,256]{1,0:T(8,128)(2,1)S(1)} %copy-done.25), channel_id=1, source_target_pairs={{0,16},{8,24},{16,0},{24,8},{1,17},{9,25},{17,1},{25,9},{2,18},{10... | collective-permute-start | bytes 294920 | tf_op jit(solution)/shard_map/ppermute | solution.py:21
  28.5 18.7 %collective-permute-start.3 = (bf16[4,192,256]{2,1,0:T(8,128)(2,1)}, bf16[4,192,256]{2,1,0:T(8,128)(2,1)}, u32[]{:S(2)}, u32[]{:S(2)}) collective-permute-start(bf16[4,192,256]{2,1,0:T(8,128)(2,1)} %pad_maximum_fusion.1.refs_3_), channel_id=1, source_target_pairs={{0,1},{1,2},{2,3},{3,4},{4,5},{5,6},{6,7},{7,0},{8,9},{9,10},{10,1... | collective-permute-start | bytes 1179656 | tf_op jit(solution)/shard_map/ppermute | solution.py:21
  30.4 16.8 %collective-permute-start.5 = (bf16[4,192,256]{2,1,0:T(8,128)(2,1)}, bf16[4,192,256]{2,1,0:T(8,128)(2,1)}, u32[]{:S(2)}, u32[]{:S(2)}) collective-permute-start(bf16[4,192,256]{2,1,0:T(8,128)(2,1)} %pad_maximum_fusion.1.refs_3_), channel_id=1, source_target_pairs={{0,7},{1,0},{2,1},{3,2},{4,3},{5,4},{6,5},{7,6},{8,15},{9,8},{10,9... | collective-permute-start | bytes 1179656 | tf_op jit(solution)/shard_map/ppermute | solution.py:21
  38.1 0.7 copy-start.14
  41.5 0.9 copy-start.2
  42.4 36.0 %copy-start.3 = (bf16[8,192,256]{2,1,0:T(8,128)(2,1)S(1)}, bf16[8,192,256]{2,1,0:T(8,128)(2,1)}, u32[]{:S(2)}) copy-start(bf16[8,192,256]{2,1,0:T(8,128)(2,1)} %after.14.refs_1_) | copy-start | bytes 2359300
  42.4 22.6 %collective-permute-start.12 = (bf16[8,192,256]{2,1,0:T(8,128)(2,1)}, bf16[8,192,256]{2,1,0:T(8,128)(2,1)S(1)}, u32[]{:S(2)}, u32[]{:S(2)}) collective-permute-start(bf16[8,192,256]{2,1,0:T(8,128)(2,1)} %after.14.refs_1_), channel_id=1, source_target_pairs={{0,8},{8,16},{16,24},{24,0},{1,9},{9,17},{17,25},{25,1},{2,10},{10... | collective-permute-start | bytes 2359304 | tf_op jit(solution)/shard_map/ppermute | solution.py:21
  43.9 22.5 %collective-permute-start.13 = (bf16[8,192,256]{2,1,0:T(8,128)(2,1)}, bf16[8,192,256]{2,1,0:T(8,128)(2,1)S(1)}, u32[]{:S(2)}, u32[]{:S(2)}) collective-permute-start(bf16[8,192,256]{2,1,0:T(8,128)(2,1)} %after.14.refs_1_), channel_id=1, source_target_pairs={{0,24},{8,0},{16,8},{24,16},{1,25},{9,1},{17,9},{25,17},{2,26},{10... | collective-permute-start | bytes 2359304 | tf_op jit(solution)/shard_map/ppermute | solution.py:21
  47.2 22.6 %all-to-all-start = ((f32[64,8,128]{2,1,0:T(8,128)}), f32[64,8,128]{2,1,0:T(8,128)S(1)}, u32[]{:S(2)}, u32[]{:S(2)}) async-start(f32[64,8,128]{2,1,0:T(8,128)} %after.9), calls=%async_computation | async-start | bytes 524288 | tf_op jit(solution)/shard_map/all_to_all | solution.py:307
  55.4 19.9 %collective-permute-start.7 = (bf16[4,192,256]{2,1,0:T(8,128)(2,1)}, bf16[4,192,256]{2,1,0:T(8,128)(2,1)}, u32[]{:S(2)}, u32[]{:S(2)}) collective-permute-start(bf16[4,192,256]{2,1,0:T(8,128)(2,1)} %collective-permute-done.5.refs_2_.refs_4_), channel_id=1, source_target_pairs={{0,7},{1,0},{2,1},{3,2},{4,3},{5,4},{6,5},{7,6},{8,15},{9,8},{10,9... | collective-permute-start | bytes 1179656 | tf_op jit(solution)/shard_map/ppermute | solution.py:21
  58.3 20.1 %collective-permute-start.4 = (bf16[4,192,256]{2,1,0:T(8,128)(2,1)}, bf16[4,192,256]{2,1,0:T(8,128)(2,1)}, u32[]{:S(2)}, u32[]{:S(2)}) collective-permute-start(bf16[4,192,256]{2,1,0:T(8,128)(2,1)} %collective-permute-done.3.refs_1_.refs_2_), channel_id=1, source_target_pairs={{0,1},{1,2},{2,3},{3,4},{4,5},{5,6},{6,7},{7,0},{8,9},{9,10},{10,1... | collective-permute-start | bytes 1179656 | tf_op jit(solution)/shard_map/ppermute | solution.py:21
  65.7 12.6 %collective-permute-start.14 = (bf16[4,192,256]{2,1,0:T(8,128)(2,1)}, bf16[4,192,256]{2,1,0:T(8,128)(2,1)}, u32[]{:S(2)}, u32[]{:S(2)}) collective-permute-start(bf16[4,192,256]{2,1,0:T(8,128)(2,1)} %slice.133), channel_id=1, source_target_pairs={{0,8},{8,16},{16,24},{24,0},{1,9},{9,17},{17,25},{25,1},{2,10},{10... | collective-permute-start | bytes 1179656 | tf_op jit(solution)/shard_map/ppermute | solution.py:21
  66.5 8.8 %copy-start.16 = (bf16[8,192,256]{2,1,0:T(8,128)(2,1)}, bf16[8,192,256]{2,1,0:T(8,128)(2,1)S(1)}, u32[]{:S(2)}) copy-start(bf16[8,192,256]{2,1,0:T(8,128)(2,1)S(1)} %collective-permute-done.13.refs_2_) | copy-start | bytes 2359300
  67.3 11.0 %collective-permute-start.15 = (bf16[4,192,256]{2,1,0:T(8,128)(2,1)}, bf16[4,192,256]{2,1,0:T(8,128)(2,1)}, u32[]{:S(2)}, u32[]{:S(2)}) collective-permute-start(bf16[4,192,256]{2,1,0:T(8,128)(2,1)} %slice.134), channel_id=1, source_target_pairs={{0,24},{8,0},{16,8},{24,16},{1,25},{9,1},{17,9},{25,17},{2,26},{10... | collective-permute-start | bytes 1179656 | tf_op jit(solution)/shard_map/ppermute | solution.py:21
  69.9 5.4 %copy-start.31 = (f32[128]{0:T(128)}, f32[128]{0:T(128)S(1)}, u32[]{:S(2)}) copy-start(f32[128]{0:T(128)S(1)} %reduce_sum.58) | copy-start | bytes 1540
  70.6 19.0 %all-to-all-start.1 = ((f32[64,8,128]{2,1,0:T(8,128)}), f32[64,8,128]{2,1,0:T(8,128)S(1)}, u32[]{:S(2)}, u32[]{:S(2)}) async-start(f32[64,8,128]{2,1,0:T(8,128)} %broadcast_in_dim_broadcast_in_dim_broadcast_in_dim.2), calls=%async_computation.1 | async-start | bytes 524288 | tf_op jit(solution)/shard_map/all_to_all | solution.py:307
  75.3 150.1 %reduce-scatter.2.cloned.1.call-start = ((), (), s32[]{:S(2)}) async-start(), calls=%async_computation.9 | async-start | bytes 3538944 | tf_op jit(solution)/shard_map/reduce_scatter | solution.py:392
  75.3 16.4 %collective-permute-start.8 = (bf16[4,192,256]{2,1,0:T(8,128)(2,1)}, bf16[4,192,256]{2,1,0:T(8,128)(2,1)S(1)}, u32[]{:S(2)}, u32[]{:S(2)}) collective-permute-start(bf16[4,192,256]{2,1,0:T(8,128)(2,1)} %after.12.refs_5_), channel_id=1, source_target_pairs={{0,7},{1,0},{2,1},{3,2},{4,3},{5,4},{6,5},{7,6},{8,15},{9,8},{10,9... | collective-permute-start | bytes 1179656 | tf_op jit(solution)/shard_map/ppermute | solution.py:21
  78.3 16.8 %collective-permute-start.6 = (bf16[4,192,256]{2,1,0:T(8,128)(2,1)}, bf16[4,192,256]{2,1,0:T(8,128)(2,1)S(1)}, u32[]{:S(2)}, u32[]{:S(2)}) collective-permute-start(bf16[4,192,256]{2,1,0:T(8,128)(2,1)} %after.10.refs_1_), channel_id=1, source_target_pairs={{0,1},{1,2},{2,3},{3,4},{4,5},{5,6},{6,7},{7,0},{8,9},{9,10},{10,1... | collective-permute-start | bytes 1179656 | tf_op jit(solution)/shard_map/ppermute | solution.py:21
  78.3 1.1 copy-start.17
  82.5 27.6 %collective-permute-start.16 = (bf16[4,8,192,256]{3,2,1,0:T(8,128)(2,1)}, bf16[4,8,192,256]{3,2,1,0:T(8,128)(2,1)}, u32[]{:S(2)}, u32[]{:S(2)}) collective-permute-start(bf16[4,8,192,256]{3,2,1,0:T(8,128)(2,1)} %stack.55.own_ref), channel_id=1, source_target_pairs={{0,32},{32,0},{1,33},{33,1},{2,34},{34,2},{3,35},{35,3},{4,36},{36... | collective-permute-start | bytes 9437192 | tf_op jit(solution)/shard_map/ppermute | solution.py:357
  91.8 0.7 copy-start.10
  93.5 6.8 %collective-permute-start.10 = (bf16[2,192,256]{2,1,0:T(8,128)(2,1)S(1)}, bf16[2,192,256]{2,1,0:T(8,128)(2,1)S(1)}, u32[]{:S(2)}, u32[]{:S(2)}) collective-permute-start(bf16[2,192,256]{2,1,0:T(8,128)(2,1)S(1)} %slice.132), channel_id=1, source_target_pairs={{0,7},{1,0},{2,1},{3,2},{4,3},{5,4},{6,5},{7,6},{8,15},{9,8},{10,9... | collective-permute-start | bytes 589832 | tf_op jit(solution)/shard_map/ppermute | solution.py:21
  95.2 0.8 copy-start.12
  95.9 14.1 %copy-start.30 = (f32[8192]{0:T(1024)S(1)}, f32[8192]{0:T(1024)}, u32[]{:S(2)}) copy-start(f32[8192]{0:T(1024)} %param.19) | copy-start | bytes 98308
  95.9 14.2 %copy-start.18 = (f32[64,1,128]{2,1,0:T(1,128)S(1)}, f32[64,1,128]{2,1,0:T(1,128)}, u32[]{:S(2)}) copy-start(f32[64,1,128]{2,1,0:T(1,128)} %get-tuple-element.35.refs_1_._) | copy-start | bytes 98308
  96.9 13.2 %copy-start.6 = (bf16[2,8192,32]{1,2,0:T(8,128)(2,1)S(1)}, bf16[2,8192,32]{1,2,0:T(8,128)(2,1)}, u32[]{:S(2)}) copy-start(bf16[2,8192,32]{1,2,0:T(8,128)(2,1)} %param.13) | copy-start | bytes 3145732
  96.9 7.8 %collective-permute-start.9 = (bf16[2,192,256]{2,1,0:T(8,128)(2,1)S(1)}, bf16[2,192,256]{2,1,0:T(8,128)(2,1)S(1)}, u32[]{:S(2)}, u32[]{:S(2)}) collective-permute-start(bf16[2,192,256]{2,1,0:T(8,128)(2,1)S(1)} %slice.131), channel_id=1, source_target_pairs={{0,1},{1,2},{2,3},{3,4},{4,5},{5,6},{6,7},{7,0},{8,9},{9,10},{10,1... | collective-permute-start | bytes 589832 | tf_op jit(solution)/shard_map/ppermute | solution.py:21
  104.7 1.0 copy-start.11
  105.7 1.0 copy-start.13
  110.0 13.8 %collective-permute-start.11 = (bf16[8,4,192,256]{3,2,1,0:T(8,128)(2,1)}, bf16[8,4,192,256]{3,2,1,0:T(8,128)(2,1)}, u32[]{:S(2)}, u32[]{:S(2)}) collective-permute-start(bf16[8,4,192,256]{3,2,1,0:T(8,128)(2,1)} %stack.54.own_ref), channel_id=1, source_target_pairs={{0,32},{32,0},{1,33},{33,1},{2,34},{34,2},{3,35},{35,3},{4,36},{36... | collective-permute-start | bytes 9437192 | tf_op jit(solution)/shard_map/ppermute | solution.py:358
  110.1 13.6 %copy-start.32 = (f32[2,512]{1,0:T(2,128)S(1)}, f32[2,512]{1,0:T(2,128)}, u32[]{:S(2)}) copy-start(f32[2,512]{1,0:T(2,128)} %param.15) | copy-start | bytes 12292
  131.1 8.7 %copy-start.19 = (f32[384,32]{1,0:T(8,128)}, f32[384,32]{1,0:T(8,128)S(1)}, u32[]{:S(2)}) copy-start(f32[384,32]{1,0:T(8,128)S(1)} %get-tuple-element.24) | copy-start | bytes 147460
  131.5 10.7 %copy-start.4 = (bf16[2,384,256]{2,1,0:T(8,128)(2,1)}, bf16[2,384,256]{2,1,0:T(8,128)(2,1)S(1)}, u32[]{:S(2)}) copy-start(bf16[2,384,256]{2,1,0:T(8,128)(2,1)S(1)} %get-tuple-element.28.grads_ref) | copy-start | bytes 1179652
  139.8 1.6 copy-start.8
  141.4 6.1 %collective-permute-start.17 = (bf16[8,4,192,256]{3,2,1,0:T(8,128)(2,1)}, bf16[8,4,192,256]{3,2,1,0:T(8,128)(2,1)}, u32[]{:S(2)}, u32[]{:S(2)}) collective-permute-start(bf16[8,4,192,256]{3,2,1,0:T(8,128)(2,1)} %get-tuple-element.23), channel_id=1, source_target_pairs={{0,32},{32,0},{1,33},{33,1},{2,34},{34,2},{3,35},{35,3},{4,36},{36... | collective-permute-start | bytes 9437192 | tf_op jit(solution)/shard_map/ppermute | solution.py:380
  143.5 4.0 %copy-start.9 = (bf16[8,4,192,256]{3,2,1,0:T(8,128)(2,1)S(1)}, bf16[8,4,192,256]{3,2,1,0:T(8,128)(2,1)}, u32[]{:S(2)}) copy-start(bf16[8,4,192,256]{3,2,1,0:T(8,128)(2,1)} %copy-done.8) | copy-start | bytes 9437188
  152.1 11.6 %copy-start.1 = (bf16[8,4,192,256]{3,2,1,0:T(8,128)(2,1)S(1)}, bf16[8,4,192,256]{3,2,1,0:T(8,128)(2,1)}, u32[]{:S(2)}) copy-start(bf16[8,4,192,256]{3,2,1,0:T(8,128)(2,1)} %stack.54.own_ref) | copy-start | bytes 9437188
  152.7 27.1 %all-to-all-start.3 = ((f32[64,8,128]{2,1,0:T(8,128)}), f32[64,8,128]{2,1,0:T(8,128)}, u32[]{:S(2)}, u32[]{:S(2)}) async-start(f32[64,8,128]{2,1,0:T(8,128)} %pad.12.refs_1_), calls=%async_computation.4 | async-start | bytes 524288 | tf_op jit(solution)/shard_map/all_to_all | solution.py:307
  163.7 5.9 %copy-start.20 = (f32[384,32]{1,0:T(8,128)S(1)}, f32[384,32]{1,0:T(8,128)}, u32[]{:S(2)}) copy-start(f32[384,32]{1,0:T(8,128)} %copy-done.19) | copy-start | bytes 147460
  163.7 17.2 %copy-start.33 = (f32[8]{0:T(128)S(1)}, f32[8]{0:T(128)}, u32[]{:S(2)}) copy-start(f32[8]{0:T(128)} %pad.25.clone) | copy-start | bytes 100
  181.7 21.8 %all-to-all-start.4 = ((f32[64,8,128]{2,1,0:T(8,128)}), f32[64,8,128]{2,1,0:T(8,128)S(1)}, u32[]{:S(2)}, u32[]{:S(2)}) async-start(f32[64,8,128]{2,1,0:T(8,128)} %maximum_maximum_fusion), calls=%async_computation.5 | async-start | bytes 524288 | tf_op jit(solution)/shard_map/all_to_all | solution.py:307
  186.4 1.2 copy-start.7
  187.6 5.3 %copy-start.5 = (bf16[2,384,256]{2,1,0:T(8,128)(2,1)S(1)}, bf16[2,384,256]{2,1,0:T(8,128)(2,1)}, u32[]{:S(2)}) copy-start(bf16[2,384,256]{2,1,0:T(8,128)(2,1)} %copy-done.4) | copy-start | bytes 1179652
  187.6 16.1 %copy-start.24 = (bf16[192,256]{1,0:T(8,128)(2,1)S(1)}, bf16[192,256]{1,0:T(8,128)(2,1)}, u32[]{:S(2)}) copy-start(bf16[192,256]{1,0:T(8,128)(2,1)} %param.10) | copy-start | bytes 294916
  192.9 19.4 %copy-start.29 = (f32[64,128]{1,0:T(8,128)S(1)}, f32[64,128]{1,0:T(8,128)}, u32[]{:S(2)}) copy-start(f32[64,128]{1,0:T(8,128)} %get-tuple-element.33) | copy-start | bytes 98308
  207.4 12.4 %all-to-all-start.5 = ((f32[8,48,256]{2,1,0:T(8,128)}), f32[8,48,256]{2,1,0:T(8,128)S(1)}, u32[]{:S(2)}, u32[]{:S(2)}) async-start(f32[8,48,256]{2,1,0:T(8,128)} %bitcast.30), calls=%async_computation.6 | async-start | bytes 786432 | tf_op jit(solution)/shard_map/all_to_all | solution.py:307
  219.8 5.6 %copy-start.23 = (f32[48,256]{1,0:T(8,128)}, f32[48,256]{1,0:T(8,128)S(1)}, u32[]{:S(2)}) copy-start(f32[48,256]{1,0:T(8,128)S(1)} %reduce_sum.63.refs_1_) | copy-start | bytes 147460
  220.6 12.3 %all-to-all-start.6 = ((f32[8,48,256]{2,1,0:T(8,128)}), f32[8,48,256]{2,1,0:T(8,128)S(1)}, u32[]{:S(2)}, u32[]{:S(2)}) async-start(f32[8,48,256]{2,1,0:T(8,128)} %broadcast_in_dim.46), calls=%async_computation.7 | async-start | bytes 786432 | tf_op jit(solution)/shard_map/all_to_all | solution.py:307
  226.6 6.3 %collective-permute-start.18 = (bf16[192,256]{1,0:T(8,128)(2,1)S(1)}, bf16[192,256]{1,0:T(8,128)(2,1)S(1)}, u32[]{:S(2)}, u32[]{:S(2)}) collective-permute-start(bf16[192,256]{1,0:T(8,128)(2,1)S(1)} %get-tuple-element.30), channel_id=1, source_target_pairs={{0,24},{8,0},{16,8},{24,16},{1,25},{9,1},{17,9},{25,17},{2,26},{10... | collective-permute-start | bytes 294920 | tf_op jit(solution)/shard_map/ppermute | solution.py:21
  227.6 7.9 %collective-permute-start.19 = (bf16[192,256]{1,0:T(8,128)(2,1)S(1)}, bf16[192,256]{1,0:T(8,128)(2,1)S(1)}, u32[]{:S(2)}, u32[]{:S(2)}) collective-permute-start(bf16[192,256]{1,0:T(8,128)(2,1)S(1)} %get-tuple-element.31), channel_id=1, source_target_pairs={{0,8},{8,16},{16,24},{24,0},{1,9},{9,17},{17,25},{25,1},{2,10},{10... | collective-permute-start | bytes 294920 | tf_op jit(solution)/shard_map/ppermute | solution.py:21
  228.7 6.9 %collective-permute-start.20 = (bf16[192,256]{1,0:T(8,128)(2,1)S(1)}, bf16[192,256]{1,0:T(8,128)(2,1)S(1)}, u32[]{:S(2)}, u32[]{:S(2)}) collective-permute-start(bf16[192,256]{1,0:T(8,128)(2,1)S(1)} %get-tuple-element.32), channel_id=1, source_target_pairs={{0,16},{8,24},{16,0},{24,8},{1,17},{9,25},{17,1},{25,9},{2,18},{10... | collective-permute-start | bytes 294920 | tf_op jit(solution)/shard_map/ppermute | solution.py:21
  232.9 2.7 %copy-start.22 = (f32[8,48,256]{2,1,0:T(8,128)}, f32[8,48,256]{2,1,0:T(8,128)S(1)}, u32[]{:S(2)}) copy-start(f32[8,48,256]{2,1,0:T(8,128)S(1)} %all-to-all-done.6.refs_0_) | copy-start | bytes 1179652
  232.9 2.7 %copy-start.26 = (bf16[192,256]{1,0:T(8,128)(2,1)}, bf16[192,256]{1,0:T(8,128)(2,1)S(1)}, u32[]{:S(2)}) copy-start(bf16[192,256]{1,0:T(8,128)(2,1)S(1)} %collective-permute-done.18.refs_1_) | copy-start | bytes 294916
  235.6 0.6 copy-start.27
  236.2 0.6 copy-start.28
Sparse Core Ops, SparseCore 0:
  9.9 90.0 all-gather.1
  152.3 56.9 reduce-scatter.1

commit v6 on v5

--- a/solution.py
+++ b/solution.py
@@ -387,12 +387,12 @@
     rows = rows.reshape(NC, NMP, tokens // NMP, 128)
     rows = jnp.where(ic == 0, rows, rows[::-1]).reshape(NC * NMP, tokens // NMP, 128)
     rows = jnp.pad(rows, ((0, 0), (0, 2), (0, 0)))
-    from_other = after(from_other, rows)
+    dots = dot_down_sums(pos, g_own, g_other, act, tile_down).reshape(NMP, NC, 1, 128)
+    dots = dots.swapaxes(0, 1).reshape(NC * NMP, 1, 128)
+    from_other = after(from_other, rows, dots)
     terms = (own_terms.astype(F32) + from_other.astype(F32)).astype(BF16)
     over_z = lax.psum_scatter(terms, "z")
     rows = sum_parts(rows, CMP)
-    dots = dot_down_sums(pos, g_own, g_other, act, tile_down).reshape(NMP, NC, 1, 128)
-    dots = dots.swapaxes(0, 1).reshape(NC * NMP, 1, 128)
     rows_sum = rows
     rows = jnp.broadcast_to(rows[None, :6], (NC * NMP, 6, 128))
     rows = exchange(jnp.concatenate([rows, dots, jnp.zeros_like(dots)], axis=1), CMP)
@@ -423,7 +423,7 @@
     over_z = jnp.roll(after(over_z, sums), 1 - iy, 0)
     sent = [step(over_z[p], "y", NY, p - 1) for p in (0, 2, 3)]
     grad_in = over_z[1].astype(F32) + sum(r.astype(F32) for r in sent)
-    sums = after(gather_small(sums, DP, NDP), *sent).reshape(384, width)
+    sums = gather_small(sums, DP, NDP).reshape(384, width)
     cores = sums[128:].reshape(NC, 128, hidden).swapaxes(0, 1).reshape(128, NC * hidden)
     return (
         grad_in.astype(BF16),

time: 254 us -> 258 us (1.016)
  blocking collectives: 0 us -> 12.1 us
  starting transfers between devices: 73 us -> 68.3 us
    all_to_all x0 -> x1, blocking collectives: none -> 12.1 us  [exchange(): return lax.all_to_all(parts, axes, 0, 0, tiled=True)]
    all_to_all x7 -> x6, starting transfers between devices: 46.5 us -> 42 us  [exchange(): return lax.all_to_all(parts, axes, 0, 0, tiled=True)]
    ppermute x1, waiting for transfers between devices: 3.98 us -> 0.01 us  [shards(): from_other = lax.ppermute(other_terms, 'core', OTHER)]
    all_to_all x7 -> x6, waiting for transfers between devices: 41.1 us -> 44.6 us  [exchange(): return lax.all_to_all(parts, axes, 0, 0, tiled=True)]
    unnamed x69 -> x61, local copies, waits for them, and re-layouts: 10.5 us -> 10.1 us
  transfers between devices with their start and end apart: 30 -> 29, of which waited for: 16 -> 14; matrix products, arithmetic and copies ran while one was open for 7% -> 10% of each run, Pallas kernels for 15% -> 14%
where the time goes in v6:
time: 258 us; the launch traced here: 257 us
  starting transfers between devices  68.3 us (26%)
  waiting for transfers between devices  67.3 us (26%)
  Pallas kernels  52.9 us (21%)
  local copies, waits for them, and re-layouts  25.4 us (10%)
  between operations  14.6 us (6%)
  other arithmetic  13.1 us (5%)
  blocking collectives  12.1 us (5%)
  matrix products  3.41 us (1%)
    all_to_all x6, waiting for transfers between devices, exchange(): return lax.all_to_all(parts, axes, 0, 0, tiled=True)  44.6 us
    all_to_all x6, starting transfers between devices, exchange(): return lax.all_to_all(parts, axes, 0, 0, tiled=True)  42 us
    ppermute x18, starting transfers between devices, step(): return lax.ppermute(array, axis, [(i, (i + shift) % n) for i in range(n)])  25.7 us
    ppermute x18, waiting for transfers between devices, step(): return lax.ppermute(array, axis, [(i, (i + shift) % n) for i in range(n)])  21.9 us
    pallas_call x1, Pallas kernels, gate_up(): call(gate_up_body, 'gate_up', (NY,), [x_spec(t, w), x_spec(t, w), pl.Bloc...  13.5 us
    all_to_all x1, blocking collectives, exchange(): return lax.all_to_all(parts, axes, 0, 0, tiled=True)  12.1 us
    unnamed x61, local copies, waits for them, and re-layouts  10.1 us
    pallas_call x1, Pallas kernels, grad_in_parts(): call(grad_in_body, 'grad_in', (NY,), [pl.BlockSpec((2, t, f), lambda i, p...  8.59 us
  transfers between devices with their start and end apart: 29, of which 14 were waited for; matrix products, arithmetic and copies ran while one was open for 10% of the time, Pallas kernels for 14%

profile of v6, /device:TPU:2, one launch (start us, length us, event | category | flops | bytes accessed | tf_op | source)
XLA Modules:
  0.0 257.1 jit_solution(3809919748922103960)
XLA Ops:
  7.9 1.8 broadcast_in_dim.40
  9.8 8.5 %all-to-all-start.2 = ((bf16[8,192,256]{2,1,0:T(8,128)(2,1)}), bf16[8,192,256]{2,1,0:T(8,128)(2,1)S(1)}, u32[]{:S(2)}, u32[]{:S(2)}) async-start(bf16[8,192,256]{2,1,0:T(8,128)(2,1)} %broadcast_in_dim.40), calls=%async_computation.2 | async-start | bytes 1572864 | tf_op jit(solution)/shard_map/all_to_all | solution.py:307
  18.3 1.7 collective-permute-start
  19.9 1.7 collective-permute-start.1
  21.6 2.0 collective-permute-start.2
  24.2 1.1 collective-permute-done.1
  25.3 2.4 collective-permute-done.2
  27.7 0.8 pad_maximum_fusion.1.refs_3_
  28.5 1.9 collective-permute-start.3
  30.4 1.3 collective-permute-start.5
  31.7 6.4 %merge_down.1 = (bf16[256,8192]{1,0:T(8,128)(2,1)}, f32[64,8,128]{2,1,0:T(8,128)S(1)}) custom-call(s32[4]{0:T(128)S(1)} %pad_add_fusion.pos_ref, bf16[512,8192]{1,0:T(8,128)(2,1)} %frozen_ref.1, bf16[32,512]{1,0:T(8,128)(2,1)S(1)} %bitcast.93, bf16[32,8192]{1,0:T(8,128)(2,1)S(1)} %copy-done.15), custom_call_target="tpu_custom_call" | custom-call | flops 1000000000 | bytes 16000000 | tf_op jit(solution)/shard_map/merge_down/pallas_call | solution.py:95
  38.8 2.6 %all-to-all-done.2.refs_0_ = bf16[8,192,256]{2,1,0:T(8,128)(2,1)S(1)} async-done(((bf16[8,192,256]{2,1,0:T(8,128)(2,1)}), bf16[8,192,256]{2,1,0:T(8,128)(2,1)S(1)}, u32[]{:S(2)}, u32[]{:S(2)}) %all-to-all-start.2) | async-done | bytes 786464 | tf_op jit(solution)/shard_map/all_to_all | solution.py:307
  41.5 0.9 copy-done.2
  42.4 1.6 collective-permute-start.12
  43.9 1.7 collective-permute-start.13
  45.6 1.6 collective-permute-done.3.refs_1_.refs_2_
  47.2 8.2 %all-to-all-start = ((f32[64,8,128]{2,1,0:T(8,128)}), f32[64,8,128]{2,1,0:T(8,128)S(1)}, u32[]{:S(2)}, u32[]{:S(2)}) async-start(f32[64,8,128]{2,1,0:T(8,128)} %after.8), calls=%async_computation | async-start | bytes 524288 | tf_op jit(solution)/shard_map/all_to_all | solution.py:307
  55.4 2.9 %collective-permute-start.7 = (bf16[4,192,256]{2,1,0:T(8,128)(2,1)}, bf16[4,192,256]{2,1,0:T(8,128)(2,1)}, u32[]{:S(2)}, u32[]{:S(2)}) collective-permute-start(bf16[4,192,256]{2,1,0:T(8,128)(2,1)} %collective-permute-done.5.refs_2_.refs_4_), channel_id=1, source_target_pairs={{0,7},{1,0},{2,1},{3,2},{4,3},{5,4},{6,5},{7,6},{8,15},{9,8},{10,9... | collective-permute-start | bytes 1179656 | tf_op jit(solution)/shard_map/ppermute | solution.py:21
  58.3 6.7 %collective-permute-done.12.refs_0_ = bf16[8,192,256]{2,1,0:T(8,128)(2,1)S(1)} collective-permute-done((bf16[8,192,256]{2,1,0:T(8,128)(2,1)}, bf16[8,192,256]{2,1,0:T(8,128)(2,1)S(1)}, u32[]{:S(2)}, u32[]{:S(2)}) %collective-permute-start.12) | collective-permute-done | bytes 786464 | tf_op jit(solution)/shard_map/ppermute | solution.py:21
  65.0 0.8 slice.133
  66.5 0.8 slice.134
  67.3 2.5 collective-permute-start.15
  70.6 5.5 %all-to-all-start.1 = ((f32[64,8,128]{2,1,0:T(8,128)}), f32[64,8,128]{2,1,0:T(8,128)}, u32[]{:S(2)}, u32[]{:S(2)}) async-start(f32[64,8,128]{2,1,0:T(8,128)} %broadcast_in_dim_broadcast_in_dim_broadcast_in_dim.2), calls=%async_computation.1 | async-start | bytes 524288 | tf_op jit(solution)/shard_map/all_to_all | solution.py:307
  76.2 2.9 %collective-permute-start.8 = (bf16[4,192,256]{2,1,0:T(8,128)(2,1)}, bf16[4,192,256]{2,1,0:T(8,128)(2,1)S(1)}, u32[]{:S(2)}, u32[]{:S(2)}) collective-permute-start(bf16[4,192,256]{2,1,0:T(8,128)(2,1)} %after.11.refs_5_), channel_id=1, source_target_pairs={{0,7},{1,0},{2,1},{3,2},{4,3},{5,4},{6,5},{7,6},{8,15},{9,8},{10,9... | collective-permute-start | bytes 1179656 | tf_op jit(solution)/shard_map/ppermute | solution.py:21
  79.1 1.1 copy-done.17
  80.3 3.0 %stack.55.own_ref = bf16[4,8,192,256]{3,2,1,0:T(8,128)(2,1)} custom-call(bf16[8,192,256]{2,1,0:T(8,128)(2,1)S(1)} %collective-permute-done.12.refs_0_, bf16[8,192,256]{2,1,0:T(8,128)(2,1)S(1)} %copy-done.3, bf16[8,192,256]{2,1,0:T(8,128)(2,1)S(1)} %copy-done.17, bf16[4,192,256]{2,1,0:T(8,128)(2,1)} %collective-permute-done.14.refs_3_, ...), custom_call_target="tpu_custom_call" | custom-call | bytes 6000000 | tf_op jit(solution)/shard_map/stack/pallas_call | solution.py:54
  83.3 7.1 %all-to-all-done.1 = f32[64,8,128]{2,1,0:T(8,128)} async-done(((f32[64,8,128]{2,1,0:T(8,128)}), f32[64,8,128]{2,1,0:T(8,128)}, u32[]{:S(2)}, u32[]{:S(2)}) %all-to-all-start.1) | async-done | bytes 262176 | tf_op jit(solution)/shard_map/all_to_all | solution.py:307
  90.3 1.6 sqrt_reduce_fusion
  93.1 1.0 slice.132
  94.1 1.7 collective-permute-start.10
  96.5 1.0 slice.131
  98.0 2.9 %collective-permute-done.10.refs_8_ = bf16[2,192,256]{2,1,0:T(8,128)(2,1)S(1)} collective-permute-done((bf16[2,192,256]{2,1,0:T(8,128)(2,1)S(1)}, bf16[2,192,256]{2,1,0:T(8,128)(2,1)S(1)}, u32[]{:S(2)}, u32[]{:S(2)}) %collective-permute-start.10) | collective-permute-done | bytes 196640 | tf_op jit(solution)/shard_map/ppermute | solution.py:21
  100.9 4.3 %collective-permute-done.9.refs_7_ = bf16[2,192,256]{2,1,0:T(8,128)(2,1)S(1)} collective-permute-done((bf16[2,192,256]{2,1,0:T(8,128)(2,1)S(1)}, bf16[2,192,256]{2,1,0:T(8,128)(2,1)S(1)}, u32[]{:S(2)}, u32[]{:S(2)}) %collective-permute-start.9) | collective-permute-done | bytes 196640 | tf_op jit(solution)/shard_map/ppermute | solution.py:21
  105.3 1.0 copy-done.11
  106.3 1.0 copy-done.13
  107.3 3.3 %stack.54.own_ref = bf16[8,4,192,256]{3,2,1,0:T(8,128)(2,1)} custom-call(bf16[4,192,256]{2,1,0:T(8,128)(2,1)S(1)} %copy-done.13, bf16[4,192,256]{2,1,0:T(8,128)(2,1)} %after.9.refs_1_, bf16[4,192,256]{2,1,0:T(8,128)(2,1)} %collective-permute-done.3.refs_1_.refs_2_, bf16[4,192,256]{2,1,0:T(8,128)(2,1)} %pad_maximum_fusion.1.refs_3_, ...), custom_call_target="tpu_custom_call" | custom-call | bytes 6000000 | tf_op jit(solution)/shard_map/stack/pallas_call | solution.py:54
  110.7 13.5 %gate_up.1 = (bf16[2,8192,256]{2,1,0:T(8,128)(2,1)}, f32[2,384,256]{2,1,0:T(8,128)S(1)}, f32[2,8,256]{2,1,0:T(8,128)S(1)}) custom-call(s32[4]{0:T(128)S(1)} %pad_add_fusion.pos_ref, bf16[4,8,192,256]{3,2,1,0:T(8,128)(2,1)} %stack.55.own_ref, bf16[4,8,192,256]{3,2,1,0:T(8,128)(2,1)} %collective-permute-done.16.other_ref, ...), custom_call_target="tpu_custom_call" | custom-call | flops 1000000000 | bytes 16000000 | tf_op jit(solution)/shard_map/gate_up/pallas_call | solution.py:253
  124.3 7.2 %grad_act.1 = (f32[384,256]{1,0:T(8,128)S(1)}, f32[384,32]{1,0:T(8,128)S(1)}) custom-call(s32[4]{0:T(128)S(1)} %pad_add_fusion.pos_ref, bf16[8,4,192,256]{3,2,1,0:T(8,128)(2,1)} %stack.54.own_ref, bf16[8,4,192,256]{3,2,1,0:T(8,128)(2,1)} %collective-permute-done.11.other_ref, f32[32,1,256]{2,1,0:T(1,128)S(1)} %div.15.scale_ref, ...), custom_call_target="tpu_custom_call" | custom-call | flops 1000000000 | bytes 16000000 | tf_op jit(solution)/shard_map/grad_act/pallas_call | solution.py:175
  132.3 8.6 %grad_in.1 = (bf16[8,4,192,256]{3,2,1,0:T(8,128)(2,1)S(1)}, bf16[8,4,192,256]{3,2,1,0:T(8,128)(2,1)}) custom-call(s32[4]{0:T(128)S(1)} %pad_add_fusion.pos_ref, bf16[2,384,256]{2,1,0:T(8,128)(2,1)S(1)} %get-tuple-element.28.grads_ref, bf16[2,8192,256]{2,1,0:T(8,128)(2,1)} %get-tuple-element.21.tile_ref), custom_call_target="tpu_custom_call" | custom-call | flops 1000000000 | bytes 16000000 | tf_op jit(solution)/shard_map/grad_in/pallas_call | solution.py:293
  140.9 1.6 copy-done.8
  143.1 1.1 fusion.5
  144.2 1.1 fusion.6
  145.5 0.8 maximum_maximum_fusion.1
  146.3 1.7 copy.31
  148.0 1.7 reshape.123
  149.7 1.1 reverse_select_fusion
  151.5 5.7 %dot_down.1 = f32[64,1,128]{2,1,0:T(1,128)S(1)} custom-call(s32[4]{0:T(128)S(1)} %pad_add_fusion.pos_ref, bf16[8,4,192,256]{3,2,1,0:T(8,128)(2,1)S(1)} %copy-done.1, bf16[8,4,192,256]{3,2,1,0:T(8,128)(2,1)} %collective-permute-done.11.other_ref, bf16[384,256]{1,0:T(8,128)(2,1)S(1)} %get-tuple-element.29.act_ref, bf16[256,8192]{1,0:T(8,128)(2,1)} %get-tuple-element.17.tile_ref), custom_call_target="tpu_custom_call" | custom-call | flops 1000000000 | bytes 16000000 | tf_op jit(solution)/shard_map/dot_down/pallas_call | solution.py:209
  157.8 1.9 copy-done.9
  159.7 4.6 %add_convert_fusion = bf16[8,4,192,256]{3,2,1,0:T(8,128)(2,1)} fusion(bf16[8,4,192,256]{3,2,1,0:T(8,128)(2,1)} %after.14, bf16[8,4,192,256]{3,2,1,0:T(8,128)(2,1)S(1)} %copy-done.9), kind=kLoop, calls=%fused_computation | loop fusion | flops 6291456 | bytes 9437184 | tf_op jit(solution)/shard_map/convert_element_type | solution.py:393
  164.5 10.5 %all-to-all-start.3 = ((f32[64,8,128]{2,1,0:T(8,128)}), f32[64,8,128]{2,1,0:T(8,128)S(1)}, u32[]{:S(2)}, u32[]{:S(2)}) async-start(f32[64,8,128]{2,1,0:T(8,128)} %pad.12.refs_1_), calls=%async_computation.4 | async-start | bytes 524288 | tf_op jit(solution)/shard_map/all_to_all | solution.py:307
  175.2 15.9 %all-to-all-done.3 = f32[64,8,128]{2,1,0:T(8,128)S(1)} async-done(((f32[64,8,128]{2,1,0:T(8,128)}), f32[64,8,128]{2,1,0:T(8,128)S(1)}, u32[]{:S(2)}, u32[]{:S(2)}) %all-to-all-start.3) | async-done | bytes 262176 | tf_op jit(solution)/shard_map/all_to_all | solution.py:307
  191.1 0.8 maximum_maximum_fusion
  191.9 4.6 %all-to-all-start.4 = ((f32[64,8,128]{2,1,0:T(8,128)}), f32[64,8,128]{2,1,0:T(8,128)S(1)}, u32[]{:S(2)}, u32[]{:S(2)}) async-start(f32[64,8,128]{2,1,0:T(8,128)} %maximum_maximum_fusion), calls=%async_computation.5 | async-start | bytes 524288 | tf_op jit(solution)/shard_map/all_to_all | solution.py:307
  196.6 5.2 %proj_gate_up.1 = f32[384,64]{1,0:T(8,128)S(1)} custom-call(s32[4]{0:T(128)S(1)} %pad_add_fusion.pos_ref, bf16[4,8,192,256]{3,2,1,0:T(8,128)(2,1)} %stack.55.own_ref, bf16[4,8,192,256]{3,2,1,0:T(8,128)(2,1)} %collective-permute-done.16.other_ref, bf16[2,32,8192]{2,1,0:T(8,128)(2,1)S(1)} %bitcast.91, f32[8,128]{1,0:T(8,128)S(1)} %reduce_sum.60._), custom_call_target="tpu_custom_call" | custom-call | flops 1000000000 | bytes 16000000 | tf_op jit(solution)/shard_map/proj_gate_up/pallas_call | solution.py:139
  202.3 11.5 %all-to-all-done.4 = f32[64,8,128]{2,1,0:T(8,128)S(1)} async-done(((f32[64,8,128]{2,1,0:T(8,128)}), f32[64,8,128]{2,1,0:T(8,128)S(1)}, u32[]{:S(2)}, u32[]{:S(2)}) %all-to-all-start.4) | async-done | bytes 262176 | tf_op jit(solution)/shard_map/all_to_all | solution.py:307
  214.5 12.1 %all_to_all.35 = f32[8,48,256]{2,1,0:T(8,128)S(1)} all-to-all(f32[8,48,256]{2,1,0:T(8,128)S(1)} %bitcast.104), channel_id=1, replica_groups=mesh['x'=4,'core'=2,'y'=4,'z'=8] {'x','core'}, dimensions={0} | all-to-all | bytes 786432 | tf_op jit(solution)/shard_map/all_to_all | solution.py:307
  226.7 0.8 broadcast_in_dim.46
  227.5 4.8 %all-to-all-start.6 = ((f32[8,48,256]{2,1,0:T(8,128)}), f32[8,48,256]{2,1,0:T(8,128)S(1)}, u32[]{:S(2)}, u32[]{:S(2)}) async-start(f32[8,48,256]{2,1,0:T(8,128)} %broadcast_in_dim.46), calls=%async_computation.7 | async-start | bytes 786432 | tf_op jit(solution)/shard_map/all_to_all | solution.py:307
  232.3 7.5 %all-to-all-done.6 = f32[8,48,256]{2,1,0:T(8,128)S(1)} async-done(((f32[8,48,256]{2,1,0:T(8,128)}), f32[8,48,256]{2,1,0:T(8,128)S(1)}, u32[]{:S(2)}, u32[]{:S(2)}) %all-to-all-start.6) | async-done | bytes 393248 | tf_op jit(solution)/shard_map/all_to_all | solution.py:307
  239.9 1.2 fusion.2
  241.1 1.1 collective-permute-start.18
  242.1 1.0 collective-permute-start.19
  245.8 0.8 reshape.131
  247.8 1.8 collective-permute-done.19
  (140 shorter events, 15.2 us)
Async XLA Ops:
  7.2 103.4 %copy-start = (bf16[2,32,512]{2,1,0:T(8,128)(2,1)S(1)}, bf16[2,32,512]{2,1,0:T(8,128)(2,1)}, u32[]{:S(2)}) copy-start(bf16[2,32,512]{2,1,0:T(8,128)(2,1)} %param.14) | copy-start | bytes 196612
  7.2 11.1 %copy-start.24 = (bf16[192,256]{1,0:T(8,128)(2,1)S(1)}, bf16[192,256]{1,0:T(8,128)(2,1)}, u32[]{:S(2)}) copy-start(bf16[192,256]{1,0:T(8,128)(2,1)} %param.11) | copy-start | bytes 294916
  7.2 24.5 %copy-start.21 = (bf16[512,32]{0,1:T(8,128)(2,1)S(1)}, bf16[512,32]{0,1:T(8,128)(2,1)}, u32[]{:S(2)}) copy-start(bf16[512,32]{0,1:T(8,128)(2,1)} %param.17) | copy-start | bytes 98308
  7.2 24.5 %copy-start.15 = (bf16[32,8192]{1,0:T(8,128)(2,1)S(1)}, bf16[32,8192]{1,0:T(8,128)(2,1)}, u32[]{:S(2)}) copy-start(bf16[32,8192]{1,0:T(8,128)(2,1)} %right_ref.3) | copy-start | bytes 1572868
  7.2 103.5 %all-gather.2.cloned.1.call-start = ((), (), s32[]{:S(2)}) async-start(), calls=%async_computation.8 | async-start | bytes 18874368 | tf_op jit(solution)/shard_map/all_gather | solution.py:338
  9.8 31.7 %all-to-all-start.2 = ((bf16[8,192,256]{2,1,0:T(8,128)(2,1)}), bf16[8,192,256]{2,1,0:T(8,128)(2,1)S(1)}, u32[]{:S(2)}, u32[]{:S(2)}) async-start(bf16[8,192,256]{2,1,0:T(8,128)(2,1)} %broadcast_in_dim.40), calls=%async_computation.2 | async-start | bytes 1572864 | tf_op jit(solution)/shard_map/all_to_all | solution.py:307
  18.3 5.9 %collective-permute-start = (bf16[192,256]{1,0:T(8,128)(2,1)S(1)}, bf16[192,256]{1,0:T(8,128)(2,1)S(1)}, u32[]{:S(2)}, u32[]{:S(2)}) collective-permute-start(bf16[192,256]{1,0:T(8,128)(2,1)S(1)} %copy-done.24), channel_id=1, source_target_pairs={{0,8},{8,16},{16,24},{24,0},{1,9},{9,17},{17,25},{25,1},{2,10},{10... | collective-permute-start | bytes 294920 | tf_op jit(solution)/shard_map/ppermute | solution.py:21
  19.9 5.3 %collective-permute-start.1 = (bf16[192,256]{1,0:T(8,128)(2,1)S(1)}, bf16[192,256]{1,0:T(8,128)(2,1)S(1)}, u32[]{:S(2)}, u32[]{:S(2)}) collective-permute-start(bf16[192,256]{1,0:T(8,128)(2,1)S(1)} %copy-done.24), channel_id=1, source_target_pairs={{0,24},{8,0},{16,8},{24,16},{1,25},{9,1},{17,9},{25,17},{2,26},{10... | collective-permute-start | bytes 294920 | tf_op jit(solution)/shard_map/ppermute | solution.py:21
  21.6 6.1 %collective-permute-start.2 = (bf16[192,256]{1,0:T(8,128)(2,1)S(1)}, bf16[192,256]{1,0:T(8,128)(2,1)S(1)}, u32[]{:S(2)}, u32[]{:S(2)}) collective-permute-start(bf16[192,256]{1,0:T(8,128)(2,1)S(1)} %copy-done.24), channel_id=1, source_target_pairs={{0,16},{8,24},{16,0},{24,8},{1,17},{9,25},{17,1},{25,9},{2,18},{10... | collective-permute-start | bytes 294920 | tf_op jit(solution)/shard_map/ppermute | solution.py:21
  28.5 18.7 %collective-permute-start.3 = (bf16[4,192,256]{2,1,0:T(8,128)(2,1)}, bf16[4,192,256]{2,1,0:T(8,128)(2,1)}, u32[]{:S(2)}, u32[]{:S(2)}) collective-permute-start(bf16[4,192,256]{2,1,0:T(8,128)(2,1)} %pad_maximum_fusion.1.refs_3_), channel_id=1, source_target_pairs={{0,1},{1,2},{2,3},{3,4},{4,5},{5,6},{6,7},{7,0},{8,9},{9,10},{10,1... | collective-permute-start | bytes 1179656 | tf_op jit(solution)/shard_map/ppermute | solution.py:21
  30.4 16.8 %collective-permute-start.5 = (bf16[4,192,256]{2,1,0:T(8,128)(2,1)}, bf16[4,192,256]{2,1,0:T(8,128)(2,1)}, u32[]{:S(2)}, u32[]{:S(2)}) collective-permute-start(bf16[4,192,256]{2,1,0:T(8,128)(2,1)} %pad_maximum_fusion.1.refs_3_), channel_id=1, source_target_pairs={{0,7},{1,0},{2,1},{3,2},{4,3},{5,4},{6,5},{7,6},{8,15},{9,8},{10,9... | collective-permute-start | bytes 1179656 | tf_op jit(solution)/shard_map/ppermute | solution.py:21
  38.1 0.7 copy-start.14
  41.5 0.9 copy-start.2
  42.4 36.8 %copy-start.3 = (bf16[8,192,256]{2,1,0:T(8,128)(2,1)S(1)}, bf16[8,192,256]{2,1,0:T(8,128)(2,1)}, u32[]{:S(2)}) copy-start(bf16[8,192,256]{2,1,0:T(8,128)(2,1)} %after.13.refs_1_) | copy-start | bytes 2359300
  42.4 22.6 %collective-permute-start.12 = (bf16[8,192,256]{2,1,0:T(8,128)(2,1)}, bf16[8,192,256]{2,1,0:T(8,128)(2,1)S(1)}, u32[]{:S(2)}, u32[]{:S(2)}) collective-permute-start(bf16[8,192,256]{2,1,0:T(8,128)(2,1)} %after.13.refs_1_), channel_id=1, source_target_pairs={{0,8},{8,16},{16,24},{24,0},{1,9},{9,17},{17,25},{25,1},{2,10},{10... | collective-permute-start | bytes 2359304 | tf_op jit(solution)/shard_map/ppermute | solution.py:21
  43.9 22.5 %collective-permute-start.13 = (bf16[8,192,256]{2,1,0:T(8,128)(2,1)}, bf16[8,192,256]{2,1,0:T(8,128)(2,1)S(1)}, u32[]{:S(2)}, u32[]{:S(2)}) collective-permute-start(bf16[8,192,256]{2,1,0:T(8,128)(2,1)} %after.13.refs_1_), channel_id=1, source_target_pairs={{0,24},{8,0},{16,8},{24,16},{1,25},{9,1},{17,9},{25,17},{2,26},{10... | collective-permute-start | bytes 2359304 | tf_op jit(solution)/shard_map/ppermute | solution.py:21
  47.2 22.6 %all-to-all-start = ((f32[64,8,128]{2,1,0:T(8,128)}), f32[64,8,128]{2,1,0:T(8,128)S(1)}, u32[]{:S(2)}, u32[]{:S(2)}) async-start(f32[64,8,128]{2,1,0:T(8,128)} %after.8), calls=%async_computation | async-start | bytes 524288 | tf_op jit(solution)/shard_map/all_to_all | solution.py:307
  55.4 20.8 %collective-permute-start.7 = (bf16[4,192,256]{2,1,0:T(8,128)(2,1)}, bf16[4,192,256]{2,1,0:T(8,128)(2,1)}, u32[]{:S(2)}, u32[]{:S(2)}) collective-permute-start(bf16[4,192,256]{2,1,0:T(8,128)(2,1)} %collective-permute-done.5.refs_2_.refs_4_), channel_id=1, source_target_pairs={{0,7},{1,0},{2,1},{3,2},{4,3},{5,4},{6,5},{7,6},{8,15},{9,8},{10,9... | collective-permute-start | bytes 1179656 | tf_op jit(solution)/shard_map/ppermute | solution.py:21
  58.2 20.9 %collective-permute-start.4 = (bf16[4,192,256]{2,1,0:T(8,128)(2,1)}, bf16[4,192,256]{2,1,0:T(8,128)(2,1)}, u32[]{:S(2)}, u32[]{:S(2)}) collective-permute-start(bf16[4,192,256]{2,1,0:T(8,128)(2,1)} %collective-permute-done.3.refs_1_.refs_2_), channel_id=1, source_target_pairs={{0,1},{1,2},{2,3},{3,4},{4,5},{5,6},{6,7},{7,0},{8,9},{9,10},{10,1... | collective-permute-start | bytes 1179656 | tf_op jit(solution)/shard_map/ppermute | solution.py:21
  65.7 13.4 %collective-permute-start.14 = (bf16[4,192,256]{2,1,0:T(8,128)(2,1)}, bf16[4,192,256]{2,1,0:T(8,128)(2,1)}, u32[]{:S(2)}, u32[]{:S(2)}) collective-permute-start(bf16[4,192,256]{2,1,0:T(8,128)(2,1)} %slice.133), channel_id=1, source_target_pairs={{0,8},{8,16},{16,24},{24,0},{1,9},{9,17},{17,25},{25,1},{2,10},{10... | collective-permute-start | bytes 1179656 | tf_op jit(solution)/shard_map/ppermute | solution.py:21
  66.5 9.7 %copy-start.16 = (bf16[8,192,256]{2,1,0:T(8,128)(2,1)}, bf16[8,192,256]{2,1,0:T(8,128)(2,1)S(1)}, u32[]{:S(2)}) copy-start(bf16[8,192,256]{2,1,0:T(8,128)(2,1)S(1)} %collective-permute-done.13.refs_2_) | copy-start | bytes 2359300
  67.3 11.8 %collective-permute-start.15 = (bf16[4,192,256]{2,1,0:T(8,128)(2,1)}, bf16[4,192,256]{2,1,0:T(8,128)(2,1)}, u32[]{:S(2)}, u32[]{:S(2)}) collective-permute-start(bf16[4,192,256]{2,1,0:T(8,128)(2,1)} %slice.134), channel_id=1, source_target_pairs={{0,24},{8,0},{16,8},{24,16},{1,25},{9,1},{17,9},{25,17},{2,26},{10... | collective-permute-start | bytes 1179656 | tf_op jit(solution)/shard_map/ppermute | solution.py:21
  69.9 6.3 %copy-start.28 = (f32[128]{0:T(128)}, f32[128]{0:T(128)S(1)}, u32[]{:S(2)}) copy-start(f32[128]{0:T(128)S(1)} %reduce_sum.58) | copy-start | bytes 1540
  70.6 19.7 %all-to-all-start.1 = ((f32[64,8,128]{2,1,0:T(8,128)}), f32[64,8,128]{2,1,0:T(8,128)}, u32[]{:S(2)}, u32[]{:S(2)}) async-start(f32[64,8,128]{2,1,0:T(8,128)} %broadcast_in_dim_broadcast_in_dim_broadcast_in_dim.2), calls=%async_computation.1 | async-start | bytes 524288 | tf_op jit(solution)/shard_map/all_to_all | solution.py:307
  76.1 163.7 %reduce-scatter.2.cloned.1.call-start = ((), (), s32[]{:S(2)}) async-start(), calls=%async_computation.9 | async-start | bytes 3538944 | tf_op jit(solution)/shard_map/reduce_scatter | solution.py:394
  76.2 16.2 %collective-permute-start.8 = (bf16[4,192,256]{2,1,0:T(8,128)(2,1)}, bf16[4,192,256]{2,1,0:T(8,128)(2,1)S(1)}, u32[]{:S(2)}, u32[]{:S(2)}) collective-permute-start(bf16[4,192,256]{2,1,0:T(8,128)(2,1)} %after.11.refs_5_), channel_id=1, source_target_pairs={{0,7},{1,0},{2,1},{3,2},{4,3},{5,4},{6,5},{7,6},{8,15},{9,8},{10,9... | collective-permute-start | bytes 1179656 | tf_op jit(solution)/shard_map/ppermute | solution.py:21
  79.1 16.6 %collective-permute-start.6 = (bf16[4,192,256]{2,1,0:T(8,128)(2,1)}, bf16[4,192,256]{2,1,0:T(8,128)(2,1)S(1)}, u32[]{:S(2)}, u32[]{:S(2)}) collective-permute-start(bf16[4,192,256]{2,1,0:T(8,128)(2,1)} %after.9.refs_1_), channel_id=1, source_target_pairs={{0,1},{1,2},{2,3},{3,4},{4,5},{5,6},{6,7},{7,0},{8,9},{9,10},{10,1... | collective-permute-start | bytes 1179656 | tf_op jit(solution)/shard_map/ppermute | solution.py:21
  79.1 1.1 copy-start.17
  83.2 27.4 %collective-permute-start.16 = (bf16[4,8,192,256]{3,2,1,0:T(8,128)(2,1)}, bf16[4,8,192,256]{3,2,1,0:T(8,128)(2,1)}, u32[]{:S(2)}, u32[]{:S(2)}) collective-permute-start(bf16[4,8,192,256]{3,2,1,0:T(8,128)(2,1)} %stack.55.own_ref), channel_id=1, source_target_pairs={{0,32},{32,0},{1,33},{33,1},{2,34},{34,2},{3,35},{35,3},{4,36},{36... | collective-permute-start | bytes 9437192 | tf_op jit(solution)/shard_map/ppermute | solution.py:357
  92.4 0.7 copy-start.10
  94.1 6.8 %collective-permute-start.10 = (bf16[2,192,256]{2,1,0:T(8,128)(2,1)S(1)}, bf16[2,192,256]{2,1,0:T(8,128)(2,1)S(1)}, u32[]{:S(2)}, u32[]{:S(2)}) collective-permute-start(bf16[2,192,256]{2,1,0:T(8,128)(2,1)S(1)} %slice.132), channel_id=1, source_target_pairs={{0,7},{1,0},{2,1},{3,2},{4,3},{5,4},{6,5},{7,6},{8,15},{9,8},{10,9... | collective-permute-start | bytes 589832 | tf_op jit(solution)/shard_map/ppermute | solution.py:21
  95.7 0.7 copy-start.12
  96.5 14.1 %copy-start.27 = (f32[8192]{0:T(1024)S(1)}, f32[8192]{0:T(1024)}, u32[]{:S(2)}) copy-start(f32[8192]{0:T(1024)} %param.19) | copy-start | bytes 98308
  96.5 14.2 %copy-start.18 = (f32[64,1,128]{2,1,0:T(1,128)S(1)}, f32[64,1,128]{2,1,0:T(1,128)}, u32[]{:S(2)}) copy-start(f32[64,1,128]{2,1,0:T(1,128)} %get-tuple-element.35.refs_1_._) | copy-start | bytes 98308
  97.5 13.2 %copy-start.6 = (bf16[2,8192,32]{1,2,0:T(8,128)(2,1)S(1)}, bf16[2,8192,32]{1,2,0:T(8,128)(2,1)}, u32[]{:S(2)}) copy-start(bf16[2,8192,32]{1,2,0:T(8,128)(2,1)} %param.13) | copy-start | bytes 3145732
  97.5 7.8 %collective-permute-start.9 = (bf16[2,192,256]{2,1,0:T(8,128)(2,1)S(1)}, bf16[2,192,256]{2,1,0:T(8,128)(2,1)S(1)}, u32[]{:S(2)}, u32[]{:S(2)}) collective-permute-start(bf16[2,192,256]{2,1,0:T(8,128)(2,1)S(1)} %slice.131), channel_id=1, source_target_pairs={{0,1},{1,2},{2,3},{3,4},{4,5},{5,6},{6,7},{7,0},{8,9},{9,10},{10,1... | collective-permute-start | bytes 589832 | tf_op jit(solution)/shard_map/ppermute | solution.py:21
  105.3 1.0 copy-start.11
  106.3 1.0 copy-start.13
  110.6 13.8 %collective-permute-start.11 = (bf16[8,4,192,256]{3,2,1,0:T(8,128)(2,1)}, bf16[8,4,192,256]{3,2,1,0:T(8,128)(2,1)}, u32[]{:S(2)}, u32[]{:S(2)}) collective-permute-start(bf16[8,4,192,256]{3,2,1,0:T(8,128)(2,1)} %stack.54.own_ref), channel_id=1, source_target_pairs={{0,32},{32,0},{1,33},{33,1},{2,34},{34,2},{3,35},{35,3},{4,36},{36... | collective-permute-start | bytes 9437192 | tf_op jit(solution)/shard_map/ppermute | solution.py:358
  110.7 13.5 %copy-start.29 = (f32[2,512]{1,0:T(2,128)S(1)}, f32[2,512]{1,0:T(2,128)}, u32[]{:S(2)}) copy-start(f32[2,512]{1,0:T(2,128)} %param.15) | copy-start | bytes 12292
  131.6 0.7 copy-start.19
  132.0 8.9 %copy-start.4 = (bf16[2,384,256]{2,1,0:T(8,128)(2,1)}, bf16[2,384,256]{2,1,0:T(8,128)(2,1)S(1)}, u32[]{:S(2)}) copy-start(bf16[2,384,256]{2,1,0:T(8,128)(2,1)S(1)} %get-tuple-element.28.grads_ref) | copy-start | bytes 1179652
  132.3 19.3 %copy-start.1 = (bf16[8,4,192,256]{3,2,1,0:T(8,128)(2,1)S(1)}, bf16[8,4,192,256]{3,2,1,0:T(8,128)(2,1)}, u32[]{:S(2)}) copy-start(bf16[8,4,192,256]{3,2,1,0:T(8,128)(2,1)} %stack.54.own_ref) | copy-start | bytes 9437188
  140.9 1.6 copy-start.8
  142.5 15.3 %collective-permute-start.17 = (bf16[8,4,192,256]{3,2,1,0:T(8,128)(2,1)}, bf16[8,4,192,256]{3,2,1,0:T(8,128)(2,1)}, u32[]{:S(2)}, u32[]{:S(2)}) collective-permute-start(bf16[8,4,192,256]{3,2,1,0:T(8,128)(2,1)} %get-tuple-element.23), channel_id=1, source_target_pairs={{0,32},{32,0},{1,33},{33,1},{2,34},{34,2},{3,35},{35,3},{4,36},{36... | collective-permute-start | bytes 9437192 | tf_op jit(solution)/shard_map/ppermute | solution.py:380
  157.8 1.9 copy-start.9
  164.4 10.6 %copy-start.20 = (f32[384,32]{1,0:T(8,128)S(1)}, f32[384,32]{1,0:T(8,128)}, u32[]{:S(2)}) copy-start(f32[384,32]{1,0:T(8,128)} %copy-done.19) | copy-start | bytes 147460
  164.4 26.8 %copy-start.26 = (f32[32,2,1,128]{3,0,1,2:T(8,128)S(1)}, f32[32,2,1,128]{3,0,1,2:T(8,128)}, u32[]{:S(2)}) copy-start(f32[32,2,1,128]{3,0,1,2:T(8,128)} %copy.32) | copy-start | bytes 98308
  164.4 32.2 %copy-start.7 = (bf16[2,8192,32]{1,2,0:T(8,128)(2,1)S(1)}, bf16[2,8192,32]{1,2,0:T(8,128)(2,1)}, u32[]{:S(2)}) copy-start(bf16[2,8192,32]{1,2,0:T(8,128)(2,1)} %param.13) | copy-start | bytes 3145732
  164.5 26.5 %all-to-all-start.3 = ((f32[64,8,128]{2,1,0:T(8,128)}), f32[64,8,128]{2,1,0:T(8,128)S(1)}, u32[]{:S(2)}, u32[]{:S(2)}) async-start(f32[64,8,128]{2,1,0:T(8,128)} %pad.12.refs_1_), calls=%async_computation.4 | async-start | bytes 524288 | tf_op jit(solution)/shard_map/all_to_all | solution.py:307
  191.9 21.9 %all-to-all-start.4 = ((f32[64,8,128]{2,1,0:T(8,128)}), f32[64,8,128]{2,1,0:T(8,128)S(1)}, u32[]{:S(2)}, u32[]{:S(2)}) async-start(f32[64,8,128]{2,1,0:T(8,128)} %maximum_maximum_fusion), calls=%async_computation.5 | async-start | bytes 524288 | tf_op jit(solution)/shard_map/all_to_all | solution.py:307
  196.5 5.3 %copy-start.5 = (bf16[2,384,256]{2,1,0:T(8,128)(2,1)S(1)}, bf16[2,384,256]{2,1,0:T(8,128)(2,1)}, u32[]{:S(2)}) copy-start(bf16[2,384,256]{2,1,0:T(8,128)(2,1)} %copy-done.4) | copy-start | bytes 1179652
  196.6 17.4 %copy-start.23 = (bf16[192,256]{1,0:T(8,128)(2,1)S(1)}, bf16[192,256]{1,0:T(8,128)(2,1)}, u32[]{:S(2)}) copy-start(bf16[192,256]{1,0:T(8,128)(2,1)} %param.10) | copy-start | bytes 294916
  196.6 17.6 %copy-start.25 = (bf16[192,256]{1,0:T(8,128)(2,1)S(1)}, bf16[192,256]{1,0:T(8,128)(2,1)}, u32[]{:S(2)}) copy-start(bf16[192,256]{1,0:T(8,128)(2,1)} %param.11) | copy-start | bytes 294916
  226.7 13.2 %copy-start.22 = (f32[48,256]{1,0:T(8,128)}, f32[48,256]{1,0:T(8,128)S(1)}, u32[]{:S(2)}) copy-start(f32[48,256]{1,0:T(8,128)S(1)} %reduce_sum.63.refs_1_) | copy-start | bytes 147460
  227.5 12.3 %all-to-all-start.6 = ((f32[8,48,256]{2,1,0:T(8,128)}), f32[8,48,256]{2,1,0:T(8,128)S(1)}, u32[]{:S(2)}, u32[]{:S(2)}) async-start(f32[8,48,256]{2,1,0:T(8,128)} %broadcast_in_dim.46), calls=%async_computation.7 | async-start | bytes 786432 | tf_op jit(solution)/shard_map/all_to_all | solution.py:307
  241.1 6.7 %collective-permute-start.18 = (bf16[192,256]{1,0:T(8,128)(2,1)S(1)}, bf16[192,256]{1,0:T(8,128)(2,1)S(1)}, u32[]{:S(2)}, u32[]{:S(2)}) collective-permute-start(bf16[192,256]{1,0:T(8,128)(2,1)S(1)} %get-tuple-element.30), channel_id=1, source_target_pairs={{0,24},{8,0},{16,8},{24,16},{1,25},{9,1},{17,9},{25,17},{2,26},{10... | collective-permute-start | bytes 294920 | tf_op jit(solution)/shard_map/ppermute | solution.py:21
  242.1 7.4 %collective-permute-start.19 = (bf16[192,256]{1,0:T(8,128)(2,1)S(1)}, bf16[192,256]{1,0:T(8,128)(2,1)S(1)}, u32[]{:S(2)}, u32[]{:S(2)}) collective-permute-start(bf16[192,256]{1,0:T(8,128)(2,1)S(1)} %get-tuple-element.31), channel_id=1, source_target_pairs={{0,8},{8,16},{16,24},{24,0},{1,9},{9,17},{17,25},{25,1},{2,10},{10... | collective-permute-start | bytes 294920 | tf_op jit(solution)/shard_map/ppermute | solution.py:21
  243.2 6.4 %collective-permute-start.20 = (bf16[192,256]{1,0:T(8,128)(2,1)S(1)}, bf16[192,256]{1,0:T(8,128)(2,1)S(1)}, u32[]{:S(2)}, u32[]{:S(2)}) collective-permute-start(bf16[192,256]{1,0:T(8,128)(2,1)S(1)} %get-tuple-element.32), channel_id=1, source_target_pairs={{0,16},{8,24},{16,0},{24,8},{1,17},{9,25},{17,1},{25,9},{2,18},{10... | collective-permute-start | bytes 294920 | tf_op jit(solution)/shard_map/ppermute | solution.py:21
Sparse Core Ops, SparseCore 0:
  9.9 90.0 all-gather.1
  164.5 56.4 reduce-scatter.1
